TPU v7x, 32 devices: a whole 2x2x4 slice. The times are simulated.
32 devices in a mesh: fsdp: 2 (over core), heads: 4 (over y, x), tensor: 4 (over z).
Axes of the slice: x: 2, y: 2, z: 4, core: 2. Of those that a mesh axis runs over, the one named last changes fastest.
Arguments:
- tokens: bfloat16 [8192, 1024], P(('fsdp', 'heads'), 'tensor'), may hold values from -6 to 6
- cotangent: bfloat16 [8192, 1024], P(('fsdp', 'heads'), 'tensor'), may hold values from -6 to 6
- lengths: int32 [4], replicated, may hold values from 512 to 3584, as said below
- norm_gain: float32 [1024], replicated, may hold values from 0.5 to 1.5
- query_weight: bfloat16 [1024, 1024], P('fsdp', 'tensor'), may hold values from -0.1875 to 0.1875
- key_weight: bfloat16 [1024, 1024], P('fsdp', 'tensor'), may hold values from -0.1875 to 0.1875
- value_weight: bfloat16 [1024, 2048], P('fsdp', 'tensor'), may hold values from -0.1875 to 0.1875
- outgate_weight: bfloat16 [1024, 2048], P('fsdp', 'tensor'), may hold values from -0.1875 to 0.1875
- alpha_weight: bfloat16 [1024, 8], P('fsdp', 'tensor'), may hold values from -0.1875 to 0.1875
- beta_weight: bfloat16 [1024, 8], P('fsdp', 'tensor'), may hold values from -0.1875 to 0.1875
- output_weight: bfloat16 [2048, 1024], P('tensor', 'fsdp'), may hold values from -0.25 to 0.25
- conv_query: float32 [4, 1024], replicated, may hold values from -3 to 3
- conv_key: float32 [4, 1024], replicated, may hold values from -3 to 3
- conv_value: float32 [4, 2048], replicated, may hold values from -3 to 3
- log_rate: float32 [8], replicated, may hold values from 0 to 2.77
- step_bias: float32 [8], replicated, may hold values from -6.9 to -2.3
- out_gain: float32 [256], replicated, may hold values from 0.5 to 1.5
- ffn_gain: float32 [1024], replicated, may hold values from 0.5 to 1.5
- gate_weight: bfloat16 [1024, 2816], P('fsdp', 'tensor'), may hold values from -0.1875 to 0.1875
- up_weight: bfloat16 [1024, 2816], P('fsdp', 'tensor'), may hold values from -0.1875 to 0.1875
- down_weight: bfloat16 [2816, 1024], P('tensor', 'fsdp'), may hold values from -0.109375 to 0.109375
Outputs:
- output: bfloat16 [8192, 1024], P(('fsdp', 'heads'), 'tensor')
- grad_tokens: float32 [8192, 1024], P(('fsdp', 'heads'), 'tensor')
- grad_query_weight: float32 [1024, 1024], P(('fsdp', 'heads'), 'tensor')
- grad_key_weight: float32 [1024, 1024], P(('fsdp', 'heads'), 'tensor')
- grad_value_weight: float32 [1024, 2048], P(('fsdp', 'heads'), 'tensor')
- grad_outgate_weight: float32 [1024, 2048], P(('fsdp', 'heads'), 'tensor')
- grad_alpha_weight: float32 [1024, 8], P(('fsdp', 'heads'), 'tensor')
- grad_beta_weight: float32 [1024, 8], P(('fsdp', 'heads'), 'tensor')
- grad_output_weight: float32 [2048, 1024], P('tensor', ('fsdp', 'heads'))
- grad_gate_weight: float32 [1024, 2816], P(('fsdp', 'heads'), 'tensor')
- grad_up_weight: float32 [1024, 2816], P(('fsdp', 'heads'), 'tensor')
- grad_down_weight: float32 [2816, 1024], P('tensor', ('fsdp', 'heads'))
- grad_conv_query: float32 [4, 1024], replicated
- grad_conv_key: float32 [4, 1024], replicated
- grad_conv_value: float32 [4, 2048], replicated
- grad_log_rate: float32 [8], replicated
- grad_step_bias: float32 [8], replicated
- grad_out_gain: float32 [256], replicated
- grad_norm_gain: float32 [1024], replicated
- grad_ffn_gain: float32 [1024], replicated
Inputs may be any that keep to these rules, and one draw needn't show every extreme that they name: `lengths`: lengths of the packed sequences in token order; each is a multiple of 64, they add up to 8192, and each is shorter than 4096.
All inputs are finite; a program needn't handle non-finite values.
Results may differ from a plain program's by a relative error of at most 0.02.
Values may be sent and summed in bfloat16 or wider, within the bound.
No kernel may reach another device: no remote copies, remote signals or barrier semaphores. Data moves between devices by JAX's collectives and lax.ppermute only.
A program may use at most 192 MiB of HBM per device.

v0:
```python
import jax
import jax.numpy as jnp
from jax import lax
from jax.sharding import PartitionSpec as P

CONV = 4
GROUP = 64


PRECISE = lax.Precision.HIGHEST
EPSILON = 1e-06


def shifted(shard, axis, by):
    devices = lax.axis_size(axis)
    pairs = [(i, i + by) for i in range(devices) if 0 <= i + by < devices]
    return lax.ppermute(shard, axis, pairs)


def convolve(padded, kernel, valid_taps):
    row_count = valid_taps.shape[0]
    summed = padded[CONV - 1 :] * kernel[CONV - 1] * valid_taps[:, CONV - 1 : CONV]
    for offset in range(CONV - 1):
        summed = (
            summed
            + padded[offset : offset + row_count]
            * kernel[offset]
            * valid_taps[:, offset : offset + 1]
        )
    return summed


def delta_rule(queries, keys_in, values, decays, beta_rate, keep_flags, state_in):
    length, key_width = queries.shape
    value_width = values.shape[1]
    blocks = length // GROUP
    query_blocks = queries.reshape(blocks, GROUP, key_width)
    key_blocks = keys_in.reshape(blocks, GROUP, key_width)
    value_blocks = values.reshape(blocks, GROUP, value_width)
    beta_blocks = beta_rate.reshape(blocks, GROUP)
    cumulative = jnp.cumsum(decays.reshape(blocks, GROUP), axis=1)
    row_index = lax.broadcasted_iota(jnp.int32, (GROUP, GROUP), 0)
    col_index = lax.broadcasted_iota(jnp.int32, (GROUP, GROUP), 1)
    lower_mask = (row_index >= col_index).astype(queries.dtype)
    strict = (row_index > col_index).astype(queries.dtype)
    fading = jnp.exp((cumulative[:, :, None] - cumulative[:, None, :]) * lower_mask) * lower_mask
    key_gram = jnp.einsum("nid,njd->nij", key_blocks, key_blocks, precision=PRECISE)
    system = (
        jnp.eye(GROUP, dtype=queries.dtype) + strict * fading * beta_blocks[:, :, None] * key_gram
    )
    growth = jnp.exp(cumulative)
    keys_wy = lax.linalg.triangular_solve(
        system,
        (beta_blocks * growth)[:, :, None] * key_blocks,
        left_side=True,
        lower=True,
        unit_diagonal=True,
    )
    values_wy = lax.linalg.triangular_solve(
        system,
        beta_blocks[:, :, None] * value_blocks,
        left_side=True,
        lower=True,
        unit_diagonal=True,
    )
    scores = jnp.einsum("nid,njd->nij", query_blocks, key_blocks, precision=PRECISE) * fading
    query_grown = query_blocks * growth[:, :, None]
    key_tail = jnp.exp(cumulative[:, -1:] - cumulative)[:, :, None] * key_blocks
    block_decay = growth[:, -1]

    def advance(carried, pieces):
        wy_keys, wy_values, block_scores, grown, tail_keys, whole_decay, keep_flag = pieces
        carried = carried * keep_flag
        fresh = wy_values - jnp.dot(wy_keys, carried, precision=PRECISE)
        result = jnp.dot(grown, carried, precision=PRECISE) + jnp.dot(
            block_scores, fresh, precision=PRECISE
        )
        carried = whole_decay * carried + jnp.dot(tail_keys.T, fresh, precision=PRECISE)
        return (carried, result)

    final_state, results = lax.scan(
        jax.checkpoint(advance),
        state_in,
        (keys_wy, values_wy, scores, query_grown, key_tail, block_decay, keep_flags),
    )
    return (results.reshape(length, value_width), final_state)


def product(left, right):
    return jnp.dot(left, right, preferred_element_type=jnp.float32)


def transposed_left(left, right):
    return lax.dot_general(
        left, right, (((0,), (0,)), ((), ())), preferred_element_type=jnp.float32
    )


def transposed_right(left, right):
    return lax.dot_general(
        left, right, (((1,), (1,)), ((), ())), preferred_element_type=jnp.float32
    )


def row_total(partial_sums):
    return lax.psum(partial_sums, "tensor")


def full_rows(row_block):
    return lax.all_gather(row_block, "tensor", axis=1, tiled=True)


def tensor_total(terms):
    return lax.psum_scatter(terms, "tensor", scatter_dimension=1, tiled=True)


def fetch_weights(
    query_weight,
    key_weight,
    value_weight,
    outgate_weight,
    alpha_weight,
    beta_weight,
    output_weight,
    gate_weight,
    up_weight,
    down_weight,
):
    return (
        lax.all_gather(query_weight, "fsdp", axis=0, tiled=True),
        lax.all_gather(key_weight, "fsdp", axis=0, tiled=True),
        lax.all_gather(value_weight, "fsdp", axis=0, tiled=True),
        lax.all_gather(outgate_weight, "fsdp", axis=0, tiled=True),
        lax.all_gather(alpha_weight, "fsdp", axis=0, tiled=True),
        lax.all_gather(beta_weight, "fsdp", axis=0, tiled=True),
        lax.all_gather(output_weight, "fsdp", axis=1, tiled=True),
        lax.all_gather(gate_weight, "fsdp", axis=0, tiled=True),
        lax.all_gather(up_weight, "fsdp", axis=0, tiled=True),
        lax.all_gather(down_weight, "fsdp", axis=1, tiled=True),
    )


def spread_into(piece, whole_shape, start, axis_number):
    return lax.dynamic_update_slice_in_dim(
        jnp.zeros(whole_shape, jnp.float32), piece, start, axis_number
    )


def per_device(
    tokens,
    cotangent,
    lengths,
    norm_gain,
    query_weight,
    key_weight,
    value_weight,
    outgate_weight,
    alpha_weight,
    beta_weight,
    output_weight,
    conv_query,
    conv_key,
    conv_value,
    log_rate,
    step_bias,
    out_gain,
    ffn_gain,
    gate_weight,
    up_weight,
    down_weight,
):
    row_count, slice_width = tokens.shape
    full_width = slice_width * lax.axis_size("tensor")
    tensor_place = lax.axis_index("tensor")
    key_cols = query_weight.shape[1]
    value_cols = value_weight.shape[1]
    head_local = alpha_weight.shape[1]
    key_width = key_cols // head_local
    head_values = value_cols // head_local
    half_width = head_values // 2
    gathered = fetch_weights(
        query_weight,
        key_weight,
        value_weight,
        outgate_weight,
        alpha_weight,
        beta_weight,
        output_weight,
        gate_weight,
        up_weight,
        down_weight,
    )
    (
        query_full,
        key_full,
        value_full,
        outgate_full,
        alpha_full,
        beta_full,
        output_full,
        gate_full,
        up_full,
        down_full,
    ) = gathered
    starts = jnp.cumsum(lengths) - lengths
    places = lax.axis_index(("fsdp", "heads")) * row_count + jnp.arange(row_count, dtype=jnp.int32)
    latest = jnp.max(jnp.where(starts[None, :] <= places[:, None], starts[None, :], 0), axis=1)
    tap_index = jnp.arange(CONV, dtype=jnp.int32)
    valid_taps = ((places - latest)[:, None] >= CONV - 1 - tap_index[None, :]).astype(jnp.float32)
    token_vals = tokens.astype(jnp.float32)
    norm_slice = lax.dynamic_slice_in_dim(norm_gain, tensor_place * slice_width, slice_width)
    ffn_slice = lax.dynamic_slice_in_dim(ffn_gain, tensor_place * slice_width, slice_width)
    scale_in = lax.rsqrt(row_total(jnp.sum(token_vals * token_vals, axis=1)) / full_width + EPSILON)
    hidden_in = full_rows((token_vals * scale_in[:, None] * norm_slice).astype(jnp.bfloat16))
    query_pre = product(hidden_in, query_full)
    key_pre = product(hidden_in, key_full)
    value_pre = product(hidden_in, value_full)
    outgate_pre = product(hidden_in, outgate_full)
    alpha_pre = product(hidden_in, alpha_full)
    beta_pre = product(hidden_in, beta_full)
    joined = jnp.concatenate([query_pre, key_pre, value_pre], axis=1)
    rim_rows = shifted(joined[row_count - (CONV - 1) :], ("fsdp", "heads"), 1)
    padded = jnp.concatenate([rim_rows, joined], axis=0)
    kernel = jnp.concatenate(
        [
            lax.dynamic_slice_in_dim(conv_query, tensor_place * key_cols, key_cols, 1),
            lax.dynamic_slice_in_dim(conv_key, tensor_place * key_cols, key_cols, 1),
            lax.dynamic_slice_in_dim(conv_value, tensor_place * value_cols, value_cols, 1),
        ],
        axis=1,
    )
    rate_slice = lax.dynamic_slice_in_dim(log_rate, tensor_place * head_local, head_local)
    bias_slice = lax.dynamic_slice_in_dim(step_bias, tensor_place * head_local, head_local)

    def prepare(padded_in, kernel_in, alpha_in, beta_in, rate_in, bias_in):
        active = jax.nn.silu(convolve(padded_in, kernel_in, valid_taps))
        query_act = active[:, :key_cols].reshape(row_count, head_local, key_width)
        key_act = active[:, key_cols : 2 * key_cols].reshape(row_count, head_local, key_width)
        query_unit = (
            query_act
            * lax.rsqrt(jnp.sum(query_act * query_act, axis=2, keepdims=True) + EPSILON)
            * key_width ** (-0.5)
        )
        key_unit = key_act * lax.rsqrt(jnp.sum(key_act * key_act, axis=2, keepdims=True) + EPSILON)
        decays = -jnp.exp(rate_in) * jax.nn.softplus(alpha_in + bias_in)
        beta_rate = jax.nn.sigmoid(beta_in)
        return (query_unit, key_unit, active[:, 2 * key_cols :], decays, beta_rate)

    prepared, prepare_back = jax.vjp(
        prepare, padded, kernel, alpha_pre, beta_pre, rate_slice, bias_slice
    )
    query_unit, key_unit, value_act, decays, beta_rate = prepared
    query_four = jnp.repeat(query_unit.astype(jnp.bfloat16), 2, axis=1)
    key_four = jnp.repeat(key_unit.astype(jnp.bfloat16), 2, axis=1)
    value_four = value_act.astype(jnp.bfloat16).reshape(row_count, 2 * head_local, half_width)
    sent_main = jnp.concatenate([query_four, key_four, value_four], axis=2)
    sent_small = jnp.stack(
        [jnp.repeat(decays, 2, axis=1), jnp.repeat(beta_rate, 2, axis=1)], axis=2
    ).astype(jnp.bfloat16)
    head_main, head_small = (
        lax.all_to_all(sent_main, "heads", split_axis=1, concat_axis=0, tiled=True),
        lax.all_to_all(sent_small, "heads", split_axis=1, concat_axis=0, tiled=True),
    )
    span_rows = head_main.shape[0]
    mixer_query = head_main[:, 0, :key_width].astype(jnp.float32)
    mixer_key = head_main[:, 0, key_width : 2 * key_width].astype(jnp.float32)
    mixer_value = head_main[:, 0, 2 * key_width :].astype(jnp.float32)
    mixer_decay = head_small[:, 0, 0].astype(jnp.float32)
    mixer_beta = head_small[:, 0, 1].astype(jnp.float32)
    block_first = (
        lax.axis_index("fsdp") * span_rows + jnp.arange(span_rows // GROUP, dtype=jnp.int32) * GROUP
    )
    keep_flags = 1.0 - jnp.any(block_first[:, None] == starts[None, :], axis=1).astype(jnp.float32)
    augmented = jnp.concatenate(
        [mixer_value, jnp.zeros((span_rows, key_width), jnp.float32)], axis=1
    )
    start_state = jnp.concatenate(
        [jnp.zeros((key_width, half_width), jnp.float32), jnp.eye(key_width, dtype=jnp.float32)],
        axis=1,
    )
    joint_out, joint_end = delta_rule(
        mixer_query, mixer_key, augmented, mixer_decay, mixer_beta, keep_flags, start_state
    )
    carry_map = joint_out[:, half_width:]
    state_in = shifted(joint_end[:, :half_width], "fsdp", 1)
    mixed_out = joint_out[:, :half_width] + jnp.dot(carry_map, state_in, precision=PRECISE)
    returned = lax.all_to_all(
        mixed_out.astype(jnp.bfloat16).reshape(span_rows, 1, half_width),
        "heads",
        split_axis=0,
        concat_axis=1,
        tiled=True,
    )
    mixed_rows = returned.astype(jnp.float32).reshape(row_count, head_local, head_values)

    def gated_norm(mixed_in, gate_in, gain_in):
        return (
            mixed_in
            * lax.rsqrt(jnp.mean(mixed_in * mixed_in, axis=2, keepdims=True) + EPSILON)
            * gain_in
            * jax.nn.silu(gate_in)
        )

    normed, norm_back = jax.vjp(
        gated_norm, mixed_rows, outgate_pre.reshape(row_count, head_local, head_values), out_gain
    )
    normed_low = normed.reshape(row_count, value_cols).astype(jnp.bfloat16)
    middle = token_vals + tensor_total(product(normed_low, output_full))
    scale_mid = lax.rsqrt(row_total(jnp.sum(middle * middle, axis=1)) / full_width + EPSILON)
    hidden_mid = full_rows((middle * scale_mid[:, None] * ffn_slice).astype(jnp.bfloat16))
    gate_act = product(hidden_mid, gate_full)
    up_act = product(hidden_mid, up_full)
    gate_sig = jax.nn.sigmoid(gate_act)
    inner_act = (gate_act * gate_sig * up_act).astype(jnp.bfloat16)
    output_rows = (middle + tensor_total(product(inner_act, down_full))).astype(jnp.bfloat16)
    gathered = fetch_weights(
        query_weight,
        key_weight,
        value_weight,
        outgate_weight,
        alpha_weight,
        beta_weight,
        output_weight,
        gate_weight,
        up_weight,
        down_weight,
    )
    (
        query_full,
        key_full,
        value_full,
        outgate_full,
        alpha_full,
        beta_full,
        output_full,
        gate_full,
        up_full,
        down_full,
    ) = gathered
    cot_full = full_rows(cotangent)
    inner_grad = transposed_right(cot_full, down_full)
    grad_down = transposed_left(inner_act, cot_full)
    gate_grad = (inner_grad * up_act * gate_sig * (1.0 + gate_act * (1.0 - gate_sig))).astype(
        jnp.bfloat16
    )
    up_grad = (inner_grad * gate_act * gate_sig).astype(jnp.bfloat16)
    grad_gate = transposed_left(hidden_mid, gate_grad)
    grad_up = transposed_left(hidden_mid, up_grad)
    mid_grad = tensor_total(
        transposed_right(gate_grad, gate_full) + transposed_right(up_grad, up_full)
    )
    scaled_mid = mid_grad * ffn_slice
    mid_dot = row_total(jnp.sum(scaled_mid * middle, axis=1))
    middle_grad = (
        cotangent.astype(jnp.float32)
        + scale_mid[:, None] * scaled_mid
        - middle * (scale_mid * scale_mid * scale_mid * mid_dot / full_width)[:, None]
    )
    ffn_gain_grad = jnp.sum(mid_grad * middle * scale_mid[:, None], axis=0)
    attn_full = full_rows(middle_grad.astype(jnp.bfloat16))
    normed_grad = transposed_right(attn_full, output_full)
    grad_output = transposed_left(normed_low, attn_full)
    mixed_grad, outgate_grad, out_gain_grad = norm_back(
        normed_grad.reshape(row_count, head_local, head_values)
    )
    sent_grad = mixed_grad.astype(jnp.bfloat16).reshape(row_count, 2 * head_local, half_width)
    span_grad = lax.all_to_all(sent_grad, "heads", split_axis=1, concat_axis=0, tiled=True)[
        :, 0, :
    ].astype(jnp.float32)
    carry_grad = lax.dot_general(
        carry_map,
        span_grad,
        (((0,), (0,)), ((), ())),
        precision=PRECISE,
        preferred_element_type=jnp.float32,
    )
    end_grad = shifted(carry_grad.astype(jnp.bfloat16), "fsdp", -1).astype(carry_grad.dtype)

    def mixer(query_in, key_in, value_in, decay_in, beta_in):
        return delta_rule(query_in, key_in, value_in, decay_in, beta_in, keep_flags, state_in)

    mixer_result, mixer_back = jax.vjp(
        mixer, mixer_query, mixer_key, mixer_value, mixer_decay, mixer_beta
    )
    query_grad, key_grad, value_grad, decay_grad, beta_grad = mixer_back((span_grad, end_grad))
    back_main = (
        jnp.concatenate([query_grad, key_grad, value_grad], axis=1)
        .astype(jnp.bfloat16)
        .reshape(span_rows, 1, 2 * key_width + half_width)
    )
    back_small = (
        jnp.stack([decay_grad, beta_grad], axis=1).astype(jnp.bfloat16).reshape(span_rows, 1, 2)
    )
    token_main, token_small = (
        lax.all_to_all(back_main, "heads", split_axis=0, concat_axis=1, tiled=True),
        lax.all_to_all(back_small, "heads", split_axis=0, concat_axis=1, tiled=True),
    )
    token_main = token_main.astype(jnp.float32)
    token_small = token_small.astype(jnp.float32)
    query_unit_grad = (
        token_main[:, :, :key_width].reshape(row_count, head_local, 2, key_width).sum(axis=2)
    )
    key_unit_grad = (
        token_main[:, :, key_width : 2 * key_width]
        .reshape(row_count, head_local, 2, key_width)
        .sum(axis=2)
    )
    value_act_grad = token_main[:, :, 2 * key_width :].reshape(row_count, value_cols)
    decay_rows = token_small[:, :, 0].reshape(row_count, head_local, 2).sum(axis=2)
    beta_rows = token_small[:, :, 1].reshape(row_count, head_local, 2).sum(axis=2)
    padded_grad, kernel_grad, alpha_grad, beta_pre_grad, rate_grad, bias_grad = prepare_back(
        (query_unit_grad, key_unit_grad, value_act_grad, decay_rows, beta_rows)
    )
    rim_grad = shifted(padded_grad[: CONV - 1], ("fsdp", "heads"), -1)
    local_grad = padded_grad[CONV - 1 :]
    joined_grad = jnp.concatenate(
        [local_grad[: row_count - (CONV - 1)], local_grad[row_count - (CONV - 1) :] + rim_grad],
        axis=0,
    )
    query_low = joined_grad[:, :key_cols].astype(jnp.bfloat16)
    key_low = joined_grad[:, key_cols : 2 * key_cols].astype(jnp.bfloat16)
    value_low = joined_grad[:, 2 * key_cols :].astype(jnp.bfloat16)
    outgate_low = outgate_grad.reshape(row_count, value_cols).astype(jnp.bfloat16)
    alpha_low = alpha_grad.astype(jnp.bfloat16)
    beta_low = beta_pre_grad.astype(jnp.bfloat16)
    grad_query = transposed_left(hidden_in, query_low)
    grad_key = transposed_left(hidden_in, key_low)
    grad_value = transposed_left(hidden_in, value_low)
    grad_outgate = transposed_left(hidden_in, outgate_low)
    grad_alpha = transposed_left(hidden_in, alpha_low)
    grad_beta = transposed_left(hidden_in, beta_low)
    input_terms = (
        transposed_right(query_low, query_full)
        + transposed_right(key_low, key_full)
        + transposed_right(value_low, value_full)
    )
    input_terms = (
        input_terms
        + transposed_right(outgate_low, outgate_full)
        + transposed_right(alpha_low, alpha_full)
        + transposed_right(beta_low, beta_full)
    )
    in_grad = tensor_total(input_terms)
    scaled_in = in_grad * norm_slice
    in_dot = row_total(jnp.sum(scaled_in * token_vals, axis=1))
    tokens_grad = (
        middle_grad
        + scale_in[:, None] * scaled_in
        - token_vals * (scale_in * scale_in * scale_in * in_dot / full_width)[:, None]
    )
    norm_gain_grad = jnp.sum(in_grad * token_vals * scale_in[:, None], axis=0)
    reduced = (
        lax.psum_scatter(grad_query, ("fsdp", "heads"), scatter_dimension=0, tiled=True),
        lax.psum_scatter(grad_key, ("fsdp", "heads"), scatter_dimension=0, tiled=True),
        lax.psum_scatter(grad_value, ("fsdp", "heads"), scatter_dimension=0, tiled=True),
        lax.psum_scatter(grad_outgate, ("fsdp", "heads"), scatter_dimension=0, tiled=True),
        lax.psum_scatter(grad_alpha, ("fsdp", "heads"), scatter_dimension=0, tiled=True),
        lax.psum_scatter(grad_beta, ("fsdp", "heads"), scatter_dimension=0, tiled=True),
        lax.psum_scatter(grad_output, ("fsdp", "heads"), scatter_dimension=1, tiled=True),
        lax.psum_scatter(grad_gate, ("fsdp", "heads"), scatter_dimension=0, tiled=True),
        lax.psum_scatter(grad_up, ("fsdp", "heads"), scatter_dimension=0, tiled=True),
        lax.psum_scatter(grad_down, ("fsdp", "heads"), scatter_dimension=1, tiled=True),
    )
    small = lax.psum(
        (
            spread_into(kernel_grad[:, :key_cols], conv_query.shape, tensor_place * key_cols, 1),
            spread_into(
                kernel_grad[:, key_cols : 2 * key_cols], conv_key.shape, tensor_place * key_cols, 1
            ),
            spread_into(
                kernel_grad[:, 2 * key_cols :], conv_value.shape, tensor_place * value_cols, 1
            ),
            spread_into(rate_grad, log_rate.shape, tensor_place * head_local, 0),
            spread_into(bias_grad, step_bias.shape, tensor_place * head_local, 0),
            out_gain_grad,
            spread_into(norm_gain_grad, norm_gain.shape, tensor_place * slice_width, 0),
            spread_into(ffn_gain_grad, ffn_gain.shape, tensor_place * slice_width, 0),
        ),
        ("fsdp", "heads", "tensor"),
    )
    return (
        output_rows,
        tokens_grad,
        reduced[0],
        reduced[1],
        reduced[2],
        reduced[3],
        reduced[4],
        reduced[5],
        reduced[6],
        reduced[7],
        reduced[8],
        reduced[9],
        small[0],
        small[1],
        small[2],
        small[3],
        small[4],
        small[5],
        small[6],
        small[7],
    )


def solution(mesh):
    in_specs = (
        P(("fsdp", "heads"), "tensor"),
        P(("fsdp", "heads"), "tensor"),
        P(),
        P(),
        P("fsdp", "tensor"),
        P("fsdp", "tensor"),
        P("fsdp", "tensor"),
        P("fsdp", "tensor"),
        P("fsdp", "tensor"),
        P("fsdp", "tensor"),
        P("tensor", "fsdp"),
        P(),
        P(),
        P(),
        P(),
        P(),
        P(),
        P(),
        P("fsdp", "tensor"),
        P("fsdp", "tensor"),
        P("tensor", "fsdp"),
    )
    out_specs = (
        P(("fsdp", "heads"), "tensor"),
        P(("fsdp", "heads"), "tensor"),
        P(("fsdp", "heads"), "tensor"),
        P(("fsdp", "heads"), "tensor"),
        P(("fsdp", "heads"), "tensor"),
        P(("fsdp", "heads"), "tensor"),
        P(("fsdp", "heads"), "tensor"),
        P(("fsdp", "heads"), "tensor"),
        P("tensor", ("fsdp", "heads")),
        P(("fsdp", "heads"), "tensor"),
        P(("fsdp", "heads"), "tensor"),
        P("tensor", ("fsdp", "heads")),
        P(),
        P(),
        P(),
        P(),
        P(),
        P(),
        P(),
        P(),
    )
    return jax.shard_map(
        per_device, mesh=mesh, in_specs=in_specs, out_specs=out_specs, check_vma=False
    )
```

profile of v0, /device:TPU:8, one launch (start us, length us, event | category | flops | bytes accessed | tf_op | source)
XLA Modules:
  0.0 3649.2 jit_solution(2576248528311877060)
XLA Ops:
  10.1 9.0 psum.84
  31.4 36.8 %all-gather.11.cloned.1.call-done = bf16[1024,1024]{1,0:T(8,128)(2,1)} async-done(((bf16[1024,256]{1,0:T(8,128)(2,1)}), bf16[1024,1024]{1,0:T(8,128)(2,1)}) %all-gather.11.cloned.1.call-update) | async-done | bytes 2097168 | tf_op jit(solution)/shard_map/all_gather | solution.py:110
  93.6 6.4 fusion.45
  122.9 33.2 all-to-all-done.1
  173.2 7.8 fusion.61
  180.9 68.5 %custom-call.12 = f32[64,1,64,64]{0,2,3,1:T(8,128)} custom-call(f32[64,1,64,64]{0,3,2,1:T(8,128)} %get-tuple-element.781), custom_call_target="InvertDiagBlocksLowerTriangular" | custom-call | tf_op jit(solution)/shard_map/triangular_solve | solution.py:59
  271.7 544.9 %while.50 = (s32[]{:T(128)}, f32[128,256]{1,0:T(8,128)S(1)}, f32[64,64,256]{2,1,0:T(8,128)}, f32[64]{0:T(128)S(1)}, f32[64]{0:T(128)S(1)}, /*index=5*/f32[64,64,...) while((s32[]{:T(128)}, f32[128,256]{1,0:T(8,128)S(1)}, ...), condition=%wide.region_9.11_spmd, body=%wide.region_8.10_spmd.sunk | while | flops 88276992 | bytes 1119365 | solution.py:81
  836.7 13.8 all-to-all-done.2
  875.9 76.0 %reduce-scatter.19.cloned.1.call-done = f32[1024,256]{1,0:T(8,128)} async-done(((f32[1024,1024]{1,0:T(8,128)}), f32[1024,256]{1,0:T(8,128)}) %reduce-scatter.19.cloned.1.call-update) | async-done | bytes 1048592 | tf_op jit(solution)/shard_map/reduce_scatter | solution.py:114
  954.3 9.4 psum.85
  968.4 43.5 %all-gather.19.cloned.1.call-done = bf16[1024,1024]{1,0:T(8,128)(2,1)} async-done(((bf16[1024,256]{1,0:T(8,128)(2,1)}), bf16[1024,1024]{1,0:T(8,128)(2,1)}) %all-gather.19.cloned.1.call-update) | async-done | bytes 2097168 | tf_op jit(solution)/shard_map/all_gather | solution.py:110
  1017.2 5.7 all-gather.23.cloned.1.call-done
  1028.2 7.2 all-gather.25.cloned.1.call-done
  1035.3 47.4 %all-gather.27.cloned.1.call-done = bf16[1024,1024]{1,0:T(8,128)(2,1)} async-done(((bf16[1024,256]{1,0:T(8,128)(2,1)}), bf16[1024,1024]{1,0:T(8,128)(2,1)}) %all-gather.27.cloned.1.call-update) | async-done | bytes 2097168 | tf_op jit(solution)/shard_map/all_gather | solution.py:110
  1082.7 7.7 multiply_convert_fusion
  1096.9 76.4 %reduce-scatter.23.cloned.1.call-done = f32[1024,256]{1,0:T(8,128)} async-done(((f32[1024,1024]{1,0:T(8,128)}), f32[1024,256]{1,0:T(8,128)}) %reduce-scatter.23.cloned.1.call-update) | async-done | bytes 1048592 | tf_op jit(solution)/shard_map/reduce_scatter | solution.py:114
  1175.9 9.6 psum.86
  1194.2 39.1 %all-gather.29.cloned.1.call-done = bf16[1024,1024]{1,0:T(8,128)(2,1)} async-done(((bf16[1024,256]{1,0:T(8,128)(2,1)}), bf16[1024,1024]{1,0:T(8,128)(2,1)}) %all-gather.29.cloned.1.call-update) | async-done | bytes 2097168 | tf_op jit(solution)/shard_map/all_gather | solution.py:110
  1233.3 6.6 fusion.52
  1278.4 369.9 %while.51 = (s32[]{:T(128)}, f32[128,128]{1,0:T(8,128)S(1)}, f32[64,128,128]{2,1,0:T(8,128)}, f32[64]{0:T(128)S(1)}, f32[64]{0:T(128)S(1)}, /*index=5*/f32[64,64...) while((s32[]{:T(128)}, f32[128,128]{1,0:T(8,128)S(1)}, ...), condition=%wide.region_22.24_spmd, body=%wide.region_21.23_spmd.sunk | while | flops 25239552 | bytes 495221 | solution.py:81
  1659.2 993.7 %while.52 = (s32[]{:T(128)}, f32[128,128]{1,0:T(8,128)S(1)}, f32[64,64,128]{2,1,0:T(8,128)}, f32[64,64,128]{2,1,0:T(8,128)}, f32[64,64,64]{2,1,0:T(8,128)}, /*in...) while((s32[]{:T(128)}, f32[128,128]{1,0:T(8,128)S(1)}, ...), condition=%wide.region_25.27_spmd, body=%wide.region_23.26_spmd.sunk | while | flops 100859904 | bytes 1951001 | solution.py:81
  2652.9 5.8 fusion.137
  2666.4 5.8 fusion.139
  2683.2 5.8 fusion.64
  2720.3 17.5 copy.310
  2737.7 17.0 copy.311
  2756.1 17.3 copy.309
  2783.6 12.3 pad_maximum_fusion
  2795.9 68.7 %reduce.21 = bf16[4096,384]{1,0:T(8,128)(2,1)} reduce(bf16[4096,1,384]{2,1,0:T(2,128)(2,1)} %pad_maximum_fusion, bf16[]{:T(256)} %broadcast.427), dimensions={1}, to_apply=%pad_maximum_fusion.reduce_sub_computation | reduce | bytes 6291458 | tf_op jit(solution)/shard_map/concatenate | solution.py:387
  2898.5 12.8 all-to-all-done.4
  2911.3 6.3 reshape.710
  2940.8 9.2 multiply_reduce_fusion.4
  2958.5 10.0 collective-permute-done.3
  2974.0 6.5 add_add_fusion
  2980.6 5.6 fusion.133
  2986.3 5.8 fusion.150
  3025.3 31.9 reduce-scatter.25.cloned.1.call-done
  3059.3 9.5 psum.87
  3068.9 68.0 %reduce-scatter.21.cloned.1.call-done = f32[1024,256]{1,0:T(8,128)} async-done(((f32[1024,1024]{1,0:T(8,128)}), f32[1024,256]{1,0:T(8,128)}) %reduce-scatter.21.cloned.1.call-update) | async-done | bytes 1048592 | tf_op jit(solution)/shard_map/reduce_scatter | solution.py:114
  3139.9 46.2 %reduce-scatter.37.cloned.1.call-done = f32[128,704]{0,1:T(8,128)} async-done(((f32[1024,704]{0,1:T(8,128)}), f32[128,704]{0,1:T(8,128)}) %reduce-scatter.37.cloned.1.call-update) | async-done | bytes 360464 | tf_op jit(solution)/shard_map/reduce_scatter | solution.py:460
  3186.2 49.1 %reduce-scatter.39.cloned.1.call-done = f32[128,704]{0,1:T(8,128)} async-done(((f32[1024,704]{0,1:T(8,128)}), f32[128,704]{0,1:T(8,128)}) %reduce-scatter.39.cloned.1.call-update) | async-done | bytes 360464 | tf_op jit(solution)/shard_map/reduce_scatter | solution.py:461
  3235.2 48.9 %reduce-scatter.41.cloned.1.call-done = f32[704,128]{1,0:T(8,128)} async-done(((f32[704,1024]{1,0:T(8,128)}), f32[704,128]{1,0:T(8,128)}) %reduce-scatter.41.cloned.1.call-update) | async-done | bytes 360464 | tf_op jit(solution)/shard_map/reduce_scatter | solution.py:462
  3284.1 45.3 %reduce-scatter.35.cloned.1.call-done = f32[512,128]{1,0:T(8,128)} async-done(((f32[512,1024]{1,0:T(8,128)}), f32[512,128]{1,0:T(8,128)}) %reduce-scatter.35.cloned.1.call-update) | async-done | bytes 262160 | tf_op jit(solution)/shard_map/reduce_scatter | solution.py:459
  3329.4 45.1 %reduce-scatter.33.cloned.1.call-done = f32[128,512]{1,0:T(8,128)} async-done(((f32[1024,512]{1,0:T(8,128)}), f32[128,512]{1,0:T(8,128)}) %reduce-scatter.33.cloned.1.call-update) | async-done | bytes 262160 | tf_op jit(solution)/shard_map/reduce_scatter | solution.py:456
  3374.6 40.1 %reduce-scatter.27.cloned.1.call-done = f32[128,256]{1,0:T(8,128)} async-done(((f32[1024,256]{1,0:T(8,128)}), f32[128,256]{1,0:T(8,128)}) %reduce-scatter.27.cloned.1.call-update) | async-done | bytes 131088 | tf_op jit(solution)/shard_map/reduce_scatter | solution.py:453
  3414.7 40.1 %reduce-scatter.29.cloned.1.call-done = f32[128,256]{1,0:T(8,128)} async-done(((f32[1024,256]{1,0:T(8,128)}), f32[128,256]{1,0:T(8,128)}) %reduce-scatter.29.cloned.1.call-update) | async-done | bytes 131088 | tf_op jit(solution)/shard_map/reduce_scatter | solution.py:454
  3454.9 45.3 %reduce-scatter.31.cloned.1.call-done = f32[128,512]{1,0:T(8,128)} async-done(((f32[1024,512]{1,0:T(8,128)}), f32[128,512]{1,0:T(8,128)}) %reduce-scatter.31.cloned.1.call-update) | async-done | bytes 262160 | tf_op jit(solution)/shard_map/reduce_scatter | solution.py:455
  3500.2 132.1 %all-reduce.18.cloned.1.call-done = (f32[4,1024]{1,0:T(4,128)}, f32[4,1024]{1,0:T(4,128)}, f32[4,2048]{1,0:T(4,128)}, f32[8]{0:T(128)}, f32[8]{0:T(128)}, /*index=5*/f32[256]{0:T(256)}, f32[1024]{0:T(1024)}, f32[1024]{0:T(1024)}) async-done(((f32[4,1024]{1,0:T(4,128)}, f32[4,1024]{1,0:T(4,128)}, f32[4,2048]{1,0:T(4,128)}, f32[8]{0:T(128)}, f32[8]{0:T(128)}, /*index=5*/f32[256]{0:T(256)}, f32[1024]{0:T(1024)}, ...) | async-done | bytes 74832 | tf_op jit(solution)/shard_map/psum | solution.py:464
  (2420 shorter events, 2314.0 us)
Async XLA Ops:
  7.3 24.1 all-gather.13.cloned.1.call-start
  8.0 60.2 %all-gather.11.cloned.1.call-start = ((), (), s32[]{:S(2)}) async-start(), calls=%async_computation.20 | async-start | bytes 2621440 | tf_op jit(solution)/shard_map/all_gather | solution.py:110
  31.3 62.2 %copy-start.90 = (f32[1,1024]{1,0:T(1,128)}, f32[1,1024]{1,0:T(1,128)S(1)}, u32[]{:S(2)}) copy-start(f32[1,1024]{1,0:T(1,128)S(1)} %get-tuple-element.788) | copy-start | bytes 12292
  31.3 62.2 %copy-start.92 = (f32[1,1024]{1,0:T(1,128)}, f32[1,1024]{1,0:T(1,128)S(1)}, u32[]{:S(2)}) copy-start(f32[1,1024]{1,0:T(1,128)S(1)} %get-tuple-element.789) | copy-start | bytes 12292
  31.3 62.2 %copy-start.94 = (f32[1,1024]{1,0:T(1,128)}, f32[1,1024]{1,0:T(1,128)S(1)}, u32[]{:S(2)}) copy-start(f32[1,1024]{1,0:T(1,128)S(1)} %get-tuple-element.790) | copy-start | bytes 12292
  31.3 62.2 %copy-start.96 = (f32[1,1024]{1,0:T(1,128)}, f32[1,1024]{1,0:T(1,128)S(1)}, u32[]{:S(2)}) copy-start(f32[1,1024]{1,0:T(1,128)S(1)} %get-tuple-element.791) | copy-start | bytes 12292
  76.6 13.6 collective-permute-start
  82.6 31.9 all-to-all-start
  114.4 41.7 %all-to-all-start.1 = ((bf16[1024,4,384]{2,0,1:T(8,128)(2,1)}), bf16[1024,4,384]{2,0,1:T(8,128)(2,1)}, u32[]{:S(2)}, u32[]{:S(2)}) async-start(bf16[1024,4,384]{2,0,1:T(8,128)(2,1)} %pad_maximum_fusion.2), calls=%async_computation.1 | async-start | bytes 6291456 | tf_op jit(solution)/shard_map/all_to_all | solution.py:261
  119.1 745.4 %all-gather.15.cloned.1.call-start = ((), (), s32[]{:S(2)}) async-start(), calls=%async_computation.22 | async-start | bytes 1572864 | tf_op jit(solution)/shard_map/all_gather | solution.py:133
  816.7 2.8 collective-permute-start.1
  831.8 18.8 all-to-all-start.2
  836.1 33.6 all-gather.17.cloned.1.call-start
  836.7 115.2 %reduce-scatter.19.cloned.1.call-start = ((), (), s32[]{:S(2)}) async-start(), calls=%async_computation.24 | async-start | bytes 5242880 | tf_op jit(solution)/shard_map/reduce_scatter | solution.py:114
  874.5 93.8 %all-gather.21.cloned.1.call-start = ((), (), s32[]{:S(2)}) async-start(), calls=%async_computation.26 | async-start | bytes 2162688 | tf_op jit(solution)/shard_map/all_gather | solution.py:137
  875.1 136.8 %all-gather.19.cloned.1.call-start = ((), (), s32[]{:S(2)}) async-start(), calls=%async_computation.25 | async-start | bytes 2621440 | tf_op jit(solution)/shard_map/all_gather | solution.py:110
  875.9 309.6 %copy-start.104 = (f32[256]{0:T(256)}, f32[256]{0:T(256)S(1)}, u32[]{:S(2)}) copy-start(f32[256]{0:T(256)S(1)} %dynamic_slice.149) | copy-start | bytes 3076
  963.7 221.8 %copy-start.65 = (f32[1024]{0:T(1024)}, f32[1024]{0:T(1024)S(1)}, u32[]{:S(2)}) copy-start(f32[1024]{0:T(1024)S(1)} %add_rsqrt_fusion.2) | copy-start | bytes 12292
  966.0 56.9 %all-gather.23.cloned.1.call-start = ((), (), s32[]{:S(2)}) async-start(), calls=%async_computation.27 | async-start | bytes 2162688 | tf_op jit(solution)/shard_map/all_gather | solution.py:138
  966.7 68.6 %all-gather.25.cloned.1.call-start = ((), (), s32[]{:S(2)}) async-start(), calls=%async_computation.28 | async-start | bytes 2162688 | tf_op jit(solution)/shard_map/all_gather | solution.py:139
  967.5 115.2 %all-gather.27.cloned.1.call-start = ((), (), s32[]{:S(2)}) async-start(), calls=%async_computation.30 | async-start | bytes 2621440 | tf_op jit(solution)/shard_map/all_gather | solution.py:110
  968.1 205.3 %reduce-scatter.23.cloned.1.call-start = ((), (), s32[]{:S(2)}) async-start(), calls=%async_computation.31 | async-start | bytes 5242880 | tf_op jit(solution)/shard_map/reduce_scatter | solution.py:114
  1096.9 136.5 %all-gather.29.cloned.1.call-start = ((), (), s32[]{:S(2)}) async-start(), calls=%async_computation.32 | async-start | bytes 2621440 | tf_op jit(solution)/shard_map/all_gather | solution.py:110
  1254.9 18.1 all-to-all-start.3
  1276.7 374.6 %collective-permute-start.2 = (bf16[128,128]{1,0:T(8,128)(2,1)S(1)}, bf16[128,128]{1,0:T(8,128)(2,1)S(1)}, u32[]{:S(2)}, u32[]{:S(2)}) collective-permute-start(bf16[128,128]{1,0:T(8,128)(2,1)S(1)} %fusion.68), channel_id=1, source_target_pairs={{16,0},{17,1},{18,2},{19,3},{20,4},{21,5},{22,6},{23,7},{24,8},{25... | collective-permute-start | bytes 98312 | tf_op jit(solution)/shard_map/ppermute | solution.py:17
  2780.1 89.0 %all-to-all-start.5 = ((bf16[4,2,1024]{2,1,0:T(2,128)(2,1)}), bf16[4,2,1024]{2,1,0:T(2,128)(2,1)S(1)}, u32[]{:S(2)}, u32[]{:S(2)}) async-start(bf16[4,2,1024]{2,1,0:T(2,128)(2,1)} %reshape.707), calls=%async_computation.8 | async-start | bytes 32768 | tf_op jit(solution)/shard_map/all_to_all | solution.py:396
  2869.1 42.2 %all-to-all-start.4 = ((bf16[4,2,196608]{2,1,0:T(2,128)(2,1)}), bf16[4,2,196608]{2,1,0:T(2,128)(2,1)}, u32[]{:S(2)}, u32[]{:S(2)}) async-start(bf16[4,2,196608]{2,1,0:T(2,128)(2,1)} %reshape.709), calls=%async_computation.7 | async-start | bytes 6291456 | tf_op jit(solution)/shard_map/all_to_all | solution.py:395
  2873.9 148.4 %reduce-scatter.43.cloned.1.call-start = ((), (), s32[]{:S(2)}) async-start(), calls=%async_computation.42 | async-start | bytes 589824
  2890.8 132.9 %reduce-scatter.45.cloned.1.call-start = ((), (), s32[]{:S(2)}) async-start(), calls=%async_computation.43 | async-start | bytes 589824
  2892.5 164.8 %reduce-scatter.25.cloned.1.call-start = ((), (), s32[]{:S(2)}) async-start(), calls=%async_computation.33 | async-start | bytes 5242880 | tf_op jit(solution)/shard_map/reduce_scatter | solution.py:114
  2951.9 16.5 collective-permute-start.3
  2980.5 156.3 %reduce-scatter.21.cloned.1.call-start = ((), (), s32[]{:S(2)}) async-start(), calls=%async_computation.29 | async-start | bytes 5242880 | tf_op jit(solution)/shard_map/reduce_scatter | solution.py:114
  2986.2 200.0 %reduce-scatter.37.cloned.1.call-start = ((), (), s32[]{:S(2)}) async-start(), calls=%async_computation.39 | async-start | bytes 3244032 | tf_op jit(solution)/shard_map/reduce_scatter | solution.py:460
  2992.1 243.1 %reduce-scatter.39.cloned.1.call-start = ((), (), s32[]{:S(2)}) async-start(), calls=%async_computation.40 | async-start | bytes 3244032 | tf_op jit(solution)/shard_map/reduce_scatter | solution.py:461
  2997.4 286.7 %reduce-scatter.41.cloned.1.call-start = ((), (), s32[]{:S(2)}) async-start(), calls=%async_computation.41 | async-start | bytes 3244032 | tf_op jit(solution)/shard_map/reduce_scatter | solution.py:462
  3002.9 326.5 %reduce-scatter.35.cloned.1.call-start = ((), (), s32[]{:S(2)}) async-start(), calls=%async_computation.38 | async-start | bytes 2359296 | tf_op jit(solution)/shard_map/reduce_scatter | solution.py:459
  3008.4 366.2 %reduce-scatter.33.cloned.1.call-start = ((), (), s32[]{:S(2)}) async-start(), calls=%async_computation.37 | async-start | bytes 2359296 | tf_op jit(solution)/shard_map/reduce_scatter | solution.py:456
  3012.3 402.4 %reduce-scatter.27.cloned.1.call-start = ((), (), s32[]{:S(2)}) async-start(), calls=%async_computation.34 | async-start | bytes 1179648 | tf_op jit(solution)/shard_map/reduce_scatter | solution.py:453
  3015.1 439.8 %reduce-scatter.29.cloned.1.call-start = ((), (), s32[]{:S(2)}) async-start(), calls=%async_computation.35 | async-start | bytes 1179648 | tf_op jit(solution)/shard_map/reduce_scatter | solution.py:454
  3016.9 483.3 %reduce-scatter.31.cloned.1.call-start = ((), (), s32[]{:S(2)}) async-start(), calls=%async_computation.36 | async-start | bytes 2359296 | tf_op jit(solution)/shard_map/reduce_scatter | solution.py:455
  3020.9 116.0 %copy-start.18 = (f32[1024,256]{1,0:T(8,128)S(1)}, f32[1024,256]{1,0:T(8,128)}, u32[]{:S(2)}) copy-start(f32[1024,256]{1,0:T(8,128)} %get-tuple-element.739) | copy-start | bytes 3145732
  3020.9 116.0 %copy-start.35 = (f32[1024,256]{1,0:T(8,128)S(1)}, f32[1024,256]{1,0:T(8,128)}, u32[]{:S(2)}) copy-start(f32[1024,256]{1,0:T(8,128)} %reduce-scatter.23.cloned.1.call-done) | copy-start | bytes 3145732
  3020.9 116.0 %copy-start.49 = (bf16[1024,256]{1,0:T(8,128)(2,1)S(1)}, bf16[1024,256]{1,0:T(8,128)(2,1)}, u32[]{:S(2)}) copy-start(bf16[1024,256]{1,0:T(8,128)(2,1)} %param.34) | copy-start | bytes 1572868
  3020.9 116.0 %copy-start.66 = (f32[1024]{0:T(1024)S(1)}, f32[1024]{0:T(1024)}, u32[]{:S(2)}) copy-start(f32[1024]{0:T(1024)} %copy-done.65) | copy-start | bytes 12292
  3020.9 116.0 %copy-start.87 = (f32[1024]{0:T(1024)S(1)}, f32[1024]{0:T(1024)}, u32[]{:S(2)}) copy-start(f32[1024]{0:T(1024)} %copy-done.86) | copy-start | bytes 12292
  3020.9 116.0 %copy-start.105 = (f32[256]{0:T(256)S(1)}, f32[256]{0:T(256)}, u32[]{:S(2)}) copy-start(f32[256]{0:T(256)} %copy-done.104) | copy-start | bytes 3076
  3021.0 611.3 %all-reduce.18.cloned.1.call-start = ((), (), s32[]{:S(2)}) async-start(), calls=%async_computation.44 | async-start | bytes 151552 | tf_op jit(solution)/shard_map/psum | solution.py:464
  3068.9 573.5 %copy-start.1 = (f32[4,2048]{1,0:T(4,128)S(1)}, f32[4,2048]{1,0:T(4,128)}, u32[]{:S(2)}) copy-start(f32[4,2048]{1,0:T(4,128)} %param.46) | copy-start | bytes 98308
  (116 other events, 1531.8 us)
Sparse Core Ops, SparseCore 0:
  9.7 10.4 all-gather.12
  22.3 45.8 all-gather.10
  121.5 11.3 all-gather.14
  838.1 11.1 all-gather.16
  874.6 77.2 reduce-scatter.18
  953.3 10.3 all-gather.20
  966.1 45.6 all-gather.18
  1013.5 9.3 all-gather.22
  1024.5 10.7 all-gather.24
  1036.8 45.8 all-gather.26
  1097.0 76.2 reduce-scatter.22
  1188.5 44.8 all-gather.28
  2890.9 35.0 reduce-scatter.42
  2929.2 34.3 reduce-scatter.44
  2980.7 76.5 reduce-scatter.24
  3059.5 77.3 reduce-scatter.20
  3140.7 45.4 reduce-scatter.36
  3190.4 44.8 reduce-scatter.38
  3239.2 44.8 reduce-scatter.40
  3288.2 41.2 reduce-scatter.34
  3333.3 41.2 reduce-scatter.32
  3378.6 36.0 reduce-scatter.26
  3418.8 36.0 reduce-scatter.28
  3458.9 41.2 reduce-scatter.30
  3507.7 124.4 all-reduce.17
where the time goes:
time: 3710 us; the launch traced here: 3650 us
  matrix products  1430 us (39%)
  waiting for transfers between devices  1010 us (27%)
  local copies, waits for them, and re-layouts  763 us (21%)
  other arithmetic  345 us (9%)
  blocking collectives  45.6 us (1%)
    dot_general x320, matrix products, advance(): fresh = wy_values - jnp.dot(wy_keys, carried, precision=PRECISE)  421 us
    dot_general x256, matrix products, advance(): jnp.dot(tail_keys.T, fresh, precision=PRECISE)  370 us
    dot_general x192, matrix products, advance(): jnp.dot(grown, carried, precision=PRECISE)  259 us
    reduce_scatter x4, waiting for transfers between devices, tensor_total(): return lax.psum_scatter(terms, 'tensor', scatter_dimension=1, tiled=True)  252 us
    squeeze x320, local copies, waits for them, and re-layouts, delta_rule(): lax.scan(jax.checkpoint(advance), state_in, (keys_wy, values_wy, scores,...  251 us
    dynamic_slice x384, local copies, waits for them, and re-layouts, delta_rule(): lax.scan(jax.checkpoint(advance), state_in, (keys_wy, values_wy, scores,...  224 us
    dot_general x192, matrix products, advance(): jnp.dot(block_scores, fresh, precision=PRECISE)  207 us
    all_gather x4, waiting for transfers between devices, full_rows(): return lax.all_gather(row_block, 'tensor', axis=1, tiled=True)  167 us
  transfers between devices with their start and end apart: 35, of which 26 were waited for; matrix products, arithmetic and copies ran while one was open for 36% of the time, Pallas kernels for 0%

commit v1 on v0

v1 whole, which is shorter than its diff:
```python
import functools

import jax
import jax.numpy as jnp
from jax import lax
from jax.experimental import pallas as pl
from jax.experimental.pallas import tpu as pltpu
from jax.sharding import PartitionSpec as P

CONV = 4
GROUP = 64
RIM = 16
PACK = 256
LANES = 128
LONGEST = 4096
EPSILON = 1e-06
FH = ("fsdp", "heads")
ALL = ("fsdp", "heads", "tensor")
BF = jnp.bfloat16
F32 = jnp.float32
VMEM_LIMIT = 56 * 1024 * 1024
INVERSE_PASSES = 1


def shifted(shard, axis, by):
    devices = lax.axis_size(axis)
    pairs = [(i, i + by) for i in range(devices) if 0 <= i + by < devices]
    return lax.ppermute(shard, axis, pairs)


def dot_on(left, right, left_dim, right_dim):
    return lax.dot_general(
        left.astype(BF),
        right.astype(BF),
        (((left_dim,), (right_dim,)), ((), ())),
        preferred_element_type=F32,
    )


def mm(left, right):
    return dot_on(left, right, 1, 0)


def mm_tn(left, right):
    return dot_on(left, right, 0, 0)


def mm_nt(left, right):
    return dot_on(left, right, 1, 1)


def mm_fine(left, right):
    if INVERSE_PASSES == 1:
        return mm(left, right)
    left_high, right_high = left.astype(BF), right.astype(BF)
    left_low = left - left_high.astype(F32)
    right_low = right - right_high.astype(F32)
    return mm(left_high, right_high) + mm(left_low, right_high) + mm(left_high, right_low)


def sigmoid(value):
    return 1.0 / (1.0 + jnp.exp(-value))


def softplus(value):
    return jnp.maximum(value, 0.0) + jnp.log(1.0 + jnp.exp(-jnp.abs(value)))


def window_taps(window, rows):
    total = window.shape[0]
    return [pltpu.roll(window, total - (RIM - CONV + 1 + j), 0)[:rows] for j in range(CONV)]


def pack_masks():
    row = lax.broadcasted_iota(jnp.int32, (PACK, PACK), 0)
    col = lax.broadcasted_iota(jnp.int32, (PACK, PACK), 1)
    apart = row ^ col
    same = apart < GROUP
    return row, col, apart, same, same & (row >= col), same & (row > col)


def packed_decay(decay, masks):
    row, col, apart, same, lower, strict = masks
    spread = jnp.broadcast_to(decay, (PACK, PACK))
    decay_row = jnp.sum(jnp.where(apart == 0, spread, 0.0), axis=0, keepdims=True)
    gam_row = jnp.sum(jnp.where(same & (row <= col), spread, 0.0), axis=0, keepdims=True)
    spread_row = jnp.broadcast_to(decay_row, (PACK, PACK))
    gam = jnp.sum(jnp.where(lower, spread_row, 0.0), axis=1, keepdims=True)
    last = jnp.sum(jnp.where(same, spread_row, 0.0), axis=1, keepdims=True)
    fading = jnp.where(lower, jnp.exp(jnp.where(lower, gam - gam_row, 0.0)), 0.0)
    return gam, last, fading


def rates_of(small, rate, bias):
    decay_tile = -jnp.exp(rate) * softplus(small + bias)
    return decay_tile, sigmoid(small)


def load_window(pre_ref, group, first, width, rows):
    start = group * PACK
    before = jnp.where(group == 0, rows, start - RIM)
    head = pre_ref[pl.ds(pl.multiple_of(before, RIM), RIM), first : first + width]
    body = pre_ref[pl.ds(pl.multiple_of(start, PACK), PACK), first : first + width]
    return jnp.concatenate([head, body], axis=0)


def active_of(window, taps_ref, valid, first, width):
    pieces = window_taps(window, PACK)
    conv = None
    for j in range(CONV):
        term = pieces[j] * taps_ref[j : j + 1, first : first + width] * valid[:, j : j + 1]
        conv = term if conv is None else conv + term
    return conv, pieces


def forward_kernel(
    keep_ref,
    pre_ref,
    small_ref,
    taps_ref,
    valid_ref,
    rate_ref,
    bias_ref,
    qkv_ref,
    inverse_ref,
    w_ref,
    u_ref,
    fold_ref,
    states_ref,
    local_ref,
    carry_ref,
    ends_ref,
    fresh_ref,
    start_ref,
    last_ref,
    joint_ref,
    *,
    heads,
    rows,
    key_width,
    value_width,
):
    groups = rows // PACK
    inner = PACK // GROUP
    key_cols = heads * key_width

    def prepare(group, _):
        start = pl.multiple_of(group * PACK, PACK)
        span = pl.ds(start, PACK)
        valid = valid_ref[span, :]
        for tile in range(2 * heads):
            first = tile * key_width
            window = load_window(pre_ref, group, first, key_width, rows)
            conv, _ = active_of(window, taps_ref, valid, first, key_width)
            act = conv * sigmoid(conv)
            scale = lax.rsqrt(jnp.sum(act * act, axis=1, keepdims=True) + EPSILON)
            if tile < heads:
                scale = scale * key_width ** (-0.5)
            qkv_ref[span, first : first + key_width] = (act * scale).astype(BF)
        for tile in range(heads):
            first = 2 * key_cols + tile * value_width
            window = load_window(pre_ref, group, first, value_width, rows)
            conv, _ = active_of(window, taps_ref, valid, first, value_width)
            qkv_ref[span, first : first + value_width] = (conv * sigmoid(conv)).astype(BF)
        return 0

    lax.fori_loop(0, groups, prepare, 0)

    def solve(group, _):
        masks = pack_masks()
        row, col, apart, same, lower, strict = masks
        start = pl.multiple_of(group * PACK, PACK)
        span = pl.ds(start, PACK)
        decay_tile, beta_tile = rates_of(small_ref[span, :], rate_ref[...], bias_ref[...])
        items = []
        for head in range(heads):
            decay = decay_tile[:, head : head + 1].astype(BF).astype(F32)
            beta = beta_tile[:, heads + head : heads + head + 1].astype(BF).astype(F32)
            key = qkv_ref[span, key_cols + head * key_width : key_cols + (head + 1) * key_width]
            gam, last, fading = packed_decay(decay, masks)
            gram = mm_nt(key, key)
            system = jnp.where(strict, fading * beta * gram, 0.0)
            inverse = jnp.where(apart == 0, 1.0, 0.0) - jnp.where(apart == 1, system, 0.0)
            items.append([decay, beta, key, gam, last, fading, system, inverse])
        level = 1
        while (1 << level) < GROUP:
            parts = [
                mm_fine(jnp.where((apart >> level) == 1, item[6], 0.0), item[7]) for item in items
            ]
            steps = [mm_fine(item[7], part) for item, part in zip(items, parts)]
            for item, step in zip(items, steps):
                item[7] = item[7] - step
            level += 1
        for head in range(heads):
            decay, beta, key, gam, last, fading, system, inverse = items[head]
            query = qkv_ref[span, head * key_width : (head + 1) * key_width]
            first = 2 * key_cols + head * value_width
            value = qkv_ref[span, first : first + value_width]
            key_f = key.astype(F32)
            growth = jnp.exp(gam)
            inverse_low = inverse.astype(BF)
            inverse_ref[group * heads + head] = inverse_low
            w = mm(inverse_low, beta * growth * key_f)
            u = mm(inverse_low, beta * value.astype(F32))
            w_low, u_low = w.astype(BF), u.astype(BF)
            w_ref[span, head * key_width : (head + 1) * key_width] = w_low
            u_ref[span, head * value_width : (head + 1) * value_width] = u_low
            scores = (mm_nt(query, key) * fading).astype(BF)
            query_w = growth * query.astype(F32) - mm(scores, w_low)
            start_ref[span, head * value_width : (head + 1) * value_width] = mm(scores, u_low)
            tail = jnp.exp(last - gam) * key_f
            block_of = lax.broadcasted_iota(jnp.int32, (PACK, 1), 0) // GROUP
            whole = jnp.exp(last)
            for b in range(inner):
                index = (group * inner + b) * heads + head
                tail_b = jnp.where(block_of == b, tail, 0.0).astype(BF)
                fold_ref[index, :key_width, :] = mm_tn(tail_b, w_low).astype(BF)
                fold_ref[index, key_width:, :] = query_w[b * GROUP : (b + 1) * GROUP].astype(BF)
                fresh_ref[index] = mm_tn(tail_b, u_low)
                last_ref[index] = jnp.broadcast_to(
                    whole[b * GROUP : b * GROUP + 1], (8, LANES)
                )
        return 0

    lax.fori_loop(0, groups, solve, 0)

    unit = jnp.where(
        lax.broadcasted_iota(jnp.int32, (key_width, key_width), 0)
        == lax.broadcasted_iota(jnp.int32, (key_width, key_width), 1),
        1.0,
        0.0,
    )
    for head in range(heads):
        joint_ref[head, :, :value_width] = jnp.zeros((key_width, value_width), F32)
        joint_ref[head, :, value_width:] = unit
    for block in range(rows // GROUP):
        span = slice(block * GROUP, (block + 1) * GROUP)
        for head in range(heads):
            index = block * heads + head
            joint = joint_ref[head] * keep_ref[block]
            joint_low = joint.astype(BF)
            states_ref[index] = joint_low
            moved = mm(fold_ref[index], joint_low)
            whole = last_ref[index, 0:1, 0:1]
            fresh = whole * joint - moved[:key_width]
            joint_ref[head, :, :value_width] = fresh[:, :value_width] + fresh_ref[index]
            joint_ref[head, :, value_width:] = fresh[:, value_width:]
            cols = slice(head * value_width, (head + 1) * value_width)
            local_ref[span, cols] = moved[key_width:, :value_width] + start_ref[span, cols]
            carry_ref[span, head * key_width : (head + 1) * key_width] = moved[
                key_width:, value_width:
            ].astype(BF)
    ends_ref[...] = joint_ref[...].astype(BF)


def mixer_forward(pre, keep, taps, valid, rate, bias, heads, key_width, value_width):
    rows = pre.shape[0] - RIM
    wide = heads * (2 * key_width + value_width)
    gate_wide = heads * value_width
    count = rows // GROUP
    packs = rows // PACK
    joint_width = key_width + value_width
    whole = lambda shape: pl.BlockSpec(shape, lambda i: (0,) * len(shape))
    outs = [
        ((rows, wide), BF),
        ((packs * heads, PACK, PACK), BF),
        ((rows, heads * key_width), BF),
        ((rows, heads * value_width), BF),
        ((count * heads, key_width + GROUP, key_width), BF),
        ((count * heads, key_width, joint_width), BF),
        ((rows, heads * value_width), F32),
        ((rows, heads * key_width), BF),
        ((heads, key_width, joint_width), BF),
    ]
    return pl.pallas_call(
        functools.partial(
            forward_kernel, heads=heads, rows=rows, key_width=key_width, value_width=value_width
        ),
        grid=(1,),
        in_specs=[
            pl.BlockSpec(memory_space=pltpu.SMEM),
            pl.BlockSpec((rows + RIM, wide), lambda i: (0, 0)),
            pl.BlockSpec((rows + RIM, LANES), lambda i: (0, (wide + gate_wide) // LANES)),
            whole(taps.shape),
            whole(valid.shape),
            whole(rate.shape),
            whole(bias.shape),
        ],
        out_specs=[whole(shape) for shape, _ in outs],
        out_shape=[jax.ShapeDtypeStruct(shape, kind) for shape, kind in outs],
        scratch_shapes=[
            pltpu.VMEM((count * heads, key_width, value_width), F32),
            pltpu.VMEM((rows, heads * value_width), F32),
            pltpu.VMEM((count * heads, 8, LANES), F32),
            pltpu.VMEM((heads, key_width, joint_width), F32),
        ],
        compiler_params=pltpu.CompilerParams(vmem_limit_bytes=VMEM_LIMIT),
        name="mixer_forward",
    )(keep, pre, pre, taps, valid, rate, bias)


def output_kernel(
    place_ref,
    local_ref,
    carry_ref,
    end1_ref,
    end2_ref,
    end3_ref,
    end4_ref,
    gate_ref,
    gain_ref,
    weight_ref,
    mixed_ref,
    normed_ref,
    partial_ref,
    enter_ref,
    *,
    heads,
    key_width,
    value_width,
):
    @pl.when(pl.program_id(0) == 0)
    def _():
        for head in range(heads):
            state = end4_ref[0, head, :, :value_width].astype(F32)
            for end in (end3_ref, end2_ref, end1_ref):
                state = end[0, head, :, :value_width].astype(F32) + mm(
                    end[0, head, :, value_width:], state
                )
            enter_ref[head] = state.astype(BF)

    for head in range(heads):
        cols = slice(head * value_width, (head + 1) * value_width)
        mixed = local_ref[:, cols] + mm(
            carry_ref[:, head * key_width : (head + 1) * key_width], enter_ref[head]
        )
        mixed_low = mixed.astype(BF)
        mixed_ref[:, cols] = mixed_low
        mixed = mixed_low.astype(F32)
        scale = lax.rsqrt(jnp.mean(mixed * mixed, axis=1, keepdims=True) + EPSILON)
        gate = gate_ref[:, cols]
        normed = mixed * scale * gain_ref[...] * (gate * sigmoid(gate))
        normed_ref[:, cols] = normed.astype(BF)
    partial_ref[...] = mm(normed_ref[...], weight_ref[...]).astype(BF)


def mixer_output(local, carry, ends, place, pre, gain, weight, key_width, value_width):
    rows, cols = local.shape
    heads = cols // value_width
    width = weight.shape[1]
    gate_block = heads * (2 * key_width + value_width) // cols
    end_shape = (1,) + ends.shape[1:]

    def end_spec(step):
        return pl.BlockSpec(end_shape, lambda i, at: (jnp.maximum(at[0] - step, 0), 0, 0, 0))

    return pl.pallas_call(
        functools.partial(
            output_kernel, heads=heads, key_width=key_width, value_width=value_width
        ),
        grid_spec=pltpu.PrefetchScalarGridSpec(
            num_scalar_prefetch=1,
            grid=(rows // PACK,),
            in_specs=[
                pl.BlockSpec((PACK, cols), lambda i, at: (i, 0)),
                pl.BlockSpec((PACK, carry.shape[1]), lambda i, at: (i, 0)),
                end_spec(1),
                end_spec(2),
                end_spec(3),
                end_spec(4),
                pl.BlockSpec((PACK, cols), lambda i, at: (i, gate_block)),
                pl.BlockSpec(gain.shape, lambda i, at: (0, 0)),
                pl.BlockSpec(weight.shape, lambda i, at: (0, 0)),
            ],
            out_specs=[
                pl.BlockSpec((PACK, cols), lambda i, at: (i, 0)),
                pl.BlockSpec((PACK, cols), lambda i, at: (i, 0)),
                pl.BlockSpec((PACK, width), lambda i, at: (i, 0)),
                pl.BlockSpec((heads, key_width, value_width), lambda i, at: (0, 0, 0)),
            ],
        ),
        out_shape=[
            jax.ShapeDtypeStruct((rows, cols), BF),
            jax.ShapeDtypeStruct((rows, cols), BF),
            jax.ShapeDtypeStruct((rows, width), BF),
            jax.ShapeDtypeStruct((heads, key_width, value_width), BF),
        ],
        compiler_params=pltpu.CompilerParams(vmem_limit_bytes=VMEM_LIMIT),
        name="mixer_output",
    )(place, local, carry, ends, ends, ends, ends, pre, gain, weight)


def gate_back_kernel(
    grad_ref,
    weight_ref,
    mixed_ref,
    gate_ref,
    gain_ref,
    fold_ref,
    states_ref,
    mixed_grad_ref,
    gate_grad_ref,
    gain_grad_ref,
    source_ref,
    enter_grad_ref,
    *,
    heads,
    key_width,
    value_width,
):
    inner = PACK // GROUP

    @pl.when(pl.program_id(0) == 0)
    def _():
        gain_grad_ref[...] = jnp.zeros_like(gain_grad_ref)
        enter_grad_ref[...] = jnp.zeros_like(enter_grad_ref)

    normed_grad = mm_nt(grad_ref[...], weight_ref[...])
    gain = gain_ref[...]
    for head in range(heads):
        cols = slice(head * value_width, (head + 1) * value_width)
        grad = normed_grad[:, cols]
        mixed = mixed_ref[:, cols].astype(F32)
        scale = lax.rsqrt(jnp.mean(mixed * mixed, axis=1, keepdims=True) + EPSILON)
        gate = gate_ref[:, cols]
        sig = sigmoid(gate)
        silu = gate * sig
        unit = mixed * scale
        scaled = grad * unit
        gate_grad_ref[:, cols] = (scaled * gain * (sig * (1.0 + gate * (1.0 - sig)))).astype(BF)
        gain_grad_ref[0:1, :] += jnp.sum(scaled * silu, axis=0, keepdims=True)
        unit_grad = grad * gain * silu
        mixed_grad = scale * (unit_grad - unit * jnp.mean(unit_grad * unit, axis=1, keepdims=True))
        mixed_grad = mixed_grad.astype(BF)
        mixed_grad_ref[:, cols] = mixed_grad
        total = enter_grad_ref[head]
        for b in range(inner):
            index = b * heads + head
            source = mm_tn(
                fold_ref[index, key_width:, :], mixed_grad[b * GROUP : (b + 1) * GROUP]
            )
            source_ref[index] = source
            total = total + mm_tn(states_ref[index, :, value_width:], source)
        enter_grad_ref[head] = total


def gate_back(grad, weight, mixed, pre, gain, fold, states, key_width, value_width):
    rows, width = grad.shape
    cols = weight.shape[0]
    heads = cols // value_width
    gate_block = heads * (2 * key_width + value_width) // cols
    step = PACK // GROUP * heads
    return pl.pallas_call(
        functools.partial(
            gate_back_kernel, heads=heads, key_width=key_width, value_width=value_width
        ),
        grid=(rows // PACK,),
        in_specs=[
            pl.BlockSpec((PACK, width), lambda i: (i, 0)),
            pl.BlockSpec(weight.shape, lambda i: (0, 0)),
            pl.BlockSpec((PACK, cols), lambda i: (i, 0)),
            pl.BlockSpec((PACK, cols), lambda i: (i, gate_block)),
            pl.BlockSpec(gain.shape, lambda i: (0, 0)),
            pl.BlockSpec((step,) + fold.shape[1:], lambda i: (i, 0, 0)),
            pl.BlockSpec((step,) + states.shape[1:], lambda i: (i, 0, 0)),
        ],
        out_specs=[
            pl.BlockSpec((PACK, cols), lambda i: (i, 0)),
            pl.BlockSpec((PACK, cols), lambda i: (i, 0)),
            pl.BlockSpec((8, value_width), lambda i: (0, 0)),
            pl.BlockSpec((step, key_width, value_width), lambda i: (i, 0, 0)),
            pl.BlockSpec((heads, key_width, value_width), lambda i: (0, 0, 0)),
        ],
        out_shape=[
            jax.ShapeDtypeStruct((rows, cols), BF),
            jax.ShapeDtypeStruct((rows, cols), BF),
            jax.ShapeDtypeStruct((8, value_width), F32),
            jax.ShapeDtypeStruct((rows // GROUP * heads, key_width, value_width), F32),
            jax.ShapeDtypeStruct((heads, key_width, value_width), F32),
        ],
        compiler_params=pltpu.CompilerParams(vmem_limit_bytes=VMEM_LIMIT),
        name="gate_back",
    )(grad, weight, mixed, pre, gain, fold, states)


def backward_kernel(
    place_ref,
    keep_ref,
    flag_ref,
    pre_ref,
    small_ref,
    taps_ref,
    valid_ref,
    rate_ref,
    bias_ref,
    qkv_ref,
    inverse_ref,
    w_ref,
    u_ref,
    fold_ref,
    states_ref,
    enter_ref,
    mixed_grad_ref,
    source_ref,
    next1_ref,
    next2_ref,
    next3_ref,
    next4_ref,
    end1_ref,
    end2_ref,
    end3_ref,
    pre_grad_ref,
    small_grad_ref,
    taps_grad_ref,
    rate_grad_ref,
    later_ref,
    whole_ref,
    conv_grad_ref,
    flow_ref,
    *,
    heads,
    rows,
    key_width,
    value_width,
):
    groups = rows // PACK
    inner = PACK // GROUP
    key_cols = heads * key_width
    wide = heads * (2 * key_width + value_width)
    taps_grad_ref[...] = jnp.zeros_like(taps_grad_ref)
    rate_grad_ref[...] = jnp.zeros_like(rate_grad_ref)
    conv_grad_ref[0:RIM, :] = jnp.zeros((RIM, wide), F32)
    conv_grad_ref[RIM + rows :, :] = jnp.zeros((RIM, wide), F32)
    small_grad_ref[rows:, :] = jnp.zeros((RIM, LANES), BF)

    def lasts(group, _):
        masks = pack_masks()
        span = pl.ds(pl.multiple_of(group * PACK, PACK), PACK)
        decay_tile, _ = rates_of(small_ref[span, :], rate_ref[...], bias_ref[...])
        for head in range(heads):
            decay = decay_tile[:, head : head + 1].astype(BF).astype(F32)
            for b in range(inner):
                total = jnp.sum(decay[b * GROUP : (b + 1) * GROUP], axis=0, keepdims=True)
                whole_ref[(group * inner + b) * heads + head] = jnp.broadcast_to(
                    jnp.exp(total), (8, LANES)
                )
        return 0

    lax.fori_loop(0, groups, lasts, 0)

    for head in range(heads):
        flow = flag_ref[3] * next4_ref[0, head].astype(F32)
        flow = flag_ref[2] * (
            next3_ref[0, head].astype(F32) + mm_tn(end3_ref[0, head, :, value_width:], flow)
        )
        flow = flag_ref[1] * (
            next2_ref[0, head].astype(F32) + mm_tn(end2_ref[0, head, :, value_width:], flow)
        )
        flow = flag_ref[0] * (
            next1_ref[0, head].astype(F32) + mm_tn(end1_ref[0, head, :, value_width:], flow)
        )
        flow_ref[head] = flow
    for block in reversed(range(rows // GROUP)):
        for head in range(heads):
            index = block * heads + head
            flow = flow_ref[head]
            flow_low = flow.astype(BF)
            later_ref[index] = flow_low
            moved = mm_tn(fold_ref[index, :key_width, :], flow_low)
            flow_ref[head] = keep_ref[block] * (
                whole_ref[index, 0:1, 0:1] * flow - moved + source_ref[index]
            )

    def back(group, _):
        masks = pack_masks()
        row, col, apart, same, lower, strict = masks
        span = pl.ds(pl.multiple_of(group * PACK, PACK), PACK)
        small = small_ref[span, :]
        valid = valid_ref[pl.ds(pl.multiple_of(group * PACK + RIM, RIM), PACK), :]
        decay_tile, beta_tile = rates_of(small, rate_ref[...], bias_ref[...])
        lane = lax.broadcasted_iota(jnp.int32, (PACK, LANES), 1)
        small_rows = jnp.zeros((PACK, LANES), F32)
        for head in range(heads):
            decay = decay_tile[:, head : head + 1].astype(BF).astype(F32)
            beta = beta_tile[:, heads + head : heads + head + 1].astype(BF).astype(F32)
            query_at = head * key_width
            key_at = key_cols + head * key_width
            value_at = 2 * key_cols + head * value_width
            query = qkv_ref[span, query_at : query_at + key_width]
            key = qkv_ref[span, key_at : key_at + key_width]
            value = qkv_ref[span, value_at : value_at + value_width]
            key_f = key.astype(F32)
            gam, last, fading = packed_decay(decay, masks)
            growth = jnp.exp(gam)
            rest = jnp.exp(last - gam)
            gram = mm_nt(key, key)
            scores = mm_nt(query, key) * fading
            system = jnp.where(strict, fading * beta * gram, 0.0)
            tail = (rest * key_f).astype(BF)
            w = w_ref[span, query_at : query_at + key_width]
            u = u_ref[span, head * value_width : (head + 1) * value_width]
            out_grad = mixed_grad_ref[span, head * value_width : (head + 1) * value_width]
            renewed, renewed_grad, state_lows, flows, drops = [], [], [], [], []
            for b in range(inner):
                index = (group * inner + b) * heads + head
                part = slice(b * GROUP, (b + 1) * GROUP)
                state = states_ref[index, :, :value_width].astype(F32) + mm(
                    states_ref[index, :, value_width:], enter_ref[head]
                )
                state_low = state.astype(BF)
                flow = later_ref[index]
                state_lows.append(state_low)
                flows.append(flow)
                renewed.append(u[part].astype(F32) - mm(w[part], state_low))
                renewed_grad.append(mm(tail[part], flow))
                shared = jnp.sum(
                    jnp.sum(state * flow.astype(F32), axis=1, keepdims=True), axis=0, keepdims=True
                )
                drops.append(
                    jnp.broadcast_to(shared * whole_ref[index, 0:1, 0:1], (GROUP, 1))
                )
            renewed = jnp.concatenate(renewed, axis=0).astype(BF)
            renewed_grad = mm_tn(scores, out_grad) + jnp.concatenate(renewed_grad, axis=0)
            renewed_low = renewed_grad.astype(BF)
            scores_grad = jnp.where(lower, mm_nt(out_grad, renewed), 0.0)
            grown_grad, tail_grad, w_grad = [], [], []
            for b in range(inner):
                part = slice(b * GROUP, (b + 1) * GROUP)
                grown_grad.append(mm_nt(out_grad[part], state_lows[b]))
                tail_grad.append(mm_nt(renewed[part], flows[b]))
                w_grad.append(mm_nt(renewed_low[part], state_lows[b]))
            grown_grad = jnp.concatenate(grown_grad, axis=0)
            tail_grad = jnp.concatenate(tail_grad, axis=0)
            w_grad = -jnp.concatenate(w_grad, axis=0)
            inverse = inverse_ref[group * heads + head]
            keys_grad = mm_tn(inverse, w_grad)
            values_grad = mm_tn(inverse, renewed_low)
            system_grad = jnp.where(strict, -(mm_nt(keys_grad, w) + mm_nt(values_grad, u)), 0.0)
            gram_beta = system_grad * fading
            gram_grad = (gram_beta * beta).astype(BF)
            pair_grad = (scores_grad * fading).astype(BF)
            changes = system_grad * system + scores_grad * scores
            query_f = query.astype(F32)
            query_grad = mm(pair_grad, key) + growth * grown_grad
            key_grad = (
                mm(gram_grad, key)
                + mm_tn(gram_grad, key)
                + mm_tn(pair_grad, query)
                + beta * growth * keys_grad
                + rest * tail_grad
            )
            value_grad = beta * values_grad
            keys_dot = growth * jnp.sum(keys_grad * key_f, axis=1, keepdims=True)
            beta_grad = (
                keys_dot
                + jnp.sum(values_grad * value.astype(F32), axis=1, keepdims=True)
                + jnp.sum(gram_beta * gram, axis=1, keepdims=True)
            )
            tail_dot = rest * jnp.sum(tail_grad * key_f, axis=1, keepdims=True)
            column = jnp.sum(changes, axis=0, keepdims=True)
            column = jnp.sum(
                jnp.where(apart == 0, jnp.broadcast_to(column, (PACK, PACK)), 0.0),
                axis=1,
                keepdims=True,
            )
            gam_grad = (
                beta * keys_dot
                + jnp.sum(changes, axis=1, keepdims=True)
                - column
                + growth * jnp.sum(grown_grad * query_f, axis=1, keepdims=True)
                - tail_dot
            )
            gam_grad_row = jnp.sum(
                jnp.where(apart == 0, jnp.broadcast_to(gam_grad, (PACK, PACK)), 0.0),
                axis=0,
                keepdims=True,
            )
            tail_row = jnp.sum(
                jnp.where(apart == 0, jnp.broadcast_to(tail_dot, (PACK, PACK)), 0.0),
                axis=0,
                keepdims=True,
            )
            decay_grad = (
                jnp.sum(
                    jnp.where(same & (col >= row), gam_grad_row, 0.0)
                    + jnp.where(same, tail_row, 0.0),
                    axis=1,
                    keepdims=True,
                )
                + jnp.concatenate(drops, axis=0)
            )
            small_rows = jnp.where(lane == head, decay_grad, small_rows)
            small_rows = jnp.where(lane == heads + head, beta_grad, small_rows)

            for first, width, unit_grad, factor in (
                (query_at, key_width, query_grad, key_width ** (-0.5)),
                (key_at, key_width, key_grad, 1.0),
                (value_at, value_width, value_grad, None),
            ):
                window = load_window(pre_ref, group, first, width, rows)
                conv, pieces = active_of(window, taps_ref, valid, first, width)
                sig = sigmoid(conv)
                act_grad = unit_grad
                if factor is not None:
                    act = conv * sig
                    scale = lax.rsqrt(jnp.sum(act * act, axis=1, keepdims=True) + EPSILON)
                    along = jnp.sum(unit_grad * act, axis=1, keepdims=True)
                    act_grad = factor * scale * (unit_grad - act * (scale * scale * along))
                conv_grad = act_grad * (sig * (1.0 + conv * (1.0 - sig)))
                conv_grad_ref[
                    pl.ds(pl.multiple_of(group * PACK + RIM, RIM), PACK), first : first + width
                ] = conv_grad
                for j in range(CONV):
                    taps_grad_ref[j : j + 1, first : first + width] += jnp.sum(
                        conv_grad * valid[:, j : j + 1] * pieces[j], axis=0, keepdims=True
                    )

        raw = small + bias_ref[...]
        slope = -jnp.exp(rate_ref[...]) * sigmoid(raw)
        small_grad = jnp.where(
            lane < heads, small_rows * slope, small_rows * beta_tile * (1.0 - beta_tile)
        )
        small_grad = jnp.where(lane < 2 * heads, small_grad, 0.0)
        small_grad_ref[span, :] = small_grad.astype(BF)
        rate_grad_ref[0:1, :] += jnp.sum(small_rows * decay_tile, axis=0, keepdims=True)
        rate_grad_ref[1:2, :] += jnp.sum(small_grad, axis=0, keepdims=True)
        return 0

    lax.fori_loop(0, groups, back, 0)

    def convolve_back(start, target, count, first):
        cols = slice(first, first + LANES)
        window = conv_grad_ref[pl.ds(start, count + RIM), cols]
        flags = valid_ref[pl.ds(start, count + RIM), :]
        total = None
        for j in range(CONV):
            term = window * (flags[:, j : j + 1] * taps_ref[j : j + 1, cols])
            shift = CONV - 1 - j
            if shift:
                term = pltpu.roll(term, count + RIM - shift, 0)
            total = term if total is None else total + term
        pre_grad_ref[pl.ds(target, count), cols] = total[:count].astype(BF)

    def spread(group, _):
        base = pl.multiple_of(group * PACK, PACK)
        for first in range(0, wide, LANES):
            convolve_back(pl.multiple_of(base + RIM, RIM), base, PACK, first)
        return 0

    lax.fori_loop(0, groups, spread, 0)
    for first in range(0, wide, LANES):
        convolve_back(0, rows, RIM, first)


def mixer_backward(
    place,
    keep,
    flags,
    pre,
    taps,
    valid,
    rate,
    bias,
    qkv,
    inverse,
    w,
    u,
    fold,
    states,
    enter,
    mixed_grad,
    source,
    enter_grads,
    ends,
    heads,
    key_width,
    value_width,
):
    rows = pre.shape[0] - RIM
    wide = heads * (2 * key_width + value_width)
    gate_wide = heads * value_width
    count = rows // GROUP
    devices = ends.shape[0]

    def whole(shape):
        return pl.BlockSpec(shape, lambda i, at: (0,) * len(shape))

    def next_spec(shape, step):
        return pl.BlockSpec(
            (1,) + shape[1:], lambda i, at: (jnp.minimum(at[0] + step, devices - 1), 0, 0, 0)
        )

    smem = pl.BlockSpec(memory_space=pltpu.SMEM)
    return pl.pallas_call(
        functools.partial(
            backward_kernel, heads=heads, rows=rows, key_width=key_width, value_width=value_width
        ),
        grid_spec=pltpu.PrefetchScalarGridSpec(
            num_scalar_prefetch=1,
            grid=(1,),
            in_specs=[
                smem,
                smem,
                pl.BlockSpec((rows + RIM, wide), lambda i, at: (0, 0)),
                pl.BlockSpec((rows + RIM, LANES), lambda i, at: (0, (wide + gate_wide) // LANES)),
                whole(taps.shape),
                whole(valid.shape),
                whole(rate.shape),
                whole(bias.shape),
                whole(qkv.shape),
                whole(inverse.shape),
                whole(w.shape),
                whole(u.shape),
                whole(fold.shape),
                whole(states.shape),
                whole(enter.shape),
                whole(mixed_grad.shape),
                whole(source.shape),
                next_spec(enter_grads.shape, 1),
                next_spec(enter_grads.shape, 2),
                next_spec(enter_grads.shape, 3),
                next_spec(enter_grads.shape, 4),
                next_spec(ends.shape, 1),
                next_spec(ends.shape, 2),
                next_spec(ends.shape, 3),
            ],
            out_specs=[
                whole((rows + RIM, wide)),
                whole((rows + RIM, LANES)),
                whole((8, wide)),
                whole((8, LANES)),
            ],
            scratch_shapes=[
                pltpu.VMEM((count * heads, key_width, value_width), BF),
                pltpu.VMEM((count * heads, 8, LANES), F32),
                pltpu.VMEM((rows + 2 * RIM, wide), F32),
                pltpu.VMEM((heads, key_width, value_width), F32),
            ],
        ),
        out_shape=[
            jax.ShapeDtypeStruct((rows + RIM, wide), BF),
            jax.ShapeDtypeStruct((rows + RIM, LANES), BF),
            jax.ShapeDtypeStruct((8, wide), F32),
            jax.ShapeDtypeStruct((8, LANES), F32),
        ],
        compiler_params=pltpu.CompilerParams(vmem_limit_bytes=VMEM_LIMIT),
        name="mixer_backward",
    )(
        place,
        keep,
        flags,
        pre,
        pre,
        taps,
        valid,
        rate,
        bias,
        qkv,
        inverse,
        w,
        u,
        fold,
        states,
        enter,
        mixed_grad,
        source,
        enter_grads,
        enter_grads,
        enter_grads,
        enter_grads,
        ends,
        ends,
        ends,
    )


def product(left, right):
    return jnp.dot(left, right, preferred_element_type=F32)


def transposed_left(left, right):
    return lax.dot_general(left, right, (((0,), (0,)), ((), ())), preferred_element_type=F32)


def transposed_right(left, right):
    return lax.dot_general(left, right, (((1,), (1,)), ((), ())), preferred_element_type=F32)


def full_rows(row_block):
    return lax.all_gather(row_block, "tensor", axis=1, tiled=True)


def tensor_total(terms):
    return lax.psum_scatter(terms.astype(BF), "tensor", scatter_dimension=1, tiled=True)


def owners(grad):
    return lax.psum_scatter(grad.astype(BF), FH, scatter_dimension=0, tiled=True).astype(F32)


def spread_into(piece, whole_shape, start, axis_number):
    return lax.dynamic_update_slice_in_dim(jnp.zeros(whole_shape, F32), piece, start, axis_number)


def lane_row(values):
    return jnp.pad(values, (0, LANES - values.shape[0]))[None, :]


def per_device(
    tokens,
    cotangent,
    lengths,
    norm_gain,
    query_weight,
    key_weight,
    value_weight,
    outgate_weight,
    alpha_weight,
    beta_weight,
    output_weight,
    conv_query,
    conv_key,
    conv_value,
    log_rate,
    step_bias,
    out_gain,
    ffn_gain,
    gate_weight,
    up_weight,
    down_weight,
):
    rows, slice_width = tokens.shape
    full_width = slice_width * lax.axis_size("tensor")
    tensor_place = lax.axis_index("tensor")
    place = lax.axis_index(FH)
    devices = lax.axis_size(FH)
    key_cols = query_weight.shape[1]
    value_cols = value_weight.shape[1]
    heads = alpha_weight.shape[1]
    key_width = key_cols // heads
    value_width = value_cols // heads
    wide = 2 * key_cols + value_cols
    hidden = gate_weight.shape[1]

    rim_slice = shifted(tokens[rows - RIM :], FH, 1)
    token_rows = full_rows(tokens)
    rim_rows = full_rows(rim_slice)
    small_shard = jnp.pad(
        jnp.concatenate([alpha_weight, beta_weight], axis=1), ((0, 0), (0, LANES - 2 * heads))
    )
    in_shard = jnp.concatenate(
        [query_weight, key_weight, value_weight, outgate_weight, small_shard], axis=1
    )
    in_full = lax.all_gather(in_shard, "fsdp", axis=0, tiled=True)
    output_full = lax.all_gather(output_weight, "fsdp", axis=1, tiled=True)
    ffn_full = lax.all_gather(jnp.stack([gate_weight, up_weight]), "fsdp", axis=1, tiled=True)
    down_full = lax.all_gather(down_weight, "fsdp", axis=1, tiled=True)
    cot_rows = full_rows(cotangent)

    starts = jnp.cumsum(lengths) - lengths
    places = place * rows + jnp.arange(rows, dtype=jnp.int32)
    latest = jnp.max(jnp.where(starts[None, :] <= places[:, None], starts[None, :], 0), axis=1)
    tap_index = jnp.arange(8, dtype=jnp.int32)
    valid = ((places - latest)[:, None] >= CONV - 1 - tap_index[None, :]).astype(F32)
    valid_padded = jnp.pad(valid, ((RIM, RIM), (0, 0)))
    block_first = place * rows + jnp.arange(rows // GROUP, dtype=jnp.int32) * GROUP
    keep = 1.0 - jnp.any(block_first[:, None] == starts[None, :], axis=1).astype(F32)
    following = place + 1 + jnp.arange(4, dtype=jnp.int32)
    flags = (following < devices).astype(F32)
    place_array = place.astype(jnp.int32)[None]
    taps = jnp.concatenate(
        [
            lax.dynamic_slice_in_dim(conv_query, tensor_place * key_cols, key_cols, 1),
            lax.dynamic_slice_in_dim(conv_key, tensor_place * key_cols, key_cols, 1),
            lax.dynamic_slice_in_dim(conv_value, tensor_place * value_cols, value_cols, 1),
        ],
        axis=1,
    )
    rate = lane_row(lax.dynamic_slice_in_dim(log_rate, tensor_place * heads, heads))
    bias = lane_row(lax.dynamic_slice_in_dim(step_bias, tensor_place * heads, heads))
    gain_row = out_gain[None, :]

    token_all = jnp.concatenate([token_rows, rim_rows], axis=0).astype(F32)
    scale_all = lax.rsqrt(jnp.mean(token_all * token_all, axis=1, keepdims=True) + EPSILON)
    hidden_in = (token_all * scale_all * norm_gain).astype(BF)
    pre = product(hidden_in, in_full)

    qkv, inverse, w, u, fold, states, local, carry, end = mixer_forward(
        pre, keep, taps, valid, rate, bias, heads, key_width, value_width
    )
    ends = lax.all_gather(end, FH, axis=0, tiled=False)
    mixed, normed, attn_terms, enter = mixer_output(
        local, carry, ends, place_array, pre, gain_row, output_full, key_width, value_width
    )
    attn = full_rows(tensor_total(attn_terms))

    middle = token_rows.astype(F32) + attn.astype(F32)
    scale_mid = lax.rsqrt(jnp.mean(middle * middle, axis=1, keepdims=True) + EPSILON)
    hidden_mid = (middle * scale_mid * ffn_gain).astype(BF)
    gate_act = product(hidden_mid, ffn_full[0])
    up_act = product(hidden_mid, ffn_full[1])
    gate_sig = jax.nn.sigmoid(gate_act)
    inner_act = (gate_act * gate_sig * up_act).astype(BF)
    inner_grad = transposed_right(cot_rows, down_full)
    gate_grad = (inner_grad * up_act * gate_sig * (1.0 + gate_act * (1.0 - gate_sig))).astype(BF)
    up_grad = (inner_grad * gate_act * gate_sig).astype(BF)
    mid_terms = transposed_right(gate_grad, ffn_full[0]) + transposed_right(up_grad, ffn_full[1])
    ffn_gain_grad = jnp.sum(mid_terms * (middle * scale_mid), axis=0)
    mid_grad = full_rows(tensor_total(mid_terms))
    output_terms = tensor_total(product(inner_act, down_full))
    middle_own = lax.dynamic_slice_in_dim(middle, tensor_place * slice_width, slice_width, 1)
    output_rows = (middle_own + output_terms.astype(F32)).astype(BF)

    scaled_mid = mid_grad.astype(F32) * ffn_gain
    mid_dot = jnp.sum(scaled_mid * middle, axis=1, keepdims=True)
    middle_grad = (
        cot_rows.astype(F32)
        + scale_mid * scaled_mid
        - middle * (scale_mid * scale_mid * scale_mid * mid_dot / full_width)
    )
    attn_grad = middle_grad.astype(BF)

    mixed_grad, outgate_grad, out_gain_grad, source, enter_grad = gate_back(
        attn_grad, output_full, mixed, pre, gain_row, fold, states, key_width, value_width
    )
    enter_grads = lax.all_gather(enter_grad.astype(BF), FH, axis=0, tiled=False)
    ffn_grads = owners(
        jnp.concatenate(
            [
                transposed_left(hidden_mid, gate_grad).astype(BF),
                transposed_left(hidden_mid, up_grad).astype(BF),
                transposed_left(cot_rows, inner_act).astype(BF),
            ],
            axis=1,
        )
    )
    out_grads = owners(
        jnp.concatenate(
            [
                transposed_left(attn_grad, normed).astype(BF),
                transposed_left(hidden_in[:rows], outgate_grad).astype(BF),
            ],
            axis=1,
        )
    )
    pre_grad, small_grad, taps_grad, rate_grad = mixer_backward(
        place_array,
        keep,
        flags,
        pre,
        taps,
        valid_padded,
        rate,
        bias,
        qkv,
        inverse,
        w,
        u,
        fold,
        states,
        enter,
        mixed_grad,
        source,
        enter_grads,
        ends,
        heads,
        key_width,
        value_width,
    )

    gate_terms = transposed_right(outgate_grad, in_full[:, wide : wide + value_cols])
    main_terms = transposed_right(pre_grad, in_full[:, :wide]) + transposed_right(
        small_grad, in_full[:, wide + value_cols :]
    )
    rim_terms = shifted(main_terms[rows:], FH, -1)
    in_terms = main_terms[:rows] + gate_terms
    norm_gain_grad = jnp.sum(in_terms * (token_all * scale_all)[:rows], axis=0) + jnp.sum(
        main_terms[rows:] * (token_all * scale_all)[rows:], axis=0
    )
    in_terms = in_terms + jnp.pad(rim_terms, ((rows - RIM, 0), (0, 0)))
    in_dot = lax.psum(jnp.sum(in_terms * (token_all[:rows] * norm_gain), axis=1), "tensor")
    in_grad = tensor_total(in_terms).astype(F32)
    late_grads = owners(
        jnp.concatenate(
            [
                transposed_left(hidden_in, pre_grad).astype(BF),
                transposed_left(hidden_in, small_grad).astype(BF),
            ],
            axis=1,
        )
    )
    norm_slice = lax.dynamic_slice_in_dim(norm_gain, tensor_place * slice_width, slice_width)
    middle_grad_own = lax.dynamic_slice_in_dim(
        middle_grad, tensor_place * slice_width, slice_width, 1
    )
    scale_in = scale_all[:rows]
    tokens_grad = (
        middle_grad_own
        + scale_in * (in_grad * norm_slice)
        - tokens.astype(F32) * (scale_in * scale_in * scale_in * in_dot[:, None] / full_width)
    )

    pieces = (
        spread_into(taps_grad[:CONV, :key_cols], conv_query.shape, tensor_place * key_cols, 1),
        spread_into(
            taps_grad[:CONV, key_cols : 2 * key_cols], conv_key.shape, tensor_place * key_cols, 1
        ),
        spread_into(
            taps_grad[:CONV, 2 * key_cols :], conv_value.shape, tensor_place * value_cols, 1
        ),
        spread_into(rate_grad[0, :heads], log_rate.shape, tensor_place * heads, 0),
        spread_into(rate_grad[1, :heads], step_bias.shape, tensor_place * heads, 0),
        out_gain_grad[0],
        norm_gain_grad,
        ffn_gain_grad,
    )
    joined = lax.psum(jnp.concatenate([piece.reshape(-1) for piece in pieces]), ALL)
    small, at = [], 0
    for piece in pieces:
        small.append(joined[at : at + piece.size].reshape(piece.shape))
        at += piece.size

    return (
        output_rows,
        tokens_grad,
        late_grads[:, :key_cols],
        late_grads[:, key_cols : 2 * key_cols],
        late_grads[:, 2 * key_cols : wide],
        out_grads[:, value_cols:],
        late_grads[:, wide : wide + heads],
        late_grads[:, wide + heads : wide + 2 * heads],
        out_grads[:, :value_cols].T,
        ffn_grads[:, :hidden],
        ffn_grads[:, hidden : 2 * hidden],
        ffn_grads[:, 2 * hidden :].T,
        *small,
    )


def solution(mesh):
    in_specs = (
        P(FH, "tensor"),
        P(FH, "tensor"),
        P(),
        P(),
        P("fsdp", "tensor"),
        P("fsdp", "tensor"),
        P("fsdp", "tensor"),
        P("fsdp", "tensor"),
        P("fsdp", "tensor"),
        P("fsdp", "tensor"),
        P("tensor", "fsdp"),
        P(),
        P(),
        P(),
        P(),
        P(),
        P(),
        P(),
        P("fsdp", "tensor"),
        P("fsdp", "tensor"),
        P("tensor", "fsdp"),
    )
    out_specs = (
        P(FH, "tensor"),
        P(FH, "tensor"),
        P(FH, "tensor"),
        P(FH, "tensor"),
        P(FH, "tensor"),
        P(FH, "tensor"),
        P(FH, "tensor"),
        P(FH, "tensor"),
        P("tensor", FH),
        P(FH, "tensor"),
        P(FH, "tensor"),
        P("tensor", FH),
        P(),
        P(),
        P(),
        P(),
        P(),
        P(),
        P(),
        P(),
    )
    return jax.shard_map(
        per_device, mesh=mesh, in_specs=in_specs, out_specs=out_specs, check_vma=False
    )
```

time: 3710 us -> 836 us (0.23); the launches traced: 3650 us -> 823 us
  matrix products: 1430 us -> 66.1 us
  local copies, waits for them, and re-layouts: 763 us -> 40.8 us
  waiting for transfers between devices: 1010 us -> 547 us
  other arithmetic: 345 us -> 39.8 us
  Pallas kernels: 0 us -> 81.8 us
    dot_general x980 -> x4, matrix products: 1330 us -> 23 us  [product(): return jnp.dot(left, right, preferred_element_type=F32)]
    reduce_scatter x12 -> x4, waiting for transfers between devices: 613 us -> 139 us  [tensor_total(): lax.psum_scatter(terms.astype(BF), 'tensor', scatter_dimension=1, tiled=T...]
    squeeze x320 -> x0, local copies, waits for them, and re-layouts: 251 us -> none  [delta_rule(): lax.scan(jax.checkpoint(advance), state_in, (keys_wy, values_wy, scores,...]
    dynamic_slice x386 -> x2, local copies, waits for them, and re-layouts: 225 us -> 0.15 us  [the longest x1 0.08 us: per_device(): lax.dynamic_slice_in_dim(log_rate, tensor_place * heads, heads)]
    reduce_sum x83 -> x4, other arithmetic: 113 us -> 9.87 us  [the longest x1 5.13 us: per_device(): ffn_gain_grad = jnp.sum(mid_terms * (middle * scale_mid), axis=0)]
    dynamic_update_slice x131 -> x5, local copies, waits for them, and re-layouts: 89.8 us -> 1.61 us  [spread_into(): lax.dynamic_update_slice_in_dim(jnp.zeros(whole_shape, F32), piece, start...]
    concatenate x6 -> x4, other arithmetic: 86.8 us -> 4.98 us  [the longest x1 2.35 us: per_device(): jnp.concatenate([transposed_left(hidden_mid, gate_grad).astype(BF), trans...]
    pallas_call x0 -> x4, Pallas kernels: none -> 81.8 us  [the longest x1 39.1 us: mixer_backward(): pl.pallas_call(functools.partial(backward_kernel, heads=heads, rows=rows,...]
  transfers between devices with their start and end apart: 35 -> 20, of which waited for: 26 -> 16; matrix products, arithmetic and copies ran while one was open for 36% -> 14% of each run, Pallas kernels for 0% -> 8%
where the time goes in v1:
time: 836 us; the launch traced here: 823 us
  waiting for transfers between devices  547 us (65%)
  Pallas kernels  81.8 us (10%)
  matrix products  66.1 us (8%)
  local copies, waits for them, and re-layouts  40.8 us (5%)
  other arithmetic  39.8 us (5%)
  blocking collectives  26.7 us (3%)
  between operations  15.3 us (2%)
    all_gather x4, waiting for transfers between devices, full_rows(): return lax.all_gather(row_block, 'tensor', axis=1, tiled=True)  158 us
    reduce_scatter x4, waiting for transfers between devices, tensor_total(): lax.psum_scatter(terms.astype(BF), 'tensor', scatter_dimension=1, tiled=T...  139 us
    psum x1, waiting for transfers between devices, per_device(): lax.psum(jnp.concatenate([piece.reshape(-1) for piece in pieces]), ALL)  116 us
    unnamed x21, waiting for transfers between devices  82.1 us
    pallas_call x1, Pallas kernels, mixer_backward(): pl.pallas_call(functools.partial(backward_kernel, heads=heads, rows=rows,...  39.1 us
    all_gather x1, waiting for transfers between devices, per_device(): ends = lax.all_gather(end, FH, axis=0, tiled=False)  26.5 us
    pallas_call x1, Pallas kernels, mixer_forward(): pl.pallas_call(functools.partial(forward_kernel, heads=heads, rows=rows,...  26.2 us
    dot_general x6, matrix products, transposed_right(): lax.dot_general(left, right, (((1,), (1,)), ((), ())), preferred_element_...  25.8 us
  transfers between devices with their start and end apart: 20, of which 16 were waited for; matrix products, arithmetic and copies ran while one was open for 14% of the time, Pallas kernels for 8%

profile of v1, /device:TPU:8, one launch (start us, length us, event | category | flops | bytes accessed | tf_op | source)
XLA Modules:
  0.0 823.3 jit_solution(14067582114583494431)
XLA Ops:
  13.4 3.4 collective-permute-start
  20.9 15.5 %all_gather.40 = bf16[16,1024]{1,0:T(8,128)(2,1)S(1)} all-gather(bf16[16,256]{1,0:T(8,128)(2,1)S(1)} %collective-permute-done), channel_id=1, replica_groups=mesh['fsdp'=2,'heads'=4,'tensor'=4] {'tensor'}, dimensions={1}, use_global_device_ids=true | all-gather | bytes 40960 | tf_op jit(solution)/shard_map/all_gather | solution.py:890
  36.3 18.8 %all-gather.13.cloned.1.call-done = bf16[1024,1024]{1,0:T(8,128)(2,1)} async-done(((bf16[1024,256]{1,0:T(8,128)(2,1)}), bf16[1024,1024]{1,0:T(8,128)(2,1)}) %all-gather.13.cloned.1.call-update) | async-done | bytes 2097168 | tf_op jit(solution)/shard_map/all_gather | solution.py:890
  57.4 3.2 broadcast_multiply_fusion
  60.6 9.8 %all-gather.15.cloned.1.call-done = bf16[1024,1664]{1,0:T(8,128)(2,1)} async-done(((bf16[512,1664]{1,0:T(8,128)(2,1)}), bf16[1024,1664]{1,0:T(8,128)(2,1)}) %all-gather.15.cloned.1.call-update) | async-done | bytes 3407888 | tf_op jit(solution)/shard_map/all_gather | solution.py:954
  70.4 9.5 %fusion.31.pre_ref.small_ref.gate_ref = f32[1040,1664]{1,0:T(8,128)} fusion(bf16[1040,1024]{1,0:T(8,128)(2,1)} %get-tuple-element.158, bf16[1024,1664]{1,0:T(8,128)(2,1)} %all-gather.15.cloned.1.call-done), kind=kOutput, calls=%fused_computation.100 | convolution fusion | flops 3544186880 | bytes 12460032 | tf_op jit(solution)/shard_map/dot_general | solution.py:878
  79.8 26.2 %mixer_forward.1 = (bf16[1024,1024]{1,0:T(8,128)(2,1)}, bf16[8,256,256]{2,1,0:T(8,128)(2,1)}, bf16[1024,256]{1,0:T(8,128)(2,1)}, bf16[1024,512]{1,0:T(8,128)(2,1...) custom-call(f32[16]{0:T(128)} %convert_subtract_fusion.keep_ref, ...), custom_call_target="tpu_custom_call" | custom-call | tf_op jit(solution)/shard_map/mixer_forward/pallas_call | solution.py:275
  106.3 26.5 %all-gather.29.cloned.1.call-done = bf16[16,128,384]{2,1,0:T(8,128)(2,1)} async-done(((bf16[2,128,384]{2,1,0:T(8,128)(2,1)}), bf16[16,128,384]{2,1,0:T(8,128)(2,1)}) %all-gather.29.cloned.1.call-update) | async-done | bytes 1572880 | tf_op jit(solution)/shard_map/all_gather | solution.py:991
  132.8 7.6 mixer_output.1
  140.5 41.7 %reduce-scatter.14.cloned.1.call-done = bf16[1024,256]{1,0:T(8,128)(2,1)} async-done(((bf16[1024,1024]{1,0:T(8,128)(2,1)}), bf16[1024,256]{1,0:T(8,128)(2,1)}) %reduce-scatter.14.cloned.1.call-update) | async-done | bytes 524304 | tf_op jit(solution)/shard_map/reduce_scatter | solution.py:894
  182.3 2.6 pad_maximum_fusion.3
  186.4 43.8 %all-gather.19.cloned.1.call-done = bf16[1024,1024]{1,0:T(8,128)(2,1)} async-done(((bf16[1024,256]{1,0:T(8,128)(2,1)}), bf16[1024,1024]{1,0:T(8,128)(2,1)}) %all-gather.19.cloned.1.call-update) | async-done | bytes 2097168 | tf_op jit(solution)/shard_map/all_gather | solution.py:890
  230.3 2.5 multiply_reduce_fusion.3
  234.9 8.5 %all-gather.21.cloned.1.call-done = bf16[2,1024,704]{1,2,0:T(8,128)(2,1)} async-done(((bf16[2,512,704]{1,2,0:T(8,128)(2,1)}), bf16[2,1024,704]{1,2,0:T(8,128)(2,1)}) %all-gather.21.cloned.1.call-update) | async-done | bytes 2883600 | tf_op jit(solution)/shard_map/all_gather | solution.py:956
  243.4 5.4 fusion.14
  248.8 3.2 fusion.13
  252.0 3.8 all-gather.23.cloned.1.call-done
  255.9 47.5 %all-gather.25.cloned.1.call-done = bf16[1024,1024]{1,0:T(8,128)(2,1)} async-done(((bf16[1024,256]{1,0:T(8,128)(2,1)}), bf16[1024,1024]{1,0:T(8,128)(2,1)}) %all-gather.25.cloned.1.call-update) | async-done | bytes 2097168 | tf_op jit(solution)/shard_map/all_gather | solution.py:890
  303.4 7.7 multiply_convert_fusion.2
  313.0 4.6 fusion.30
  317.6 41.2 %reduce-scatter.18.cloned.1.call-done = bf16[1024,256]{1,0:T(8,128)(2,1)} async-done(((bf16[1024,1024]{1,0:T(8,128)(2,1)}), bf16[1024,256]{1,0:T(8,128)(2,1)}) %reduce-scatter.18.cloned.1.call-update) | async-done | bytes 524304 | tf_op jit(solution)/shard_map/reduce_scatter | solution.py:894
  359.4 47.7 %all-gather.27.cloned.1.call-done = bf16[1024,1024]{1,0:T(8,128)(2,1)} async-done(((bf16[1024,256]{1,0:T(8,128)(2,1)}), bf16[1024,1024]{1,0:T(8,128)(2,1)}) %all-gather.27.cloned.1.call-update) | async-done | bytes 2097168 | tf_op jit(solution)/shard_map/all_gather | solution.py:890
  407.0 5.1 multiply_reduce_fusion.1
  412.3 4.7 fusion.23
  417.1 8.9 %gate_back.1 = (bf16[1024,512]{1,0:T(8,128)(2,1)}, bf16[1024,512]{1,0:T(8,128)(2,1)}, f32[8,256]{1,0:T(8,128)}, f32[32,128,256]{2,1,0:T(8,128)}, f32[2,128,256]{2,1,0:T(8,128)}) custom-call(bf16[1024,1024]{1,0:T(8,128)(2,1)} %get-tuple-element.148.grad_ref, bf16[512,1024]{1,0:T(8,128)(2,1)} %all-gather.17.cloned.1.call-done.weight_ref, ...), custom_call_target="tpu_custom_call" | custom-call | tf_op jit(solution)/shard_map/gate_back/pallas_call | solution.py:453
  427.7 3.8 convolution_convert_fusion.2
  435.2 2.4 pad_maximum_fusion
  437.6 6.4 copy.65
  446.5 4.9 convolution_convert_fusion.1
  451.5 2.5 maximum_convert_fusion
  454.7 2.3 convolution_convert_fusion.5
  457.1 2.3 fusion.8
  459.3 39.1 %mixer_backward.1 = (bf16[1040,1024]{1,0:T(8,128)(2,1)}, bf16[1040,128]{1,0:T(8,128)(2,1)}, f32[8,1024]{1,0:T(8,128)}, f32[8,128]{1,0:T(8,128)}) custom-call(s32[1]{0:T(128)} %bitcast.place_ref, f32[16]{0:T(128)} %convert_subtract_fusion.keep_ref, f32[4]{0:T(128)} %compare_convert_fusion.1.flag_ref, f32[1040,1664]{1,0:T(8,128)} %fusion.31.pre_ref.small_ref.gate_ref, ...), custom_call_target="tpu_custom_call" | custom-call | tf_op jit(solution)/shard_map/mixer_backward/pallas_call | solution.py:794
  498.4 4.7 fusion.6
  508.0 3.2 collective-permute-done.1
  511.1 5.2 fusion
  519.1 2.6 copy.63
  521.7 2.3 convolution_convert_fusion.6
  524.6 3.2 convolution_convert_fusion
  528.0 2.5 copy.61
  534.3 16.5 %reduce-scatter.16.cloned.1.call-done = bf16[1024,256]{1,0:T(8,128)(2,1)} async-done(((bf16[1024,1024]{1,0:T(8,128)(2,1)}), bf16[1024,256]{1,0:T(8,128)(2,1)}) %reduce-scatter.16.cloned.1.call-update) | async-done | bytes 524304 | tf_op jit(solution)/shard_map/reduce_scatter | solution.py:894
  550.8 2.3 add_convert_fusion
  553.1 11.2 %psum.14 = f32[1024,1]{0,1:T(1,128)S(1)} all-reduce(f32[1024,1]{0,1:T(1,128)S(1)} %bitcast.99), channel_id=1, replica_groups=mesh['fsdp'=2,'heads'=4,'tensor'=4] {'tensor'}, use_global_device_ids=true, to_apply=%region_11.12 | all-reduce | flops 1024 | bytes 8192 | tf_op jit(solution)/shard_map/psum | solution.py:1081
  564.3 115.9 %all-reduce.7.cloned.1.call-done = f32[18704]{0:T(1024)} async-done(((f32[18704]{0:T(1024)}), f32[18704]{0:T(1024)}) %all-reduce.7.cloned.1.call-update) | async-done | bytes 74832 | tf_op jit(solution)/shard_map/psum | solution.py:1117
  687.7 36.0 %reduce-scatter.24.cloned.1.call-done = bf16[128,1024]{1,0:T(8,128)(2,1)} async-done(((bf16[1024,1024]{1,0:T(8,128)(2,1)}), bf16[128,1024]{1,0:T(8,128)(2,1)}) %reduce-scatter.24.cloned.1.call-update) | async-done | bytes 262160
  726.4 43.3 %reduce-scatter.22.cloned.1.call-done = bf16[128,1152]{1,0:T(8,128)(2,1)} async-done(((bf16[1024,1152]{1,0:T(8,128)(2,1)}), bf16[128,1152]{1,0:T(8,128)(2,1)}) %reduce-scatter.22.cloned.1.call-update) | async-done | bytes 294928
  773.9 39.6 %reduce-scatter.20.cloned.1.call-done = bf16[1024,256]{1,0:T(8,128)(2,1)} async-done(((bf16[1024,1024]{1,0:T(8,128)(2,1)}), bf16[1024,256]{1,0:T(8,128)(2,1)}) %reduce-scatter.20.cloned.1.call-update) | async-done | bytes 524304 | tf_op jit(solution)/shard_map/reduce_scatter | solution.py:894
  813.5 2.7 multiply_subtract_fusion.1
  (196 shorter events, 53.7 us)
Async XLA Ops:
  7.2 10.8 %copy-start = (f32[4,2048]{1,0:T(4,128)S(1)}, f32[4,2048]{1,0:T(4,128)}, u32[]{:S(2)}) copy-start(f32[4,2048]{1,0:T(4,128)} %param.34) | copy-start | bytes 98308
  7.2 4.8 copy-start.21
  7.2 47.9 %all-gather.13.cloned.1.call-start = ((), (), s32[]{:S(2)}) async-start(), calls=%async_computation.7 | async-start | bytes 2621440 | tf_op jit(solution)/shard_map/all_gather | solution.py:890
  8.0 62.4 %all-gather.15.cloned.1.call-start = ((), (), s32[]{:S(2)}) async-start(), calls=%async_computation.8 | async-start | bytes 5111808 | tf_op jit(solution)/shard_map/all_gather | solution.py:954
  10.8 2.5 copy-start.10
  10.9 6.1 copy-start.28
  10.9 6.2 copy-start.29
  10.9 6.2 copy-start.30
  13.3 44.1 %copy-start.24 = (f32[1024]{0:T(1024)S(1)}, f32[1024]{0:T(1024)}, u32[]{:S(2)}) copy-start(f32[1024]{0:T(1024)} %param.24) | copy-start | bytes 12292
  13.3 92.9 %all-gather.17.cloned.1.call-start = ((), (), s32[]{:S(2)}) async-start(), calls=%async_computation.9 | async-start | bytes 1572864 | tf_op jit(solution)/shard_map/all_gather | solution.py:955
  13.4 7.5 collective-permute-start
  16.8 115.9 %all-gather.29.cloned.1.call-start = ((), (), s32[]{:S(2)}) async-start(), calls=%async_computation.20 | async-start | bytes 1769472 | tf_op jit(solution)/shard_map/all_gather | solution.py:991
  106.0 76.2 %reduce-scatter.14.cloned.1.call-start = ((), (), s32[]{:S(2)}) async-start(), calls=%async_computation.10 | async-start | bytes 2621440 | tf_op jit(solution)/shard_map/reduce_scatter | solution.py:894
  140.4 89.8 %all-gather.19.cloned.1.call-start = ((), (), s32[]{:S(2)}) async-start(), calls=%async_computation.11 | async-start | bytes 2621440 | tf_op jit(solution)/shard_map/all_gather | solution.py:890
  182.2 61.2 %all-gather.21.cloned.1.call-start = ((), (), s32[]{:S(2)}) async-start(), calls=%async_computation.12 | async-start | bytes 4325376 | tf_op jit(solution)/shard_map/all_gather | solution.py:956
  184.9 71.0 %all-gather.23.cloned.1.call-start = ((), (), s32[]{:S(2)}) async-start(), calls=%async_computation.13 | async-start | bytes 2162688 | tf_op jit(solution)/shard_map/all_gather | solution.py:957
  185.6 117.8 %all-gather.25.cloned.1.call-start = ((), (), s32[]{:S(2)}) async-start(), calls=%async_computation.15 | async-start | bytes 2621440 | tf_op jit(solution)/shard_map/all_gather | solution.py:890
  186.4 46.4 %copy-start.23 = (f32[1024]{0:T(1024)S(1)}, f32[1024]{0:T(1024)}, u32[]{:S(2)}) copy-start(f32[1024]{0:T(1024)} %param.38) | copy-start | bytes 12292
  186.4 172.5 %reduce-scatter.18.cloned.1.call-start = ((), (), s32[]{:S(2)}) async-start(), calls=%async_computation.16 | async-start | bytes 2621440 | tf_op jit(solution)/shard_map/reduce_scatter | solution.py:894
  230.3 2.5 copy-start.3
  243.4 5.4 copy-start.15
  243.4 5.4 copy-start.19
  303.4 7.7 copy-start.20
  317.6 89.4 %all-gather.27.cloned.1.call-start = ((), (), s32[]{:S(2)}) async-start(), calls=%async_computation.17 | async-start | bytes 2621440 | tf_op jit(solution)/shard_map/all_gather | solution.py:890
  358.9 100.4 %all-gather.31.cloned.1.call-start = ((), (), s32[]{:S(2)}) async-start(), calls=%async_computation.21 | async-start | bytes 1179648 | tf_op jit(solution)/shard_map/all_gather | solution.py:1026
  407.0 5.1 copy-start.4
  407.0 5.2 copy-start.6
  407.0 5.3 copy-start.13
  427.7 103.6 %reduce-scatter.26.cloned.1.call-start = ((), (), s32[]{:S(2)}) async-start(), calls=%async_computation.24 | async-start | bytes 5013504
  427.7 3.9 copy-start.16
  427.7 3.9 copy-start.32
  444.0 106.8 %reduce-scatter.16.cloned.1.call-start = ((), (), s32[]{:S(2)}) async-start(), calls=%async_computation.14 | async-start | bytes 2621440 | tf_op jit(solution)/shard_map/reduce_scatter | solution.py:894
  451.5 228.8 %all-reduce.7.cloned.1.call-start = ((), (), s32[]{:S(2)}) async-start(), calls=%async_computation.19 | async-start | bytes 155648 | tf_op jit(solution)/shard_map/psum | solution.py:1117
  451.5 3.2 copy-start.5
  451.5 3.2 copy-start.27
  454.7 2.3 copy-start.17
  457.1 47.9 %slice-start = ((s8[4259840]{0:T(1024)(128)(4,1)}), s8[65536]{0:T(1024)(128)(4,1)S(1)}, s32[]{:S(2)}) async-start(s8[4259840]{0:T(1024)(128)(4,1)} %bitcast.83), calls=%async_computation.25 | async-start | bytes 131072
  459.3 45.6 %slice-start.1 = ((s8[4259840]{0:T(1024)(128)(4,1)}), s8[4194304]{0:T(1024)(128)(4,1)S(1)}, s32[]{:S(2)}) async-start(s8[4259840]{0:T(1024)(128)(4,1)} %bitcast.83), calls=%async_computation.26 | async-start | bytes 8388608
  498.4 4.7 copy-start.22
  503.1 4.0 copy-start.25
  503.1 8.0 copy-start.18
  505.0 6.2 collective-permute-start.1
  517.1 206.6 %reduce-scatter.24.cloned.1.call-start = ((), (), s32[]{:S(2)}) async-start(), calls=%async_computation.23 | async-start | bytes 2359296
  521.7 2.4 copy-start.12
  521.7 248.1 %reduce-scatter.22.cloned.1.call-start = ((), (), s32[]{:S(2)}) async-start(), calls=%async_computation.22 | async-start | bytes 2654208
  521.7 2.8 copy-start.26
  530.5 283.0 %reduce-scatter.20.cloned.1.call-start = ((), (), s32[]{:S(2)}) async-start(), calls=%async_computation.18 | async-start | bytes 2621440 | tf_op jit(solution)/shard_map/reduce_scatter | solution.py:894
  770.9 45.3 %copy-start.1 = (f32[4,2048]{1,0:T(4,128)S(1)}, f32[4,2048]{1,0:T(4,128)}, u32[]{:S(2)}) copy-start(f32[4,2048]{1,0:T(4,128)} %param.34) | copy-start | bytes 98308
  (8 other events, 14.4 us)
Sparse Core Ops, SparseCore 0:
  9.6 45.4 all-gather.12
  56.7 13.6 all-gather.14
  71.9 10.1 all-gather.16
  106.1 26.5 all-gather.28
  140.6 41.6 reduce-scatter.13
  183.7 46.5 all-gather.18
  231.9 11.5 all-gather.20
  245.0 10.7 all-gather.22
  257.5 45.8 all-gather.24
  317.7 41.1 reduce-scatter.17
  360.4 46.5 all-gather.26
  427.8 23.0 all-gather.30
  454.3 52.6 reduce-scatter.25
  509.2 41.4 reduce-scatter.15
  556.8 123.4 all-reduce.6
  683.4 40.2 reduce-scatter.23
  727.2 42.4 reduce-scatter.21
  771.9 41.5 reduce-scatter.19

commit v2 on v1

v2 whole, which is shorter than its diff:
```python
import functools

import jax
import jax.numpy as jnp
from jax import lax
from jax.experimental import pallas as pl
from jax.experimental.pallas import tpu as pltpu
from jax.sharding import PartitionSpec as P

CONV = 4
GROUP = 64
RIM = 16
PACK = 256
LANES = 128
LONGEST = 4096
EPSILON = 1e-06
FH = ("fsdp", "heads")
ALL = ("fsdp", "heads", "tensor")
BF = jnp.bfloat16
F32 = jnp.float32
VMEM_LIMIT = 56 * 1024 * 1024
INVERSE_PASSES = 1
CHUNKS = 2


def cost(micros):
    return pl.CostEstimate(flops=int(micros * 1e9), bytes_accessed=int(micros * 3e6), transcendentals=0)


def shifted(shard, axis, by):
    devices = lax.axis_size(axis)
    pairs = [(i, i + by) for i in range(devices) if 0 <= i + by < devices]
    return lax.ppermute(shard, axis, pairs)


def dot_on(left, right, left_dim, right_dim):
    return lax.dot_general(
        left.astype(BF),
        right.astype(BF),
        (((left_dim,), (right_dim,)), ((), ())),
        preferred_element_type=F32,
    )


def mm(left, right):
    return dot_on(left, right, 1, 0)


def mm_tn(left, right):
    return dot_on(left, right, 0, 0)


def mm_nt(left, right):
    return dot_on(left, right, 1, 1)


def mm_fine(left, right):
    if INVERSE_PASSES == 1:
        return mm(left, right)
    left_high, right_high = left.astype(BF), right.astype(BF)
    left_low = left - left_high.astype(F32)
    right_low = right - right_high.astype(F32)
    return mm(left_high, right_high) + mm(left_low, right_high) + mm(left_high, right_low)


def sigmoid(value):
    return 1.0 / (1.0 + jnp.exp(-value))


def softplus(value):
    return jnp.maximum(value, 0.0) + jnp.log(1.0 + jnp.exp(-jnp.abs(value)))


def window_taps(window, rows):
    total = window.shape[0]
    return [pltpu.roll(window, total - (RIM - CONV + 1 + j), 0)[:rows] for j in range(CONV)]


def pack_masks():
    row = lax.broadcasted_iota(jnp.int32, (PACK, PACK), 0)
    col = lax.broadcasted_iota(jnp.int32, (PACK, PACK), 1)
    apart = row ^ col
    same = apart < GROUP
    return row, col, apart, same, same & (row >= col), same & (row > col)


def packed_decay(decay, masks):
    row, col, apart, same, lower, strict = masks
    spread = jnp.broadcast_to(decay, (PACK, PACK))
    decay_row = jnp.sum(jnp.where(apart == 0, spread, 0.0), axis=0, keepdims=True)
    gam_row = jnp.sum(jnp.where(same & (row <= col), spread, 0.0), axis=0, keepdims=True)
    spread_row = jnp.broadcast_to(decay_row, (PACK, PACK))
    gam = jnp.sum(jnp.where(lower, spread_row, 0.0), axis=1, keepdims=True)
    last = jnp.sum(jnp.where(same, spread_row, 0.0), axis=1, keepdims=True)
    fading = jnp.where(lower, jnp.exp(jnp.where(lower, gam - gam_row, 0.0)), 0.0)
    return gam, last, fading


def rates_of(small, rate, bias):
    decay_tile = -jnp.exp(rate) * softplus(small + bias)
    return decay_tile, sigmoid(small)


def load_window(pre_ref, group, first, width, rows):
    start = group * PACK
    before = jnp.where(group == 0, rows, start - RIM)
    head = pre_ref[pl.ds(pl.multiple_of(before, RIM), RIM), first : first + width]
    body = pre_ref[pl.ds(pl.multiple_of(start, PACK), PACK), first : first + width]
    return jnp.concatenate([head, body], axis=0)


def active_of(window, taps_ref, valid, first, width):
    pieces = window_taps(window, PACK)
    conv = None
    for j in range(CONV):
        term = pieces[j] * taps_ref[j : j + 1, first : first + width] * valid[:, j : j + 1]
        conv = term if conv is None else conv + term
    return conv, pieces


def net_of(changes, apart):
    column = jnp.sum(changes, axis=0, keepdims=True)
    column = jnp.where(apart == 0, jnp.broadcast_to(column, changes.shape), 0.0)
    return jnp.sum(changes - column, axis=1, keepdims=True)


def column_of(tile, lane):
    return tile[:, lane : lane + 1].astype(BF).astype(F32)


def forward_kernel(
    keep_ref,
    pre_ref,
    small_ref,
    taps_ref,
    valid_ref,
    rate_ref,
    bias_ref,
    keys_ref,
    inverse_ref,
    w_ref,
    u_ref,
    fold_ref,
    states_ref,
    ends_ref,
    fresh_ref,
    last_ref,
    joint_ref,
    *,
    heads,
    rows,
    key_width,
    value_width,
):
    groups = rows // PACK
    inner = PACK // GROUP
    key_cols = heads * key_width

    def solve(group, _):
        masks = pack_masks()
        row, col, apart, same, lower, strict = masks
        start = pl.multiple_of(group * PACK, PACK)
        span = pl.ds(start, PACK)
        valid = valid_ref[span, :]
        decay_tile, beta_tile = rates_of(small_ref[span, :], rate_ref[...], bias_ref[...])
        items = []
        for head in range(heads):
            decay = column_of(decay_tile, head)
            beta = column_of(beta_tile, heads + head)
            first = key_cols + head * key_width
            window = load_window(pre_ref, group, first, key_width, rows)
            conv, _ = active_of(window, taps_ref, valid, first, key_width)
            act = conv * sigmoid(conv)
            scale = lax.rsqrt(jnp.sum(act * act, axis=1, keepdims=True) + EPSILON)
            key = (act * scale).astype(BF)
            keys_ref[span, head * key_width : (head + 1) * key_width] = key
            gam, last, fading = packed_decay(decay, masks)
            gram = mm_nt(key, key)
            system = jnp.where(strict, fading * beta * gram, 0.0)
            inverse = jnp.where(apart == 0, 1.0, 0.0) - jnp.where(apart == 1, system, 0.0)
            items.append([beta, key, gam, last, system, inverse])
        level = 1
        while (1 << level) < GROUP:
            parts = [
                mm_fine(jnp.where((apart >> level) == 1, item[4], 0.0), item[5]) for item in items
            ]
            steps = [mm_fine(item[5], part) for item, part in zip(items, parts)]
            for item, step in zip(items, steps):
                item[5] = item[5] - step
            level += 1
        for head in range(heads):
            beta, key, gam, last, system, inverse = items[head]
            cols = slice(head * value_width, (head + 1) * value_width)
            first = 2 * key_cols + head * value_width
            window = load_window(pre_ref, group, first, value_width, rows)
            conv, _ = active_of(window, taps_ref, valid, first, value_width)
            value = (conv * sigmoid(conv)).astype(BF)
            keys_ref[span, key_cols + head * value_width : key_cols + (head + 1) * value_width] = (
                value
            )
            key_f = key.astype(F32)
            inverse_low = inverse.astype(BF)
            inverse_ref[group * heads + head] = inverse_low
            w_low = mm(inverse_low, beta * jnp.exp(gam) * key_f).astype(BF)
            u_low = mm(inverse_low, beta * value.astype(F32)).astype(BF)
            w_ref[span, head * key_width : (head + 1) * key_width] = w_low
            u_ref[span, cols] = u_low
            tail = jnp.exp(last - gam) * key_f
            block_of = lax.broadcasted_iota(jnp.int32, (PACK, 1), 0) // GROUP
            whole = jnp.exp(last)
            for b in range(inner):
                index = (group * inner + b) * heads + head
                tail_b = jnp.where(block_of == b, tail, 0.0).astype(BF)
                fold_ref[index] = mm_tn(tail_b, w_low).astype(BF)
                fresh_ref[index] = mm_tn(tail_b, u_low)
                last_ref[index] = jnp.broadcast_to(
                    whole[b * GROUP : b * GROUP + 1], (8, LANES)
                )
        return 0

    lax.fori_loop(0, groups, solve, 0)

    unit = jnp.where(
        lax.broadcasted_iota(jnp.int32, (key_width, key_width), 0)
        == lax.broadcasted_iota(jnp.int32, (key_width, key_width), 1),
        1.0,
        0.0,
    )
    for head in range(heads):
        joint_ref[head, :, :value_width] = jnp.zeros((key_width, value_width), F32)
        joint_ref[head, :, value_width:] = unit
    for block in range(rows // GROUP):
        for head in range(heads):
            index = block * heads + head
            joint = joint_ref[head] * keep_ref[block]
            joint_low = joint.astype(BF)
            states_ref[index] = joint_low
            fresh = last_ref[index, 0:1, 0:1] * joint - mm(fold_ref[index], joint_low)
            joint_ref[head, :, :value_width] = fresh[:, :value_width] + fresh_ref[index]
            joint_ref[head, :, value_width:] = fresh[:, value_width:]
    ends_ref[...] = joint_ref[...].astype(BF)


def mixer_forward(pre, keep, taps, valid, rate, bias, heads, key_width, value_width):
    rows = pre.shape[0] - RIM
    wide = heads * (2 * key_width + value_width)
    gate_wide = heads * value_width
    count = rows // GROUP
    packs = rows // PACK
    joint_width = key_width + value_width
    whole = lambda shape: pl.BlockSpec(shape, lambda i: (0,) * len(shape))
    outs = [
        ((rows, wide - heads * key_width), BF),
        ((packs * heads, PACK, PACK), BF),
        ((rows, heads * key_width), BF),
        ((rows, heads * value_width), BF),
        ((count * heads, key_width, key_width), BF),
        ((count * heads, key_width, joint_width), BF),
        ((heads, key_width, joint_width), BF),
    ]
    return pl.pallas_call(
        functools.partial(
            forward_kernel, heads=heads, rows=rows, key_width=key_width, value_width=value_width
        ),
        grid=(1,),
        in_specs=[
            pl.BlockSpec(memory_space=pltpu.SMEM),
            pl.BlockSpec((rows + RIM, wide), lambda i: (0, 0)),
            pl.BlockSpec((rows + RIM, LANES), lambda i: (0, (wide + gate_wide) // LANES)),
            whole(taps.shape),
            whole(valid.shape),
            whole(rate.shape),
            whole(bias.shape),
        ],
        out_specs=[whole(shape) for shape, _ in outs],
        out_shape=[jax.ShapeDtypeStruct(shape, kind) for shape, kind in outs],
        scratch_shapes=[
            pltpu.VMEM((count * heads, key_width, value_width), F32),
            pltpu.VMEM((count * heads, 8, LANES), F32),
            pltpu.VMEM((heads, key_width, joint_width), F32),
        ],
        compiler_params=pltpu.CompilerParams(vmem_limit_bytes=VMEM_LIMIT),
        cost_estimate=cost(20),
        name="mixer_forward",
    )(keep, pre, pre, taps, valid, rate, bias)


def query_kernel(
    pre_ref,
    small_ref,
    taps_ref,
    valid_ref,
    rate_ref,
    bias_ref,
    keys_ref,
    w_ref,
    u_ref,
    states_ref,
    queries_ref,
    query_w_ref,
    local_ref,
    carry_ref,
    *,
    heads,
    rows,
    key_width,
    value_width,
):
    inner = PACK // GROUP

    def ask(group, _):
        masks = pack_masks()
        span = pl.ds(pl.multiple_of(group * PACK, PACK), PACK)
        valid = valid_ref[span, :]
        decay_tile, _ = rates_of(small_ref[span, :], rate_ref[...], bias_ref[...])
        for head in range(heads):
            cols = slice(head * key_width, (head + 1) * key_width)
            value_at = slice(head * value_width, (head + 1) * value_width)
            window = load_window(pre_ref, group, head * key_width, key_width, rows)
            conv, _ = active_of(window, taps_ref, valid, head * key_width, key_width)
            act = conv * sigmoid(conv)
            scale = lax.rsqrt(jnp.sum(act * act, axis=1, keepdims=True) + EPSILON)
            query = (act * (scale * key_width ** (-0.5))).astype(BF)
            queries_ref[span, cols] = query
            gam, last, fading = packed_decay(column_of(decay_tile, head), masks)
            scores = (mm_nt(query, keys_ref[span, cols]) * fading).astype(BF)
            query_w = (
                jnp.exp(gam) * query.astype(F32) - mm(scores, w_ref[span, cols])
            ).astype(BF)
            start = mm(scores, u_ref[span, value_at])
            local, carry = [], []
            for b in range(inner):
                index = (group * inner + b) * heads + head
                part = slice(b * GROUP, (b + 1) * GROUP)
                query_w_ref[index] = query_w[part]
                moved = mm(query_w[part], states_ref[index])
                local.append(moved[:, :value_width])
                carry.append(moved[:, value_width:])
            local_ref[span, value_at] = start + jnp.concatenate(local, axis=0)
            carry_ref[span, cols] = jnp.concatenate(carry, axis=0).astype(BF)
        return 0

    lax.fori_loop(0, rows // PACK, ask, 0)


def mixer_query(pre, taps, valid, rate, bias, keys, w, u, states, heads, key_width, value_width):
    rows = pre.shape[0] - RIM
    wide = heads * (2 * key_width + value_width)
    gate_wide = heads * value_width
    whole = lambda shape: pl.BlockSpec(shape, lambda i: (0,) * len(shape))
    outs = [
        ((rows, heads * key_width), BF),
        ((rows // GROUP * heads, GROUP, key_width), BF),
        ((rows, heads * value_width), F32),
        ((rows, heads * key_width), BF),
    ]
    return pl.pallas_call(
        functools.partial(
            query_kernel, heads=heads, rows=rows, key_width=key_width, value_width=value_width
        ),
        grid=(1,),
        in_specs=[
            pl.BlockSpec((rows + RIM, heads * key_width), lambda i: (0, 0)),
            pl.BlockSpec((rows + RIM, LANES), lambda i: (0, (wide + gate_wide) // LANES)),
            whole(taps.shape),
            whole(valid.shape),
            whole(rate.shape),
            whole(bias.shape),
            pl.BlockSpec((rows, heads * key_width), lambda i: (0, 0)),
            whole(w.shape),
            whole(u.shape),
            whole(states.shape),
        ],
        out_specs=[whole(shape) for shape, _ in outs],
        out_shape=[jax.ShapeDtypeStruct(shape, kind) for shape, kind in outs],
        compiler_params=pltpu.CompilerParams(vmem_limit_bytes=VMEM_LIMIT),
        cost_estimate=cost(10),
        name="mixer_query",
    )(pre, pre, taps, valid, rate, bias, keys, w, u, states)


def rotated(shard, axis, by):
    devices = lax.axis_size(axis)
    return lax.ppermute(shard, axis, [(i, (i + by) % devices) for i in range(devices)])


def rotations(shard, axis):
    return [shard] + [rotated(shard, axis, by) for by in range(1, lax.axis_size(axis))]


def scattered(pieces, axis):
    total = pieces[0].astype(F32)
    for by in range(1, lax.axis_size(axis)):
        total = total + rotated(pieces[by], axis, by).astype(F32)
    return total


def axis_total(values, axis):
    return scattered([values] * lax.axis_size(axis), axis)


def exchanged(parts):
    return rotations(scattered(parts, "tensor").astype(BF), "tensor")


def swapped(shard):
    return lax.ppermute(shard, "fsdp", [(0, 1), (1, 0)])


def weight_rows(shard, axis):
    return lax.all_gather(shard, "fsdp", axis=axis, tiled=True)


def owners(grad):
    return lax.psum_scatter(grad, FH, scatter_dimension=0, tiled=True).astype(F32)


def owners_by_steps(grad):
    if lax.axis_size("fsdp") != 2:
        return owners(grad)
    half = grad.shape[0] // 2
    core = lax.axis_index("fsdp")
    mine = lax.dynamic_slice_in_dim(grad, core * half, half)
    other = swapped(lax.dynamic_slice_in_dim(grad, (1 - core) * half, half))
    grad = (mine.astype(F32) + other.astype(F32)).astype(BF)
    count = lax.axis_size("heads")
    rows = half // count
    spot = lax.axis_index("heads")
    return scattered(
        [
            lax.dynamic_slice_in_dim(grad, lax.rem(spot + by, count) * rows, rows)
            for by in range(count)
        ],
        "heads",
    )


def padded(width):
    return -(-width // LANES) * LANES


def weight_kernel(*refs, rows):
    out_ref = refs[-1]
    at = 0
    for index, many in enumerate(rows):
        left, right = refs[2 * index], refs[2 * index + 1]
        width = right.shape[1]
        part = mm_tn(left[...], right[...]).astype(BF)
        out_ref[:, at : at + width] = part
        if width < padded(width):
            out_ref[:, at + width : at + padded(width)] = jnp.zeros(
                (part.shape[0], padded(width) - width), BF
            )
        at += padded(width)


def weight_grads(*pairs):
    features = pairs[0][0].shape[1]
    total = sum(padded(right.shape[1]) for _, right in pairs)
    specs, args = [], []
    for left, right in pairs:
        many = right.shape[0]
        specs.append(pl.BlockSpec((many, PACK), lambda i: (0, i)))
        specs.append(pl.BlockSpec(right.shape, lambda i: (0, 0)))
        args += [left, right]
    return pl.pallas_call(
        functools.partial(weight_kernel, rows=[right.shape[0] for _, right in pairs]),
        grid=(features // PACK,),
        in_specs=specs,
        out_specs=pl.BlockSpec((PACK, total), lambda i: (i, 0)),
        out_shape=jax.ShapeDtypeStruct((features, total), BF),
        compiler_params=pltpu.CompilerParams(vmem_limit_bytes=VMEM_LIMIT),
        cost_estimate=cost(5),
        name="weight_grads",
    )(*args)


def total_batches(values):
    if lax.axis_size("fsdp") == 2:
        values = values + swapped(values)
    else:
        values = lax.psum(values, "fsdp")
    return axis_total(values, "heads")


def feature_blocks(pieces, place, whole_ref):
    count = len(pieces)
    width = whole_ref.shape[1] // count
    for by, piece in enumerate(pieces):
        at = lax.rem(place + count - by, count) * width
        whole_ref[:, pl.ds(pl.multiple_of(at, width), width)] = piece


def project_kernel(place_ref, *refs, count):
    pieces = refs[:count]
    gain_ref, weight_ref, token_ref, hidden_ref, scale_ref, pre_ref = refs[count:]
    rows = pieces[0].shape[0] - RIM

    @pl.when(pl.program_id(0) == 0)
    def _():
        feature_blocks([piece[...] for piece in pieces], place_ref[0], token_ref)

        def norm(start, many):
            span = pl.ds(start, many)
            values = token_ref[span, :].astype(F32)
            scale = lax.rsqrt(jnp.mean(values * values, axis=1, keepdims=True) + EPSILON)
            hidden_ref[span, :] = (values * scale * gain_ref[...]).astype(BF)
            scale_ref[span, :] = jnp.broadcast_to(scale, (many, LANES))

        for start in range(0, rows, PACK):
            norm(start, PACK)
        norm(rows, RIM)

    pre_ref[...] = mm(hidden_ref[...], weight_ref[...])


def project(tensor_place, pieces, gain, weight):
    total = pieces[0].shape[0]
    features, outs = weight.shape
    count = len(pieces)
    tile = 2 * LANES
    whole = lambda shape: pl.BlockSpec(shape, lambda i, at: (0,) * len(shape))
    return pl.pallas_call(
        functools.partial(project_kernel, count=count),
        grid_spec=pltpu.PrefetchScalarGridSpec(
            num_scalar_prefetch=1,
            grid=(outs // tile,),
            in_specs=[whole(piece.shape) for piece in pieces]
            + [whole(gain.shape), pl.BlockSpec((features, tile), lambda i, at: (0, i))],
            out_specs=[
                whole((total, features)),
                whole((total, features)),
                whole((total, LANES)),
                pl.BlockSpec((total, tile), lambda i, at: (0, i)),
            ],
        ),
        out_shape=[
            jax.ShapeDtypeStruct((total, features), BF),
            jax.ShapeDtypeStruct((total, features), BF),
            jax.ShapeDtypeStruct((total, LANES), F32),
            jax.ShapeDtypeStruct((total, outs), F32),
        ],
        compiler_params=pltpu.CompilerParams(vmem_limit_bytes=VMEM_LIMIT),
        cost_estimate=cost(8),
        name="project",
    )(tensor_place, *pieces, gain, weight)


def output_kernel(
    place_ref,
    local_ref,
    carry_ref,
    end1_ref,
    end2_ref,
    end3_ref,
    end4_ref,
    gate_ref,
    gain_ref,
    weight_ref,
    mixed_ref,
    normed_ref,
    enter_ref,
    *partial_refs,
    heads,
    key_width,
    value_width,
    chunks,
):
    step = pl.program_id(0)

    @pl.when(step == 0)
    def _():
        for head in range(heads):
            state = end4_ref[head, :, :value_width].astype(F32)
            for end in (end3_ref, end2_ref, end1_ref):
                state = end[head, :, :value_width].astype(F32) + mm(
                    end[head, :, value_width:], state
                )
            enter_ref[head] = state.astype(BF)

    for head in range(heads):
        cols = slice(head * value_width, (head + 1) * value_width)
        mixed = local_ref[:, cols] + mm(
            carry_ref[:, head * key_width : (head + 1) * key_width], enter_ref[head]
        )
        mixed_low = mixed.astype(BF)
        mixed_ref[:, cols] = mixed_low
        mixed = mixed_low.astype(F32)
        scale = lax.rsqrt(jnp.mean(mixed * mixed, axis=1, keepdims=True) + EPSILON)
        gate = gate_ref[:, cols]
        normed = mixed * scale * gain_ref[...] * (gate * sigmoid(gate))
        normed_ref[:, cols] = normed.astype(BF)
    count = len(partial_refs) // chunks
    width = weight_ref.shape[1] // count
    steps = pl.num_programs(0) // chunks
    for by in range(count):
        at = lax.rem(place_ref[0] + by, count) * width
        part = mm(normed_ref[...], weight_ref[:, pl.ds(pl.multiple_of(at, width), width)])
        for chunk in range(chunks):

            @pl.when(step // steps == chunk)
            def _():
                partial_refs[chunk * count + by][...] = part.astype(BF)


def mixer_output(
    local, carry, ends, tensor_place, pre, gain, weight, key_width, value_width, chunks, count
):
    rows, cols = local.shape
    heads = cols // value_width
    width = weight.shape[1] // count
    gate_block = heads * (2 * key_width + value_width) // cols
    steps = rows // PACK // chunks
    whole = lambda shape: pl.BlockSpec(shape, lambda i, at: (0,) * len(shape))

    def part_spec(chunk):
        return pl.BlockSpec(
            (PACK, width), lambda i, at: (jnp.clip(i - chunk * steps, 0, steps - 1), 0)
        )

    outs = pl.pallas_call(
        functools.partial(
            output_kernel,
            heads=heads,
            key_width=key_width,
            value_width=value_width,
            chunks=chunks,
        ),
        grid_spec=pltpu.PrefetchScalarGridSpec(
            num_scalar_prefetch=1,
            grid=(rows // PACK,),
            in_specs=[
                pl.BlockSpec((PACK, cols), lambda i, at: (i, 0)),
                pl.BlockSpec((PACK, carry.shape[1]), lambda i, at: (i, 0)),
                whole(ends[0].shape),
                whole(ends[0].shape),
                whole(ends[0].shape),
                whole(ends[0].shape),
                pl.BlockSpec((PACK, cols), lambda i, at: (i, gate_block)),
                whole(gain.shape),
                whole((cols, weight.shape[1])),
            ],
            out_specs=[
                pl.BlockSpec((PACK, cols), lambda i, at: (i, 0)),
                pl.BlockSpec((PACK, cols), lambda i, at: (i, 0)),
                whole((heads, key_width, value_width)),
            ]
            + [part_spec(chunk) for chunk in range(chunks) for _ in range(count)],
        ),
        out_shape=[
            jax.ShapeDtypeStruct((rows, cols), BF),
            jax.ShapeDtypeStruct((rows, cols), BF),
            jax.ShapeDtypeStruct((heads, key_width, value_width), BF),
        ]
        + [jax.ShapeDtypeStruct((rows // chunks, width), BF)] * (chunks * count),
        compiler_params=pltpu.CompilerParams(vmem_limit_bytes=VMEM_LIMIT),
        cost_estimate=cost(7),
        name="mixer_output",
    )(tensor_place, local, carry, *ends, pre, gain, weight)
    parts = outs[3:]
    return outs[0], outs[1], outs[2], [parts[c * count : (c + 1) * count] for c in range(chunks)]


def feed_kernel(place_ref, *refs, count, aliased):
    attn = refs[:count]
    cot_ref, token_ref, gain_ref, gate_ref, up_ref, down_ref = refs[count : count + 6]
    outs = refs[count + 6 + aliased :]
    middle_ref, hidden_ref, inner_ref, gate_grad_ref, up_grad_ref = outs[:5]
    out_refs, mid_refs = outs[5 : 5 + count], outs[5 + count : 5 + 2 * count]
    whole_ref = outs[5 + 2 * count]
    first = down_ref.shape[0] - inner_ref.shape[1]
    place = place_ref[0]
    feature_blocks([piece[...] for piece in attn], place, whole_ref)
    middle = token_ref[...].astype(F32) + whole_ref[...].astype(F32)
    middle_ref[...] = middle
    scale = lax.rsqrt(jnp.mean(middle * middle, axis=1, keepdims=True) + EPSILON)
    hidden = (middle * scale * gain_ref[...]).astype(BF)
    hidden_ref[...] = hidden
    many = inner_ref.shape[1]
    gate = mm(hidden, gate_ref[:, :many])
    up = mm(hidden, up_ref[:, :many])
    inner_grad = mm_nt(cot_ref[...], down_ref[first:, :])
    sig = sigmoid(gate)
    silu = gate * sig
    inner_ref[...] = (silu * up).astype(BF)
    gate_grad_ref[...] = (inner_grad * up * (sig * (1.0 + gate * (1.0 - sig)))).astype(BF)
    up_grad_ref[...] = (inner_grad * silu).astype(BF)
    width = whole_ref.shape[1] // count
    for by in range(count):
        at = lax.rem(place + by, count) * width
        span = pl.ds(pl.multiple_of(at, width), width)
        mid_refs[by][...] = (
            mm_nt(gate_grad_ref[...], gate_ref[span, :many])
            + mm_nt(up_grad_ref[...], up_ref[span, :many])
        ).astype(BF)
        out_refs[by][...] = mm(inner_ref[...], down_ref[first:, span]).astype(BF)


def feed_forward(chunk, chunks, tensor_place, attn, cot, token, gain, feed, down, hidden, before):
    rows, features = cot.shape
    count = len(attn)
    width = features // count
    steps = rows // PACK // chunks
    first = chunk * steps
    whole = lambda shape: pl.BlockSpec(shape, lambda i, at: (0,) * len(shape))
    rows_at = lambda size: pl.BlockSpec((PACK, size), lambda i, at: (first + i, 0))
    part = pl.BlockSpec((PACK, width), lambda i, at: (i, 0))
    inputs = [*attn, cot, token, gain, feed, feed, down]
    kept = [
        (features, F32),
        (features, BF),
        (hidden, BF),
        (hidden, BF),
        (hidden, BF),
    ] + [(width, BF)] * count
    outs = pl.pallas_call(
        functools.partial(feed_kernel, count=count, aliased=len(before)),
        grid_spec=pltpu.PrefetchScalarGridSpec(
            num_scalar_prefetch=1,
            grid=(steps,),
            in_specs=[part] * count
            + [rows_at(features)] * 2
            + [
                whole(gain.shape),
                pl.BlockSpec((features, feed.shape[1] // 2), lambda i, at: (0, 0)),
                pl.BlockSpec((features, feed.shape[1] // 2), lambda i, at: (0, 1)),
                whole(down.shape),
            ]
            + [pl.BlockSpec(memory_space=pl.ANY)] * len(before),
            out_specs=[rows_at(size) for size, _ in kept] + [part] * count,
            scratch_shapes=[pltpu.VMEM((PACK, features), BF)],
        ),
        out_shape=[jax.ShapeDtypeStruct((rows, size), kind) for size, kind in kept]
        + [jax.ShapeDtypeStruct((rows // chunks, width), BF)] * count,
        input_output_aliases={1 + len(inputs) + i: i for i in range(len(before))},
        compiler_params=pltpu.CompilerParams(vmem_limit_bytes=VMEM_LIMIT),
        cost_estimate=cost(10),
        name="feed_forward",
    )(tensor_place, *inputs, *before)
    return outs[: 5 + count], outs[5 + count :]


def gate_back_kernel(
    place_ref, *refs, count, aliased, heads, key_width, value_width
):
    pieces = refs[:count]
    (
        middle_ref,
        cot_ref,
        ffn_gain_ref,
        weight_ref,
        mixed_ref,
        gate_ref,
        gain_ref,
        query_w_ref,
        states_ref,
    ) = refs[count : count + 9]
    (
        attn_grad_ref,
        mixed_grad_ref,
        gate_grad_ref,
        source_ref,
        own_ref,
        ffn_gain_grad_ref,
        gain_grad_ref,
        enter_grad_ref,
        whole_ref,
        middle_grad_ref,
    ) = refs[count + 9 + aliased :]
    inner = PACK // GROUP

    @pl.when(pl.program_id(0) == 0)
    def _():
        gain_grad_ref[...] = jnp.zeros_like(gain_grad_ref)
        ffn_gain_grad_ref[...] = jnp.zeros_like(ffn_gain_grad_ref)
        enter_grad_ref[...] = jnp.zeros_like(enter_grad_ref)

    feature_blocks([piece[...] for piece in pieces], place_ref[0], whole_ref)
    middle = middle_ref[...]
    scale_mid = lax.rsqrt(jnp.mean(middle * middle, axis=1, keepdims=True) + EPSILON)
    hidden_grad = whole_ref[...].astype(F32)
    unit_mid = middle * scale_mid
    ffn_gain_grad_ref[0:1, :] += jnp.sum(hidden_grad * unit_mid, axis=0, keepdims=True)
    scaled_mid = hidden_grad * ffn_gain_ref[...]
    along = jnp.mean(scaled_mid * unit_mid, axis=1, keepdims=True)
    middle_grad = cot_ref[...].astype(F32) + scale_mid * (scaled_mid - unit_mid * along)
    middle_grad_ref[...] = middle_grad
    width = own_ref.shape[1]
    own_ref[...] = middle_grad_ref[
        :, pl.ds(pl.multiple_of(place_ref[0] * width, width), width)
    ]
    attn_grad = middle_grad.astype(BF)
    attn_grad_ref[...] = attn_grad
    normed_grad = mm_nt(attn_grad, weight_ref[...])
    gain = gain_ref[...]
    for head in range(heads):
        cols = slice(head * value_width, (head + 1) * value_width)
        grad = normed_grad[:, cols]
        mixed = mixed_ref[:, cols].astype(F32)
        scale = lax.rsqrt(jnp.mean(mixed * mixed, axis=1, keepdims=True) + EPSILON)
        gate = gate_ref[:, cols]
        sig = sigmoid(gate)
        silu = gate * sig
        unit = mixed * scale
        scaled = grad * unit
        gate_grad_ref[:, cols] = (scaled * gain * (sig * (1.0 + gate * (1.0 - sig)))).astype(BF)
        gain_grad_ref[0:1, :] += jnp.sum(scaled * silu, axis=0, keepdims=True)
        unit_grad = grad * gain * silu
        mixed_grad = scale * (unit_grad - unit * jnp.mean(unit_grad * unit, axis=1, keepdims=True))
        mixed_grad = mixed_grad.astype(BF)
        mixed_grad_ref[:, cols] = mixed_grad
        total = enter_grad_ref[head]
        for b in range(inner):
            index = b * heads + head
            source = mm_tn(
                query_w_ref[index], mixed_grad[b * GROUP : (b + 1) * GROUP]
            )
            source_ref[index] = source
            total = total + mm_tn(states_ref[index, :, value_width:], source)
        enter_grad_ref[head] = total


def gate_back(
    chunk,
    chunks,
    tensor_place,
    pieces,
    middle,
    cot,
    ffn_gain,
    weight,
    mixed,
    pre,
    gain,
    query_w,
    states,
    before,
    key_width,
    value_width,
):
    rows, features = middle.shape
    width = pieces[0].shape[1]
    cols = mixed.shape[1]
    heads = cols // value_width
    gate_block = heads * (2 * key_width + value_width) // cols
    step = PACK // GROUP * heads
    steps = rows // PACK // chunks
    first = chunk * steps
    whole = lambda shape: pl.BlockSpec(shape, lambda i, at: (0,) * len(shape))
    rows_at = lambda size, col=0: pl.BlockSpec((PACK, size), lambda i, at: (first + i, col))
    blocks_at = lambda shape: pl.BlockSpec((step,) + shape, lambda i, at: (first + i, 0, 0))
    inputs = [*pieces, middle, cot, ffn_gain, weight, mixed, pre, gain, query_w, states]
    outs = pl.pallas_call(
        functools.partial(
            gate_back_kernel,
            count=len(pieces),
            aliased=len(before),
            heads=heads,
            key_width=key_width,
            value_width=value_width,
        ),
        grid_spec=pltpu.PrefetchScalarGridSpec(
            num_scalar_prefetch=1,
            grid=(steps,),
            in_specs=[pl.BlockSpec((PACK, width), lambda i, at: (i, 0))] * len(pieces)
            + [
                rows_at(features),
                rows_at(features),
                whole(ffn_gain.shape),
                whole((cols, features)),
                rows_at(cols),
                rows_at(cols, gate_block),
                whole(gain.shape),
                blocks_at(query_w.shape[1:]),
                blocks_at(states.shape[1:]),
            ]
            + [pl.BlockSpec(memory_space=pl.ANY)] * len(before),
            out_specs=[
                rows_at(features),
                rows_at(cols),
                rows_at(cols),
                blocks_at((key_width, value_width)),
                rows_at(width),
                whole((8, features)),
                whole((8, value_width)),
                whole((heads, key_width, value_width)),
            ],
            scratch_shapes=[pltpu.VMEM((PACK, features), BF), pltpu.VMEM((PACK, features), F32)],
        ),
        out_shape=[
            jax.ShapeDtypeStruct((rows, features), BF),
            jax.ShapeDtypeStruct((rows, cols), BF),
            jax.ShapeDtypeStruct((rows, cols), BF),
            jax.ShapeDtypeStruct((rows // GROUP * heads, key_width, value_width), F32),
            jax.ShapeDtypeStruct((rows, width), F32),
            jax.ShapeDtypeStruct((8, features), F32),
            jax.ShapeDtypeStruct((8, value_width), F32),
            jax.ShapeDtypeStruct((heads, key_width, value_width), F32),
        ],
        input_output_aliases={1 + len(inputs) + i: i for i in range(len(before))},
        compiler_params=pltpu.CompilerParams(vmem_limit_bytes=VMEM_LIMIT),
        cost_estimate=cost(7),
        name="gate_back",
    )(tensor_place, *inputs, *before)
    return outs[:5], outs[5:]


def input_kernel(
    place_ref,
    pre_grad_ref,
    small_grad_ref,
    gate_grad_ref,
    weight_ref,
    token_ref,
    scale_ref,
    gain_ref,
    dot_ref,
    gain_grad_ref,
    rim_ref,
    part_ref,
    terms_ref,
):
    rows = gate_grad_ref.shape[0]
    wide = pre_grad_ref.shape[1]
    gate_wide = gate_grad_ref.shape[1]
    small_wide = small_grad_ref.shape[1]
    width = token_ref.shape[1]
    step = pl.program_id(0)

    @pl.when(step == 0)
    def _():
        dot_ref[...] = jnp.zeros_like(dot_ref)

    terms = mm_nt(pre_grad_ref[...], weight_ref[:, :wide])
    terms = terms + mm_nt(
        small_grad_ref[...], weight_ref[:, wide + gate_wide : wide + gate_wide + small_wide]
    )
    terms_ref[...] = terms
    terms_ref[:rows, :] += mm_nt(gate_grad_ref[...], weight_ref[:, wide : wide + gate_wide])
    rim_ref[...] = terms_ref[rows:, :]
    terms = terms_ref[...]
    product = terms * token_ref[...].astype(F32)
    dot_ref[...] += jnp.sum(product * gain_ref[...], axis=1, keepdims=True)
    total = jnp.sum(product * scale_ref[:, 0:1], axis=0, keepdims=True)
    gain_grad_ref[...] = jnp.broadcast_to(total, gain_grad_ref.shape)
    part_ref[...] = terms[:rows].astype(BF)


def input_terms(tensor_place, pre_grad, small_grad, gate_grad, weight, token, scale, gain, count):
    total, wide = pre_grad.shape
    rows, gate_wide = gate_grad.shape
    features, outs = weight.shape
    width = features // count
    whole = lambda shape: pl.BlockSpec(shape, lambda i, at: (0,) * len(shape))
    spot = lambda i, at: lax.rem(at[0] + i, count)
    found = pl.pallas_call(
        input_kernel,
        grid_spec=pltpu.PrefetchScalarGridSpec(
            num_scalar_prefetch=1,
            grid=(count,),
            in_specs=[
                whole(pre_grad.shape),
                whole(small_grad.shape),
                whole(gate_grad.shape),
                pl.BlockSpec((width, outs), lambda i, at: (spot(i, at), 0)),
                pl.BlockSpec((total, width), lambda i, at: (0, spot(i, at))),
                whole(scale.shape),
                pl.BlockSpec((1, width), lambda i, at: (0, spot(i, at))),
            ],
            out_specs=[
                whole((total, LANES)),
                pl.BlockSpec((8, width), lambda i, at: (0, spot(i, at))),
                pl.BlockSpec((RIM, width), lambda i, at: (0, spot(i, at))),
                pl.BlockSpec((rows, width), lambda i, at: (0, spot(i, at))),
            ],
            scratch_shapes=[pltpu.VMEM((total, width), F32)],
        ),
        out_shape=[
            jax.ShapeDtypeStruct((total, LANES), F32),
            jax.ShapeDtypeStruct((8, features), F32),
            jax.ShapeDtypeStruct((RIM, features), F32),
            jax.ShapeDtypeStruct((rows, features), BF),
        ],
        compiler_params=pltpu.CompilerParams(vmem_limit_bytes=VMEM_LIMIT),
        cost_estimate=cost(8),
        name="input_terms",
    )(tensor_place, pre_grad, small_grad, gate_grad, weight, token, scale, gain)
    return found


def conv_back(unit_grad, window, taps_ref, valid, first, width, factor, taps_grad_ref):
    conv, pieces = active_of(window, taps_ref, valid, first, width)
    sig = sigmoid(conv)
    act_grad = unit_grad
    if factor is not None:
        act = conv * sig
        scale = lax.rsqrt(jnp.sum(act * act, axis=1, keepdims=True) + EPSILON)
        along = jnp.sum(unit_grad * act, axis=1, keepdims=True)
        act_grad = (factor * scale) * (unit_grad - act * (scale * scale * along))
    conv_grad = act_grad * (sig * (1.0 + conv * (1.0 - sig)))
    for j in range(CONV):
        taps_grad_ref[j : j + 1, first : first + width] += jnp.sum(
            conv_grad * valid[:, j : j + 1] * pieces[j], axis=0, keepdims=True
        )
    return conv_grad


def ready_kernel(
    pre_ref,
    small_ref,
    taps_ref,
    valid_ref,
    rate_ref,
    bias_ref,
    queries_ref,
    keys_ref,
    w_ref,
    u_ref,
    states_ref,
    enter_ref,
    mixed_grad_ref,
    true_ref,
    whole_ref,
    renewed_ref,
    base_ref,
    key_part_ref,
    conv_grad_ref,
    taps_grad_ref,
    along_ref,
    *,
    heads,
    rows,
    key_width,
    value_width,
):
    groups = rows // PACK
    inner = PACK // GROUP
    taps_grad_ref[...] = jnp.zeros_like(taps_grad_ref)
    def ready(group, _):
        masks = pack_masks()
        row, col, apart, same, lower, strict = masks
        span = pl.ds(pl.multiple_of(group * PACK, PACK), PACK)
        valid = valid_ref[pl.ds(pl.multiple_of(group * PACK + RIM, RIM), PACK), :]
        decay_tile, _ = rates_of(small_ref[span, :], rate_ref[...], bias_ref[...])
        lane = lax.broadcasted_iota(jnp.int32, (PACK, LANES), 1)
        along = jnp.zeros((PACK, LANES), F32)
        for head in range(heads):
            cols = slice(head * key_width, (head + 1) * key_width)
            value_at = slice(head * value_width, (head + 1) * value_width)
            query = queries_ref[span, cols]
            key = keys_ref[span, cols]
            gam, last, fading = packed_decay(column_of(decay_tile, head), masks)
            whole = jnp.exp(last)
            scores = mm_nt(query, key) * fading
            w = w_ref[span, cols]
            u = u_ref[span, value_at]
            out_grad = mixed_grad_ref[span, value_at]
            renewed, grown_grad = [], []
            for b in range(inner):
                index = (group * inner + b) * heads + head
                part = slice(b * GROUP, (b + 1) * GROUP)
                whole_ref[index] = jnp.broadcast_to(whole[b * GROUP : b * GROUP + 1], (8, LANES))
                state = (
                    states_ref[index, :, :value_width].astype(F32)
                    + mm(states_ref[index, :, value_width:], enter_ref[head])
                ).astype(BF)
                true_ref[index] = state
                renewed.append(u[part].astype(F32) - mm(w[part], state))
                grown_grad.append(mm_nt(out_grad[part], state))
            renewed = jnp.concatenate(renewed, axis=0).astype(BF)
            renewed_ref[span, value_at] = renewed
            base_ref[span, value_at] = mm_tn(scores, out_grad)
            scores_grad = jnp.where(lower, mm_nt(out_grad, renewed), 0.0)
            pair_grad = (scores_grad * fading).astype(BF)
            grown_grad = jnp.exp(gam) * jnp.concatenate(grown_grad, axis=0)
            query_grad = mm(pair_grad, key) + grown_grad
            along = jnp.where(
                lane == head,
                net_of(scores_grad * scores, apart)
                + jnp.sum(grown_grad * query.astype(F32), axis=1, keepdims=True),
                along,
            )
            key_part_ref[span, cols] = mm_tn(pair_grad, query)
            window = load_window(pre_ref, group, head * key_width, key_width, rows)
            conv_grad_ref[span, cols] = conv_back(
                query_grad,
                window,
                taps_ref,
                valid,
                head * key_width,
                key_width,
                key_width ** (-0.5),
                taps_grad_ref,
            )
        along_ref[span, :] = along
        return 0

    lax.fori_loop(0, groups, ready, 0)


def mixer_ready(
    pre,
    taps,
    valid,
    rate,
    bias,
    queries,
    keys,
    w,
    u,
    states,
    enter,
    mixed_grad,
    heads,
    key_width,
    value_width,
):
    rows = pre.shape[0] - RIM
    wide = heads * (2 * key_width + value_width)
    gate_wide = heads * value_width
    count = rows // GROUP
    key_cols = heads * key_width
    whole = lambda shape: pl.BlockSpec(shape, lambda i: (0,) * len(shape))
    outs = [
        ((count * heads, key_width, value_width), BF),
        ((count * heads, 8, LANES), F32),
        ((rows, heads * value_width), BF),
        ((rows, heads * value_width), F32),
        ((rows, key_cols), F32),
        ((rows, key_cols), F32),
        ((8, key_cols), F32),
        ((rows, LANES), F32),
    ]
    return pl.pallas_call(
        functools.partial(
            ready_kernel, heads=heads, rows=rows, key_width=key_width, value_width=value_width
        ),
        grid=(1,),
        in_specs=[
            pl.BlockSpec((rows + RIM, key_cols), lambda i: (0, 0)),
            pl.BlockSpec((rows + RIM, LANES), lambda i: (0, (wide + gate_wide) // LANES)),
            whole(taps.shape),
            whole(valid.shape),
            whole(rate.shape),
            whole(bias.shape),
            whole(queries.shape),
            pl.BlockSpec((rows, key_cols), lambda i: (0, 0)),
            whole(w.shape),
            whole(u.shape),
            whole(states.shape),
            whole(enter.shape),
            whole(mixed_grad.shape),
        ],
        out_specs=[whole(shape) for shape, _ in outs],
        out_shape=[jax.ShapeDtypeStruct(shape, kind) for shape, kind in outs],
        compiler_params=pltpu.CompilerParams(vmem_limit_bytes=VMEM_LIMIT),
        cost_estimate=cost(14),
        name="mixer_ready",
    )(
        pre,
        pre,
        taps,
        valid,
        rate,
        bias,
        queries,
        keys,
        w,
        u,
        states,
        enter,
        mixed_grad,
    )


def backward_kernel(
    keep_ref,
    pre_ref,
    small_ref,
    taps_ref,
    valid_ref,
    rate_ref,
    bias_ref,
    keys_ref,
    inverse_ref,
    w_ref,
    u_ref,
    fold_ref,
    source_ref,
    true_ref,
    whole_ref,
    renewed_ref,
    base_ref,
    key_part_ref,
    query_conv_ref,
    query_taps_ref,
    along_ref,
    next1_ref,
    next2_ref,
    next3_ref,
    next4_ref,
    pre_grad_ref,
    small_grad_ref,
    taps_grad_ref,
    rate_grad_ref,
    later_ref,
    conv_grad_ref,
    flow_ref,
    *,
    heads,
    rows,
    key_width,
    value_width,
):
    groups = rows // PACK
    inner = PACK // GROUP
    key_cols = heads * key_width
    wide = heads * (2 * key_width + value_width)
    taps_grad_ref[...] = jnp.zeros_like(taps_grad_ref)
    taps_grad_ref[:, :key_cols] = query_taps_ref[...]
    rate_grad_ref[...] = jnp.zeros_like(rate_grad_ref)
    conv_grad_ref[0:RIM, :] = jnp.zeros((RIM, wide), F32)
    conv_grad_ref[RIM + rows :, :] = jnp.zeros((RIM, wide), F32)
    conv_grad_ref[RIM : RIM + rows, :key_cols] = query_conv_ref[...]
    small_grad_ref[rows:, :] = jnp.zeros((RIM, LANES), BF)

    for head in range(heads):
        flow = next4_ref[head, :, :value_width].astype(F32)
        for near in (next3_ref, next2_ref, next1_ref):
            flow = near[head, :, :value_width].astype(F32) + mm_tn(
                near[head, :, value_width:], flow
            )
        flow_ref[head] = flow
    for block in reversed(range(rows // GROUP)):
        for head in range(heads):
            index = block * heads + head
            flow = flow_ref[head]
            flow_low = flow.astype(BF)
            later_ref[index] = flow_low
            flow_ref[head] = keep_ref[block] * (
                whole_ref[index, 0:1, 0:1] * flow
                - mm_tn(fold_ref[index], flow_low)
                + source_ref[index]
            )

    def back(group, _):
        masks = pack_masks()
        row, col, apart, same, lower, strict = masks
        span = pl.ds(pl.multiple_of(group * PACK, PACK), PACK)
        small = small_ref[span, :]
        valid = valid_ref[pl.ds(pl.multiple_of(group * PACK + RIM, RIM), PACK), :]
        decay_tile, beta_tile = rates_of(small, rate_ref[...], bias_ref[...])
        lane = lax.broadcasted_iota(jnp.int32, (PACK, LANES), 1)
        small_rows = jnp.zeros((PACK, LANES), F32)
        for head in range(heads):
            decay = column_of(decay_tile, head)
            beta = column_of(beta_tile, heads + head)
            cols = slice(head * key_width, (head + 1) * key_width)
            value_at = slice(head * value_width, (head + 1) * value_width)
            key = keys_ref[span, cols]
            value = keys_ref[span, key_cols + head * value_width : key_cols + (head + 1) * value_width]
            key_f = key.astype(F32)
            gam, last, fading = packed_decay(decay, masks)
            growth = jnp.exp(gam)
            rest = jnp.exp(last - gam)
            gram = mm_nt(key, key)
            tail = (rest * key_f).astype(BF)
            w = w_ref[span, cols]
            u = u_ref[span, value_at]
            renewed = renewed_ref[span, value_at]
            renewed_grad, drops = [], []
            for b in range(inner):
                index = (group * inner + b) * heads + head
                flow = later_ref[index]
                renewed_grad.append(mm(tail[b * GROUP : (b + 1) * GROUP], flow))
                shared = true_ref[index].astype(F32) * flow.astype(F32)
                shared = jnp.sum(jnp.sum(shared, axis=1, keepdims=True), axis=0, keepdims=True)
                drops.append(
                    jnp.broadcast_to(shared * whole_ref[index, 0:1, 0:1], (GROUP, 1))
                )
            renewed_low = (base_ref[span, value_at] + jnp.concatenate(renewed_grad, axis=0)).astype(
                BF
            )
            tail_grad, w_grad = [], []
            for b in range(inner):
                index = (group * inner + b) * heads + head
                part = slice(b * GROUP, (b + 1) * GROUP)
                tail_grad.append(mm_nt(renewed[part], later_ref[index]))
                w_grad.append(mm_nt(renewed_low[part], true_ref[index]))
            tail_grad = jnp.concatenate(tail_grad, axis=0)
            w_grad = -jnp.concatenate(w_grad, axis=0)
            inverse = inverse_ref[group * heads + head]
            keys_grad = mm_tn(inverse, w_grad)
            values_grad = mm_tn(inverse, renewed_low)
            system_grad = jnp.where(strict, -(mm_nt(keys_grad, w) + mm_nt(values_grad, u)), 0.0)
            gram_beta = system_grad * fading
            gram_grad = (gram_beta * beta).astype(BF)
            key_grad = (
                mm(gram_grad, key)
                + mm_tn(gram_grad, key)
                + key_part_ref[span, cols]
                + beta * growth * keys_grad
                + rest * tail_grad
            )
            value_grad = beta * values_grad
            keys_dot = growth * jnp.sum(keys_grad * key_f, axis=1, keepdims=True)
            beta_grad = (
                keys_dot
                + jnp.sum(values_grad * value.astype(F32), axis=1, keepdims=True)
                + jnp.sum(gram_beta * gram, axis=1, keepdims=True)
            )
            tail_dot = rest * jnp.sum(tail_grad * key_f, axis=1, keepdims=True)
            system = jnp.where(strict, fading * beta * gram, 0.0)
            gam_grad = (
                along_ref[span, head : head + 1]
                + beta * keys_dot
                + net_of(system_grad * system, apart)
            )
            gam_grad_row = jnp.sum(
                jnp.where(apart == 0, jnp.broadcast_to(gam_grad, (PACK, PACK)), 0.0),
                axis=0,
                keepdims=True,
            )
            tail_row = jnp.sum(
                jnp.where(apart == 0, jnp.broadcast_to(tail_dot, (PACK, PACK)), 0.0),
                axis=0,
                keepdims=True,
            )
            decay_grad = jnp.sum(
                jnp.where(same, jnp.where(col >= row, gam_grad_row, tail_row), 0.0),
                axis=1,
                keepdims=True,
            ) + jnp.concatenate(drops, axis=0)
            small_rows = jnp.where(lane == head, decay_grad, small_rows)
            small_rows = jnp.where(lane == heads + head, beta_grad, small_rows)

            for first, width, unit_grad, factor in (
                (key_cols + head * key_width, key_width, key_grad, 1.0),
                (2 * key_cols + head * value_width, value_width, value_grad, None),
            ):
                window = load_window(pre_ref, group, first, width, rows)
                conv_grad_ref[
                    pl.ds(pl.multiple_of(group * PACK + RIM, RIM), PACK), first : first + width
                ] = conv_back(
                    unit_grad, window, taps_ref, valid, first, width, factor, taps_grad_ref
                )

        raw = small + bias_ref[...]
        slope = -jnp.exp(rate_ref[...]) * sigmoid(raw)
        small_grad = jnp.where(
            lane < heads, small_rows * slope, small_rows * beta_tile * (1.0 - beta_tile)
        )
        small_grad = jnp.where(lane < 2 * heads, small_grad, 0.0)
        small_grad_ref[span, :] = small_grad.astype(BF)
        rate_grad_ref[0:1, :] += jnp.sum(small_rows * decay_tile, axis=0, keepdims=True)
        rate_grad_ref[1:2, :] += jnp.sum(small_grad, axis=0, keepdims=True)
        return 0

    lax.fori_loop(0, groups, back, 0)

    def convolve_back(start, target, count, first):
        cols = slice(first, first + LANES)
        window = conv_grad_ref[pl.ds(start, count + RIM), cols]
        flags = valid_ref[pl.ds(start, count + RIM), :]
        total = None
        for j in range(CONV):
            term = window * (flags[:, j : j + 1] * taps_ref[j : j + 1, cols])
            shift = CONV - 1 - j
            if shift:
                term = pltpu.roll(term, count + RIM - shift, 0)
            total = term if total is None else total + term
        pre_grad_ref[pl.ds(target, count), cols] = total[:count].astype(BF)

    def spread(group, _):
        base = pl.multiple_of(group * PACK, PACK)
        for first in range(0, wide, LANES):
            convolve_back(pl.multiple_of(base + RIM, RIM), base, PACK, first)
        return 0

    lax.fori_loop(0, groups, spread, 0)
    for first in range(0, wide, LANES):
        convolve_back(0, rows, RIM, first)


def mixer_backward(
    keep,
    pre,
    taps,
    valid,
    rate,
    bias,
    keys,
    inverse,
    w,
    u,
    fold,
    source,
    found,
    nexts,
    heads,
    key_width,
    value_width,
):
    rows = pre.shape[0] - RIM
    wide = heads * (2 * key_width + value_width)
    gate_wide = heads * value_width
    count = rows // GROUP
    whole = lambda shape: pl.BlockSpec(shape, lambda i: (0,) * len(shape))
    outs = [
        ((rows + RIM, wide), BF),
        ((rows + RIM, LANES), BF),
        ((8, wide), F32),
        ((8, LANES), F32),
    ]
    given = [taps, valid, rate, bias, keys, inverse, w, u, fold, source, *found, *nexts]
    return pl.pallas_call(
        functools.partial(
            backward_kernel, heads=heads, rows=rows, key_width=key_width, value_width=value_width
        ),
        grid=(1,),
        in_specs=[
            pl.BlockSpec(memory_space=pltpu.SMEM),
            pl.BlockSpec((rows + RIM, wide), lambda i: (0, 0)),
            pl.BlockSpec((rows + RIM, LANES), lambda i: (0, (wide + gate_wide) // LANES)),
        ]
        + [whole(array.shape) for array in given],
        out_specs=[whole(shape) for shape, _ in outs],
        out_shape=[jax.ShapeDtypeStruct(shape, kind) for shape, kind in outs],
        scratch_shapes=[
            pltpu.VMEM((count * heads, key_width, value_width), BF),
            pltpu.VMEM((rows + 2 * RIM, wide), F32),
            pltpu.VMEM((heads, key_width, value_width), F32),
        ],
        compiler_params=pltpu.CompilerParams(vmem_limit_bytes=VMEM_LIMIT),
        cost_estimate=cost(25),
        name="mixer_backward",
    )(keep, pre, pre, *given)


def spread_into(piece, whole_shape, start, axis_number):
    return lax.dynamic_update_slice_in_dim(jnp.zeros(whole_shape, F32), piece, start, axis_number)


def lane_row(values):
    return jnp.pad(values, (0, LANES - values.shape[0]))[None, :]


def per_device(
    tokens,
    cotangent,
    lengths,
    norm_gain,
    query_weight,
    key_weight,
    value_weight,
    outgate_weight,
    alpha_weight,
    beta_weight,
    output_weight,
    conv_query,
    conv_key,
    conv_value,
    log_rate,
    step_bias,
    out_gain,
    ffn_gain,
    gate_weight,
    up_weight,
    down_weight,
):
    rows, slice_width = tokens.shape
    count = lax.axis_size("tensor")
    full_width = slice_width * count
    tensor_place = lax.axis_index("tensor")
    tensor_array = tensor_place.astype(jnp.int32)[None]
    place = lax.axis_index(FH)
    key_cols = query_weight.shape[1]
    value_cols = value_weight.shape[1]
    heads = alpha_weight.shape[1]
    key_width = key_cols // heads
    value_width = value_cols // heads
    wide = 2 * key_cols + value_cols
    reach = LONGEST // rows

    rim_slice = shifted(tokens[rows - RIM :], FH, 1)
    token_pieces = rotations(jnp.concatenate([tokens, rim_slice], axis=0), "tensor")
    small_shard = jnp.pad(
        jnp.concatenate([alpha_weight, beta_weight], axis=1), ((0, 0), (0, 2 * LANES - 2 * heads))
    )
    in_full = weight_rows(
        jnp.concatenate(
            [query_weight, key_weight, value_weight, outgate_weight, small_shard], axis=1
        ),
        0,
    )
    hidden = gate_weight.shape[1]
    room = ((0, 0), (0, padded(hidden) - hidden))
    down_full = weight_rows(jnp.concatenate([output_weight, down_weight], axis=0), 1)
    feed_full = weight_rows(
        jnp.concatenate([jnp.pad(gate_weight, room), jnp.pad(up_weight, room)], axis=1), 0
    )

    starts = jnp.cumsum(lengths) - lengths
    places = place * rows + jnp.arange(rows, dtype=jnp.int32)
    latest = jnp.max(jnp.where(starts[None, :] <= places[:, None], starts[None, :], 0), axis=1)
    tap_index = jnp.arange(8, dtype=jnp.int32)
    valid = ((places - latest)[:, None] >= CONV - 1 - tap_index[None, :]).astype(F32)
    valid_padded = jnp.pad(valid, ((RIM, RIM), (0, 0)))
    block_first = place * rows + jnp.arange(rows // GROUP, dtype=jnp.int32) * GROUP
    keep = 1.0 - jnp.any(block_first[:, None] == starts[None, :], axis=1).astype(F32)
    taps = jnp.concatenate(
        [
            lax.dynamic_slice_in_dim(conv_query, tensor_place * key_cols, key_cols, 1),
            lax.dynamic_slice_in_dim(conv_key, tensor_place * key_cols, key_cols, 1),
            lax.dynamic_slice_in_dim(conv_value, tensor_place * value_cols, value_cols, 1),
        ],
        axis=1,
    )
    rate = lane_row(lax.dynamic_slice_in_dim(log_rate, tensor_place * heads, heads))
    bias = lane_row(lax.dynamic_slice_in_dim(step_bias, tensor_place * heads, heads))
    gain_row = out_gain[None, :]
    norm_row = norm_gain[None, :]
    ffn_row = ffn_gain[None, :]

    token_rows, hidden_in, scale_in, pre = project(
        tensor_array, token_pieces, norm_row, in_full
    )
    cot_held, *_ = lax.optimization_barrier((cotangent, *token_pieces[1:]))
    cot_rows = lax.all_gather(cot_held, "tensor", axis=1, tiled=True)

    keys, inverse, w, u, fold, states, end = mixer_forward(
        pre, keep, taps, valid, rate, bias, heads, key_width, value_width
    )
    queries, query_w, local, carry = mixer_query(
        pre, taps, valid, rate, bias, keys, w, u, states, heads, key_width, value_width
    )
    ends = [shifted(end, FH, by) for by in range(1, reach + 1)]
    ends[0], cot_rows = lax.optimization_barrier((ends[0], cot_rows))
    mixed, normed, enter, attn_parts = mixer_output(
        local,
        carry,
        ends,
        tensor_array,
        pre,
        gain_row,
        down_full,
        key_width,
        value_width,
        CHUNKS,
        count,
    )

    kept, mid_parts = (), []
    attn_chunks = [exchanged(parts) for parts in attn_parts]
    for chunk in range(CHUNKS):
        kept, mid = feed_forward(
            chunk,
            CHUNKS,
            tensor_array,
            attn_chunks[chunk],
            cot_rows,
            token_rows,
            ffn_row,
            feed_full,
            down_full,
            hidden,
            kept,
        )
        mid_parts.append(mid)
    middle, hidden_mid, inner_act, gate_grad, up_grad, *out_parts = kept
    back_kept, sums = (), []
    mid_chunks = [exchanged(parts) for parts in mid_parts]
    inner_held = lax.optimization_barrier((inner_act, mid_chunks[0][0]))[0]
    feed_local = weight_grads(
        (hidden_mid, gate_grad), (hidden_mid, up_grad), (cot_rows, inner_held)
    )
    feed_grads = owners(feed_local)
    mid_chunks[0][0] = lax.optimization_barrier((mid_chunks[0][0], feed_local))[0]
    for chunk in range(CHUNKS):
        back_kept, found = gate_back(
            chunk,
            CHUNKS,
            tensor_array,
            mid_chunks[chunk],
            middle,
            cot_rows,
            ffn_row,
            down_full,
            mixed,
            pre,
            gain_row,
            query_w,
            states,
            back_kept,
            key_width,
            value_width,
        )
        sums.append(found)
    attn_grad, mixed_grad, outgate_grad, source, middle_grad_own = back_kept
    ffn_gain_grad, out_gain_grad, enter_grad = [sum(group[1:], group[0]) for group in zip(*sums)]

    enter_low = jnp.concatenate([enter_grad.astype(BF), end[:, :, value_width:]], axis=2)
    nexts = [shifted(enter_low, FH, -by) for by in range(1, reach + 1)]
    attn_held, feed_grads = lax.optimization_barrier((attn_grad, feed_grads))
    out_local = weight_grads((attn_held, normed), (hidden_in, outgate_grad))
    out_grads = owners(out_local)
    mixed_held, out_held = lax.optimization_barrier((mixed_grad, out_parts, out_local))[:2]
    found = mixer_ready(
        pre,
        taps,
        valid_padded,
        rate,
        bias,
        queries,
        keys,
        w,
        u,
        states,
        enter,
        mixed_held,
        heads,
        key_width,
        value_width,
    )
    output_terms = scattered(out_held, "tensor")
    middle_own = lax.dynamic_slice_in_dim(middle, tensor_place * slice_width, slice_width, 1)
    output_rows = (middle_own + output_terms).astype(BF)
    pre_grad, small_grad, taps_grad, rate_grad = mixer_backward(
        keep,
        pre,
        taps,
        valid_padded,
        rate,
        bias,
        keys,
        inverse,
        w,
        u,
        fold,
        source,
        found,
        nexts,
        heads,
        key_width,
        value_width,
    )

    pre_grad, out_grads = lax.optimization_barrier((pre_grad, out_grads))
    in_dot, norm_gain_grad, rim_terms, in_part = input_terms(
        tensor_array, pre_grad, small_grad, outgate_grad, in_full, token_rows, scale_in, norm_row, count
    )
    in_grad = lax.psum_scatter(in_part, "tensor", scatter_dimension=1, tiled=True).astype(F32)
    late_held = lax.optimization_barrier((pre_grad, in_part))[0]
    late_grads = owners_by_steps(weight_grads((hidden_in, late_held), (hidden_in, small_grad)))
    rim = shifted(jnp.concatenate([rim_terms, in_dot[rows:]], axis=1), FH, -1)
    in_dot = in_dot[:rows, 0] + jnp.pad(rim[:, full_width], (rows - RIM, 0))
    rim_blocks = [
        lax.dynamic_slice_in_dim(
            rim, lax.rem(tensor_place + by, count) * slice_width, slice_width, 1
        ).reshape(-1)
        for by in range(count)
    ]

    own_gain_grad = lax.dynamic_slice_in_dim(
        ffn_gain_grad[0], tensor_place * slice_width, slice_width
    )
    pieces = (
        spread_into(taps_grad[:CONV, :key_cols], conv_query.shape, tensor_place * key_cols, 1),
        spread_into(
            taps_grad[:CONV, key_cols : 2 * key_cols], conv_key.shape, tensor_place * key_cols, 1
        ),
        spread_into(
            taps_grad[:CONV, 2 * key_cols :], conv_value.shape, tensor_place * value_cols, 1
        ),
        out_gain_grad[0],
        norm_gain_grad[0],
        spread_into(own_gain_grad, ffn_gain.shape, tensor_place * slice_width, 0),
        spread_into(rate_grad[0, :heads], log_rate.shape, tensor_place * heads, 0),
        spread_into(rate_grad[1, :heads], step_bias.shape, tensor_place * heads, 0),
    )
    flat = jnp.concatenate([piece.reshape(-1) for piece in pieces])
    flat = jnp.pad(flat, (0, -flat.size % (8 * LANES))).reshape(-1, LANES)
    flat = total_batches(flat).reshape(-1)
    joined = scattered(
        [jnp.concatenate([flat, in_dot, block]).reshape(-1, LANES) for block in rim_blocks], "tensor"
    ).reshape(-1)
    small, at = [], 0
    for piece in pieces:
        small.append(joined[at : at + piece.size].reshape(piece.shape))
        at += piece.size
    in_dot = joined[flat.size : flat.size + rows]
    rim_grad = joined[flat.size + rows :].reshape(RIM, slice_width)

    norm_slice = lax.dynamic_slice_in_dim(norm_gain, tensor_place * slice_width, slice_width)
    in_grad = in_grad + jnp.pad(rim_grad, ((rows - RIM, 0), (0, 0)))
    scale = scale_in[:rows, :1]
    tokens_grad = (
        middle_grad_own
        + scale * (in_grad * norm_slice)
        - tokens.astype(F32) * (scale * scale * scale * in_dot[:, None] / full_width)
    )

    return (
        output_rows,
        tokens_grad,
        late_grads[:, :key_cols],
        late_grads[:, key_cols : 2 * key_cols],
        late_grads[:, 2 * key_cols : wide],
        out_grads[:, value_cols:],
        late_grads[:, wide : wide + heads],
        late_grads[:, wide + heads : wide + 2 * heads],
        out_grads[:, :value_cols].T,
        feed_grads[:, :hidden],
        feed_grads[:, padded(hidden) : padded(hidden) + hidden],
        feed_grads[:, 2 * padded(hidden) : 2 * padded(hidden) + hidden].T,
        small[0],
        small[1],
        small[2],
        small[6],
        small[7],
        small[3],
        small[4],
        small[5],
    )


def solution(mesh):
    in_specs = (
        P(FH, "tensor"),
        P(FH, "tensor"),
        P(),
        P(),
        P("fsdp", "tensor"),
        P("fsdp", "tensor"),
        P("fsdp", "tensor"),
        P("fsdp", "tensor"),
        P("fsdp", "tensor"),
        P("fsdp", "tensor"),
        P("tensor", "fsdp"),
        P(),
        P(),
        P(),
        P(),
        P(),
        P(),
        P(),
        P("fsdp", "tensor"),
        P("fsdp", "tensor"),
        P("tensor", "fsdp"),
    )
    out_specs = (
        P(FH, "tensor"),
        P(FH, "tensor"),
        P(FH, "tensor"),
        P(FH, "tensor"),
        P(FH, "tensor"),
        P(FH, "tensor"),
        P(FH, "tensor"),
        P(FH, "tensor"),
        P("tensor", FH),
        P(FH, "tensor"),
        P(FH, "tensor"),
        P("tensor", FH),
        P(),
        P(),
        P(),
        P(),
        P(),
        P(),
        P(),
        P(),
    )
    return jax.shard_map(
        per_device, mesh=mesh, in_specs=in_specs, out_specs=out_specs, check_vma=False
    )
```

time: 836 us -> 533 us (0.64)
  waiting for transfers between devices: 547 us -> 195 us
  Pallas kernels: 81.8 us -> 177 us
  starting transfers between devices: 6.21 us -> 75.5 us
  matrix products: 66.1 us -> 0 us
  blocking collectives: 26.7 us -> 0 us
  other arithmetic: 39.8 us -> 21.8 us
    all_gather x10 -> x4, waiting for transfers between devices: 206 us -> 0.02 us  [the longest x3 0.02 us: weight_rows(): return lax.all_gather(shard, 'fsdp', axis=axis, tiled=True)]
    ppermute x0 -> x41, waiting for transfers between devices: none -> 190 us  [the longest x39 190 us: rotated(): lax.ppermute(shard, axis, [(i, (i + by) % devices) for i in range(devices)])]
    reduce_scatter x4 -> x3, waiting for transfers between devices: 139 us -> 0.01 us  [the longest x2 0.01 us: owners(): lax.psum_scatter(grad, FH, scatter_dimension=0, tiled=True).astype(F32)]
    psum x1 -> x0, waiting for transfers between devices: 116 us -> none  [per_device(): lax.psum(jnp.concatenate([piece.reshape(-1) for piece in pieces]), ALL)]
    pallas_call x1 -> x11, Pallas kernels: 8.94 us -> 111 us  [the longest x3 24.4 us: weight_grads(): pl.pallas_call(functools.partial(weight_kernel, rows=[right.shape[0] for...]
    unnamed x21 -> x7, waiting for transfers between devices: 82.1 us -> 0.12 us
    dot_general x17 -> x0, matrix products: 66.1 us -> none  [the longest x6 25.8 us: transposed_right(): lax.dot_general(left, right, (((1,), (1,)), ((), ())), preferred_element_...]
    ppermute x0 -> x41, starting transfers between devices: none -> 54.7 us  [the longest x39 51.1 us: rotated(): lax.ppermute(shard, axis, [(i, (i + by) % devices) for i in range(devices)])]
  transfers between devices with their start and end apart: 20 -> 58, of which waited for: 16 -> 30; matrix products, arithmetic and copies ran while one was open for 14% -> 9% of each run, Pallas kernels for 8% -> 30%
where the time goes in v2:
time: 533 us; the launch traced here: 523 us
  waiting for transfers between devices  195 us (37%)
  Pallas kernels  177 us (33%)
  starting transfers between devices  75.5 us (14%)
  local copies, waits for them, and re-layouts  38.1 us (7%)
  other arithmetic  21.8 us (4%)
  between operations  15.6 us (3%)
    ppermute x39, waiting for transfers between devices, rotated(): lax.ppermute(shard, axis, [(i, (i + by) % devices) for i in range(devices)])  190 us
    ppermute x39, starting transfers between devices, rotated(): lax.ppermute(shard, axis, [(i, (i + by) % devices) for i in range(devices)])  51.1 us
    pallas_call x1, Pallas kernels, mixer_backward(): pl.pallas_call(functools.partial(backward_kernel, heads=heads, rows=rows,...  33.4 us
    pallas_call x3, Pallas kernels, weight_grads(): pl.pallas_call(functools.partial(weight_kernel, rows=[right.shape[0] for...  24.4 us
    pallas_call x2, Pallas kernels, feed_forward(): pl.pallas_call(functools.partial(feed_kernel, count=count, aliased=len(be...  23.2 us
    pallas_call x1, Pallas kernels, mixer_forward(): pl.pallas_call(functools.partial(forward_kernel, heads=heads, rows=rows,...  22.1 us
    ppermute x10, starting transfers between devices, shifted(): return lax.ppermute(shard, axis, pairs)  20.4 us
    unnamed x131, local copies, waits for them, and re-layouts  16.1 us
  transfers between devices with their start and end apart: 58, of which 30 were waited for; matrix products, arithmetic and copies ran while one was open for 9% of the time, Pallas kernels for 30%

profile of v2, /device:TPU:8, one launch (start us, length us, event | category | flops | bytes accessed | tf_op | source)
XLA Modules:
  0.0 523.3 jit_solution(11903149713243200781)
XLA Ops:
  12.7 3.5 collective-permute-start
  22.2 10.3 %collective-permute-done.1.refs_1_ = bf16[1040,256]{1,0:T(8,128)(2,1)S(1)} collective-permute-done((bf16[1040,256]{1,0:T(8,128)(2,1)S(1)}, bf16[1040,256]{1,0:T(8,128)(2,1)S(1)}, u32[]{:S(2)}, u32[]{:S(2)}) %collective-permute-start.1) | collective-permute-done | bytes 532512 | tf_op jit(solution)/shard_map/ppermute | solution.py:384
  32.5 33.3 %collective-permute-done.2.refs_2_ = bf16[1040,256]{1,0:T(8,128)(2,1)S(1)} collective-permute-done((bf16[1040,256]{1,0:T(8,128)(2,1)S(1)}, bf16[1040,256]{1,0:T(8,128)(2,1)S(1)}, u32[]{:S(2)}, u32[]{:S(2)}) %collective-permute-start.2) | collective-permute-done | bytes 532512 | tf_op jit(solution)/shard_map/ppermute | solution.py:384
  75.7 12.1 %project.1 = (bf16[1040,1024]{1,0:T(8,128)(2,1)}, bf16[1040,1024]{1,0:T(8,128)(2,1)}, f32[1040,128]{1,0:T(8,128)}, f32[1040,1792]{1,0:T(8,128)}) custom-call(s32[1]{0:T(128)} %bitcast.place_ref, bf16[1040,256]{1,0:T(8,128)(2,1)} %copy-done.15, bf16[1040,256]{1,0:T(8,128)(2,1)} %copy-done.30, bf16[1040,256]{1,0:T(8,128)(2,1)} %copy-done.31, ...), custom_call_target="tpu_custom_call" | custom-call | flops 8000000000 | bytes 24000000 | tf_op jit(solution)/shard_map/project/pallas_call | solution.py:523
  87.7 22.1 %mixer_forward.1 = (bf16[1024,768]{1,0:T(8,128)(2,1)}, bf16[8,256,256]{2,1,0:T(8,128)(2,1)}, bf16[1024,256]{1,0:T(8,128)(2,1)}, bf16[1024,512]{1,0:T(8,128)(2,1)...) custom-call(f32[16]{0:T(128)} %convert_subtract_fusion.keep_ref, ...), custom_call_target="tpu_custom_call" | custom-call | flops 20000000000 | bytes 60000000 | tf_op jit(solution)/shard_map/mixer_forward/pallas_call | solution.py:261
  111.8 3.4 collective-permute-start.5
  115.3 3.6 collective-permute-start.6
  120.4 11.8 %mixer_query.1 = (bf16[1024,256]{1,0:T(8,128)(2,1)}, bf16[32,64,128]{2,1,0:T(8,128)(2,1)}, f32[1024,512]{1,0:T(8,128)}, bf16[1024,256]{1,0:T(8,128)(2,1)}) custom-call(f32[1040,1792]{1,0:T(8,128)} %get-tuple-element.119.pre_ref.small_ref.gate_ref.refs_9_, f32[1040,1792]{1,0:T(8,128)} %get-tuple-element.119.pre_ref.small_ref.gate_ref.refs_9_, ...), custom_call_target="tpu_custom_call" | custom-call | flops 10000000000 | bytes 30000000 | tf_op jit(solution)/shard_map/mixer_query/pallas_call | solution.py:357
  133.0 10.4 %mixer_output.1 = (bf16[1024,512]{1,0:T(8,128)(2,1)}, bf16[1024,512]{1,0:T(8,128)(2,1)}, bf16[2,128,256]{2,1,0:T(8,128)(2,1)}, bf16[512,256]{1,0:T(8,128)(2,1)},...) custom-call(s32[1]{0:T(128)} %bitcast.place_ref, ...), custom_call_target="tpu_custom_call" | custom-call | flops 7000000000 | bytes 21000000 | tf_op jit(solution)/shard_map/mixer_output/pallas_call | solution.py:621
  149.3 16.2 %collective-permute-done.14 = bf16[512,256]{1,0:T(8,128)(2,1)S(1)} collective-permute-done((bf16[512,256]{1,0:T(8,128)(2,1)}, bf16[512,256]{1,0:T(8,128)(2,1)S(1)}, u32[]{:S(2)}, u32[]{:S(2)}) %collective-permute-start.14) | collective-permute-done | bytes 262176 | tf_op jit(solution)/shard_map/ppermute | solution.py:384
  165.5 11.2 %collective-permute-done.15 = bf16[512,256]{1,0:T(8,128)(2,1)S(1)} collective-permute-done((bf16[512,256]{1,0:T(8,128)(2,1)}, bf16[512,256]{1,0:T(8,128)(2,1)S(1)}, u32[]{:S(2)}, u32[]{:S(2)}) %collective-permute-start.15) | collective-permute-done | bytes 262176 | tf_op jit(solution)/shard_map/ppermute | solution.py:384
  177.9 3.8 collective-permute-start.18
  181.8 12.0 %collective-permute-done.10 = bf16[512,256]{1,0:T(8,128)(2,1)S(1)} collective-permute-done((bf16[512,256]{1,0:T(8,128)(2,1)}, bf16[512,256]{1,0:T(8,128)(2,1)S(1)}, u32[]{:S(2)}, u32[]{:S(2)}) %collective-permute-start.10) | collective-permute-done | bytes 262176 | tf_op jit(solution)/shard_map/ppermute | solution.py:384
  195.6 5.6 %collective-permute-done.9 = bf16[512,256]{1,0:T(8,128)(2,1)S(1)} collective-permute-done((bf16[512,256]{1,0:T(8,128)(2,1)}, bf16[512,256]{1,0:T(8,128)(2,1)S(1)}, u32[]{:S(2)}, u32[]{:S(2)}) %collective-permute-start.9) | collective-permute-done | bytes 262176 | tf_op jit(solution)/shard_map/ppermute | solution.py:384
  202.4 3.4 collective-permute-start.12
  205.8 2.7 collective-permute-done.17.refs_1_
  208.5 15.0 %collective-permute-done.18.refs_2_ = bf16[512,256]{1,0:T(8,128)(2,1)S(1)} collective-permute-done((bf16[512,256]{1,0:T(8,128)(2,1)S(1)}, bf16[512,256]{1,0:T(8,128)(2,1)S(1)}, u32[]{:S(2)}, u32[]{:S(2)}) %collective-permute-start.18) | collective-permute-done | bytes 262176 | tf_op jit(solution)/shard_map/ppermute | solution.py:384
  224.3 11.6 %feed_forward.2 = (f32[1024,1024]{1,0:T(8,128)}, bf16[1024,1024]{1,0:T(8,128)(2,1)}, bf16[1024,704]{1,0:T(8,128)(2,1)}, bf16[1024,704]{1,0:T(8,128)(2,1)}, bf16[...) custom-call(s32[1]{0:T(128)} %bitcast.place_ref, ...), custom_call_target="tpu_custom_call" | custom-call | flops 10000000000 | bytes 30000000 | tf_op jit(solution)/shard_map/feed_forward/pallas_call | solution.py:716
  236.0 3.4 collective-permute-start.27
  242.2 11.6 %feed_forward.3 = (f32[1024,1024]{1,0:T(8,128)}, bf16[1024,1024]{1,0:T(8,128)(2,1)}, bf16[1024,704]{1,0:T(8,128)(2,1)}, bf16[1024,704]{1,0:T(8,128)(2,1)}, bf16[...) custom-call(s32[1]{0:T(128)} %bitcast.place_ref, ...), custom_call_target="tpu_custom_call", output_to_operand_aliasing={{0}: (11, {}), {1}: (12, {}), {2}: (13, {}), {3}: (14, {}),... | custom-call | flops 10000000000 | bytes 30000000 | tf_op jit(solution)/shard_map/feed_forward/pallas_call | solution.py:716
  254.3 3.1 collective-permute-done.27
  257.8 10.4 %weight_grads.3 = bf16[1024,2304]{1,0:T(8,128)(2,1)} custom-call(bf16[1024,1024]{1,0:T(8,128)(2,1)} %get-tuple-element.159.refs_0_.refs_2_, bf16[1024,704]{1,0:T(8,128)(2,1)} %get-tuple-element.160.refs_1_, bf16[1024,1024]{1,0:T(8,128)(2,1)} %get-tuple-element.159.refs_0_.refs_2_, bf16[1024,704]{1,0:T(8,128)(2,1)} %get-tuple-element.161.refs_3_, ...), custom_call_target="tpu_custom_call" | custom-call | flops 5000000000 | bytes 15000000 | tf_op jit(solution)/shard_map/weight_grads/pallas_call | solution.py:466
  269.3 3.0 collective-permute-start.21
  274.3 2.3 collective-permute-start.30
  278.4 2.7 collective-permute-start.31
  284.2 9.8 %collective-permute-done.21 = bf16[512,256]{1,0:T(8,128)(2,1)S(1)} collective-permute-done((bf16[512,256]{1,0:T(8,128)(2,1)S(1)}, bf16[512,256]{1,0:T(8,128)(2,1)S(1)}, u32[]{:S(2)}, u32[]{:S(2)}) %collective-permute-start.21) | collective-permute-done | bytes 262176 | tf_op jit(solution)/shard_map/ppermute | solution.py:384
  294.0 16.0 %collective-permute-done.22 = bf16[512,256]{1,0:T(8,128)(2,1)S(1)} collective-permute-done((bf16[512,256]{1,0:T(8,128)(2,1)S(1)}, bf16[512,256]{1,0:T(8,128)(2,1)S(1)}, u32[]{:S(2)}, u32[]{:S(2)}) %collective-permute-start.22) | collective-permute-done | bytes 262176 | tf_op jit(solution)/shard_map/ppermute | solution.py:384
  312.3 14.1 %collective-permute-done.30.refs_2_ = bf16[512,256]{1,0:T(8,128)(2,1)S(1)} collective-permute-done((bf16[512,256]{1,0:T(8,128)(2,1)S(1)}, bf16[512,256]{1,0:T(8,128)(2,1)S(1)}, u32[]{:S(2)}, u32[]{:S(2)}) %collective-permute-start.30) | collective-permute-done | bytes 262176 | tf_op jit(solution)/shard_map/ppermute | solution.py:384
  327.6 7.5 %gate_back.2 = (bf16[1024,1024]{1,0:T(8,128)(2,1)}, bf16[1024,512]{1,0:T(8,128)(2,1)}, bf16[1024,512]{1,0:T(8,128)(2,1)}, f32[32,128,256]{2,1,0:T(8,128)}, f32[1...) custom-call(s32[1]{0:T(128)} %bitcast.place_ref, bf16[512,256]{1,0:T(8,128)(2,1)} %copy-done.20, ...), custom_call_target="tpu_custom_call" | custom-call | flops 7000000000 | bytes 21000000 | tf_op jit(solution)/shard_map/gate_back/pallas_call | solution.py:853
  338.7 7.4 %gate_back.3 = (bf16[1024,1024]{1,0:T(8,128)(2,1)}, bf16[1024,512]{1,0:T(8,128)(2,1)}, bf16[1024,512]{1,0:T(8,128)(2,1)}, f32[32,128,256]{2,1,0:T(8,128)}, f32[1...) custom-call(s32[1]{0:T(128)} %bitcast.place_ref, ...), custom_call_target="tpu_custom_call", output_to_operand_aliasing={{0}: (14, {}), {1}: (15, {}), {2}: (16, {}), {3}: (17, {}),... | custom-call | flops 7000000000 | bytes 21000000 | tf_op jit(solution)/shard_map/gate_back/pallas_call | solution.py:853
  356.0 6.4 %weight_grads.4 = bf16[1024,1024]{1,0:T(8,128)(2,1)} custom-call(bf16[1024,1024]{1,0:T(8,128)(2,1)} %get-tuple-element.176.refs_0_, bf16[1024,512]{1,0:T(8,128)(2,1)} %get-tuple-element.177.refs_1_, bf16[1040,1024]{1,0:T(8,128)(2,1)} %get-tuple-element.178.refs_2_.refs_0_, bf16[1024,512]{1,0:T(8,128)(2,1)} %get-tuple-element.179.refs_3_.gate_grad_ref), custom_call_target="tpu_custom_call" | custom-call | flops 5000000000 | bytes 15000000 | tf_op jit(solution)/shard_map/weight_grads/pallas_call | solution.py:466
  362.6 16.1 %mixer_ready.1 = (bf16[32,128,256]{2,1,0:T(8,128)(2,1)}, f32[32,8,128]{2,1,0:T(8,128)}, bf16[1024,512]{1,0:T(8,128)(2,1)}, f32[1024,512]{1,0:T(8,128)}, f32[1024...) custom-call(f32[1040,1792]{1,0:T(8,128)} %get-tuple-element.119.pre_ref.small_ref.gate_ref.refs_9_, ...), custom_call_target="tpu_custom_call" | custom-call | flops 14000000000 | bytes 42000000 | tf_op jit(solution)/shard_map/mixer_ready/pallas_call | solution.py:1134
  378.7 2.0 collective-permute-start.33
  380.7 2.2 collective-permute-start.34
  383.7 33.4 %mixer_backward.1 = (bf16[1040,1024]{1,0:T(8,128)(2,1)}, bf16[1040,128]{1,0:T(8,128)(2,1)}, f32[8,1024]{1,0:T(8,128)}, f32[8,128]{1,0:T(8,128)}) custom-call(f32[16]{0:T(128)} %convert_subtract_fusion.keep_ref, f32[1040,1792]{1,0:T(8,128)} %get-tuple-element.119.pre_ref.small_ref.gate_ref.refs_9_, ...), custom_call_target="tpu_custom_call" | custom-call | flops 24999999488 | bytes 75000000 | tf_op jit(solution)/shard_map/mixer_backward/pallas_call | solution.py:1416
  423.7 2.5 add_convert_fusion.1
  427.2 9.0 %input_terms.1 = (f32[1040,128]{1,0:T(8,128)}, f32[8,1024]{1,0:T(8,128)}, f32[16,1024]{1,0:T(8,128)}, bf16[1024,1024]{1,0:T(8,128)(2,1)}) custom-call(s32[1]{0:T(128)} %bitcast.place_ref, bf16[1040,1024]{1,0:T(8,128)(2,1)} %get-tuple-element.215.pre_grad_ref.refs_1_, bf16[1040,128]{1,0:T(8,128)(2,1)} %get-tuple-element.204.small_grad_ref.refs_3_, ...), custom_call_target="tpu_custom_call" | custom-call | flops 8000000000 | bytes 24000000 | tf_op jit(solution)/shard_map/input_terms/pallas_call | solution.py:956
  436.2 7.6 %weight_grads.5 = bf16[1024,1152]{1,0:T(8,128)(2,1)} custom-call(bf16[1040,1024]{1,0:T(8,128)(2,1)} %get-tuple-element.178.refs_2_.refs_0_, bf16[1040,1024]{1,0:T(8,128)(2,1)} %get-tuple-element.215.pre_grad_ref.refs_1_, bf16[1040,1024]{1,0:T(8,128)(2,1)} %get-tuple-element.178.refs_2_.refs_0_, bf16[1040,128]{1,0:T(8,128)(2,1)} %get-tuple-element.204.small_grad_ref.refs_3_), custom_call_target="tpu_custom_call" | custom-call | flops 5000000000 | bytes 15000000 | tf_op jit(solution)/shard_map/weight_grads/pallas_call | solution.py:466
  445.2 3.6 collective-permute-start.47
  452.9 4.0 collective-permute-done.43
  457.2 2.4 collective-permute-start.40
  465.8 2.5 collective-permute-start.45
  469.9 4.7 collective-permute-done.44
  474.6 10.9 %collective-permute-done.45 = f32[192,128]{1,0:T(8,128)} collective-permute-done((f32[192,128]{1,0:T(8,128)}, f32[192,128]{1,0:T(8,128)}, u32[]{:S(2)}, u32[]{:S(2)}) %collective-permute-start.45) | collective-permute-done | bytes 98336 | tf_op jit(solution)/shard_map/ppermute | solution.py:384
  485.5 2.6 collective-permute-done.46
  500.4 4.4 collective-permute-done.48
  504.8 4.8 collective-permute-done.49
  513.7 2.4 multiply_subtract_fusion
  (304 shorter events, 102.6 us)
Async XLA Ops:
  7.2 68.5 %all-gather.5.cloned.1.call-start = ((), (), s32[]{:S(2)}) async-start(), calls=%async_computation.3 | async-start | bytes 5505024 | tf_op jit(solution)/shard_map/all_gather | solution.py:411
  12.6 119.5 %all-gather.7.cloned.1.call-start = ((), (), s32[]{:S(2)}) async-start(), calls=%async_computation.4 | async-start | bytes 2621440 | tf_op jit(solution)/shard_map/all_gather | solution.py:1529
  17.6 14.9 %collective-permute-start.1 = (bf16[1040,256]{1,0:T(8,128)(2,1)S(1)}, bf16[1040,256]{1,0:T(8,128)(2,1)S(1)}, u32[]{:S(2)}, u32[]{:S(2)}) collective-permute-start(bf16[1040,256]{1,0:T(8,128)(2,1)S(1)} %constant_dynamic-update-slice_fusion.refs_0_), channel_id=1, source_target_pairs={{0,1},{1,2},{2,3},{3,0},{4,5},{5,6},{6,7},{7,4},{8,9},{9,10},{10,1... | collective-permute-start | bytes 1597448 | tf_op jit(solution)/shard_map/ppermute | solution.py:384
  19.2 46.6 %collective-permute-start.2 = (bf16[1040,256]{1,0:T(8,128)(2,1)S(1)}, bf16[1040,256]{1,0:T(8,128)(2,1)S(1)}, u32[]{:S(2)}, u32[]{:S(2)}) collective-permute-start(bf16[1040,256]{1,0:T(8,128)(2,1)S(1)} %constant_dynamic-update-slice_fusion.refs_0_), channel_id=1, source_target_pairs={{0,2},{1,3},{2,0},{3,1},{4,6},{5,7},{6,4},{7,5},{8,10},{9,11},{10,... | collective-permute-start | bytes 1597448 | tf_op jit(solution)/shard_map/ppermute | solution.py:384
  20.4 47.3 %collective-permute-start.3 = (bf16[1040,256]{1,0:T(8,128)(2,1)S(1)}, bf16[1040,256]{1,0:T(8,128)(2,1)}, u32[]{:S(2)}, u32[]{:S(2)}) collective-permute-start(bf16[1040,256]{1,0:T(8,128)(2,1)S(1)} %constant_dynamic-update-slice_fusion.refs_0_), channel_id=1, source_target_pairs={{0,3},{1,0},{2,1},{3,2},{4,7},{5,4},{6,5},{7,6},{8,11},{9,8},{10,9... | collective-permute-start | bytes 1597448 | tf_op jit(solution)/shard_map/ppermute | solution.py:384
  67.8 64.4 %all-gather.9.cloned.1.call-start = ((), (), s32[]{:S(2)}) async-start(), calls=%async_computation.5 | async-start | bytes 3735552 | tf_op jit(solution)/shard_map/all_gather | solution.py:411
  69.0 139.5 %all-gather.11.cloned.1.call-start = ((), (), s32[]{:S(2)}) async-start(), calls=%async_computation.6 | async-start | bytes 4718592 | tf_op jit(solution)/shard_map/all_gather | solution.py:411
  71.7 283.2 %reduce-scatter.4.cloned.1.call-start = ((), (), s32[]{:S(2)}) async-start(), calls=%async_computation.7 | async-start | bytes 5308416 | tf_op jit(solution)/shard_map/reduce_scatter | solution.py:415
  109.9 22.2 %collective-permute-start.4 = (bf16[2,128,384]{2,1,0:T(8,128)(2,1)}, bf16[2,128,384]{2,1,0:T(8,128)(2,1)S(1)}, u32[]{:S(2)}, u32[]{:S(2)}) collective-permute-start(bf16[2,128,384]{2,1,0:T(8,128)(2,1)} %get-tuple-element.126), channel_id=1, source_target_pairs={{0,4},{4,8},{8,12},{12,16},{16,20},{20,24},{24,28},{1,5},{5,9},{9,... | collective-permute-start | bytes 589832 | tf_op jit(solution)/shard_map/ppermute | solution.py:33
  111.8 20.3 %collective-permute-start.5 = (bf16[2,128,384]{2,1,0:T(8,128)(2,1)}, bf16[2,128,384]{2,1,0:T(8,128)(2,1)S(1)}, u32[]{:S(2)}, u32[]{:S(2)}) collective-permute-start(bf16[2,128,384]{2,1,0:T(8,128)(2,1)} %get-tuple-element.126), channel_id=1, source_target_pairs={{0,8},{4,12},{8,16},{12,20},{16,24},{20,28},{1,9},{5,13},{9,17},{1... | collective-permute-start | bytes 589832 | tf_op jit(solution)/shard_map/ppermute | solution.py:33
  115.3 16.9 %collective-permute-start.6 = (bf16[2,128,384]{2,1,0:T(8,128)(2,1)}, bf16[2,128,384]{2,1,0:T(8,128)(2,1)S(1)}, u32[]{:S(2)}, u32[]{:S(2)}) collective-permute-start(bf16[2,128,384]{2,1,0:T(8,128)(2,1)} %get-tuple-element.126), channel_id=1, source_target_pairs={{0,12},{4,16},{8,20},{12,24},{16,28},{1,13},{5,17},{9,21},{13,25},... | collective-permute-start | bytes 589832 | tf_op jit(solution)/shard_map/ppermute | solution.py:33
  118.9 13.3 %collective-permute-start.7 = (bf16[2,128,384]{2,1,0:T(8,128)(2,1)}, bf16[2,128,384]{2,1,0:T(8,128)(2,1)S(1)}, u32[]{:S(2)}, u32[]{:S(2)}) collective-permute-start(bf16[2,128,384]{2,1,0:T(8,128)(2,1)} %get-tuple-element.126), channel_id=1, source_target_pairs={{0,16},{4,20},{8,24},{12,28},{1,17},{5,21},{9,25},{13,29},{2,18},{... | collective-permute-start | bytes 589832 | tf_op jit(solution)/shard_map/ppermute | solution.py:33
  143.5 22.0 %collective-permute-start.14 = (bf16[512,256]{1,0:T(8,128)(2,1)}, bf16[512,256]{1,0:T(8,128)(2,1)S(1)}, u32[]{:S(2)}, u32[]{:S(2)}) collective-permute-start(bf16[512,256]{1,0:T(8,128)(2,1)} %get-tuple-element.136), channel_id=1, source_target_pairs={{0,1},{1,2},{2,3},{3,0},{4,5},{5,6},{6,7},{7,4},{8,9},{9,10},{10,1... | collective-permute-start | bytes 786440 | tf_op jit(solution)/shard_map/ppermute | solution.py:384
  143.5 33.2 %collective-permute-start.15 = (bf16[512,256]{1,0:T(8,128)(2,1)}, bf16[512,256]{1,0:T(8,128)(2,1)S(1)}, u32[]{:S(2)}, u32[]{:S(2)}) collective-permute-start(bf16[512,256]{1,0:T(8,128)(2,1)} %get-tuple-element.137), channel_id=1, source_target_pairs={{0,2},{1,3},{2,0},{3,1},{4,6},{5,7},{6,4},{7,5},{8,10},{9,11},{10,... | collective-permute-start | bytes 786440 | tf_op jit(solution)/shard_map/ppermute | solution.py:384
  145.3 31.4 %collective-permute-start.16 = (bf16[512,256]{1,0:T(8,128)(2,1)}, bf16[512,256]{1,0:T(8,128)(2,1)S(1)}, u32[]{:S(2)}, u32[]{:S(2)}) collective-permute-start(bf16[512,256]{1,0:T(8,128)(2,1)} %get-tuple-element.138), channel_id=1, source_target_pairs={{0,3},{1,0},{2,1},{3,2},{4,7},{5,4},{6,5},{7,6},{8,11},{9,8},{10,9... | collective-permute-start | bytes 786440 | tf_op jit(solution)/shard_map/ppermute | solution.py:384
  147.3 46.5 %collective-permute-start.10 = (bf16[512,256]{1,0:T(8,128)(2,1)}, bf16[512,256]{1,0:T(8,128)(2,1)S(1)}, u32[]{:S(2)}, u32[]{:S(2)}) collective-permute-start(bf16[512,256]{1,0:T(8,128)(2,1)} %get-tuple-element.132), channel_id=1, source_target_pairs={{0,3},{1,0},{2,1},{3,2},{4,7},{5,4},{6,5},{7,6},{8,11},{9,8},{10,9... | collective-permute-start | bytes 786440 | tf_op jit(solution)/shard_map/ppermute | solution.py:384
  148.0 47.6 %collective-permute-start.8 = (bf16[512,256]{1,0:T(8,128)(2,1)}, bf16[512,256]{1,0:T(8,128)(2,1)S(1)}, u32[]{:S(2)}, u32[]{:S(2)}) collective-permute-start(bf16[512,256]{1,0:T(8,128)(2,1)} %get-tuple-element.130), channel_id=1, source_target_pairs={{0,1},{1,2},{2,3},{3,0},{4,5},{5,6},{6,7},{7,4},{8,9},{9,10},{10,1... | collective-permute-start | bytes 786440 | tf_op jit(solution)/shard_map/ppermute | solution.py:384
  165.5 35.7 %collective-permute-start.9 = (bf16[512,256]{1,0:T(8,128)(2,1)}, bf16[512,256]{1,0:T(8,128)(2,1)S(1)}, u32[]{:S(2)}, u32[]{:S(2)}) collective-permute-start(bf16[512,256]{1,0:T(8,128)(2,1)} %get-tuple-element.131), channel_id=1, source_target_pairs={{0,2},{1,3},{2,0},{3,1},{4,6},{5,7},{6,4},{7,5},{8,10},{9,11},{10,... | collective-permute-start | bytes 786440 | tf_op jit(solution)/shard_map/ppermute | solution.py:384
  177.9 30.7 %collective-permute-start.17 = (bf16[512,256]{1,0:T(8,128)(2,1)S(1)}, bf16[512,256]{1,0:T(8,128)(2,1)S(1)}, u32[]{:S(2)}, u32[]{:S(2)}) collective-permute-start(bf16[512,256]{1,0:T(8,128)(2,1)S(1)} %add_convert_fusion.4.refs_0_), channel_id=1, source_target_pairs={{0,1},{1,2},{2,3},{3,0},{4,5},{5,6},{6,7},{7,4},{8,9},{9,10},{10,1... | collective-permute-start | bytes 786440 | tf_op jit(solution)/shard_map/ppermute | solution.py:384
  177.9 45.6 %collective-permute-start.18 = (bf16[512,256]{1,0:T(8,128)(2,1)S(1)}, bf16[512,256]{1,0:T(8,128)(2,1)S(1)}, u32[]{:S(2)}, u32[]{:S(2)}) collective-permute-start(bf16[512,256]{1,0:T(8,128)(2,1)S(1)} %add_convert_fusion.4.refs_0_), channel_id=1, source_target_pairs={{0,2},{1,3},{2,0},{3,1},{4,6},{5,7},{6,4},{7,5},{8,10},{9,11},{10,... | collective-permute-start | bytes 786440 | tf_op jit(solution)/shard_map/ppermute | solution.py:384
  193.8 29.8 %collective-permute-start.19 = (bf16[512,256]{1,0:T(8,128)(2,1)S(1)}, bf16[512,256]{1,0:T(8,128)(2,1)S(1)}, u32[]{:S(2)}, u32[]{:S(2)}) collective-permute-start(bf16[512,256]{1,0:T(8,128)(2,1)S(1)} %add_convert_fusion.4.refs_0_), channel_id=1, source_target_pairs={{0,3},{1,0},{2,1},{3,2},{4,7},{5,4},{6,5},{7,6},{8,11},{9,8},{10,9... | collective-permute-start | bytes 786440 | tf_op jit(solution)/shard_map/ppermute | solution.py:384
  202.3 37.1 %collective-permute-start.11 = (bf16[512,256]{1,0:T(8,128)(2,1)S(1)}, bf16[512,256]{1,0:T(8,128)(2,1)S(1)}, u32[]{:S(2)}, u32[]{:S(2)}) collective-permute-start(bf16[512,256]{1,0:T(8,128)(2,1)S(1)} %add_convert_fusion.5.refs_0_), channel_id=1, source_target_pairs={{0,1},{1,2},{2,3},{3,0},{4,5},{5,6},{6,7},{7,4},{8,9},{9,10},{10,1... | collective-permute-start | bytes 786440 | tf_op jit(solution)/shard_map/ppermute | solution.py:384
  202.4 39.0 %collective-permute-start.12 = (bf16[512,256]{1,0:T(8,128)(2,1)S(1)}, bf16[512,256]{1,0:T(8,128)(2,1)S(1)}, u32[]{:S(2)}, u32[]{:S(2)}) collective-permute-start(bf16[512,256]{1,0:T(8,128)(2,1)S(1)} %add_convert_fusion.5.refs_0_), channel_id=1, source_target_pairs={{0,2},{1,3},{2,0},{3,1},{4,6},{5,7},{6,4},{7,5},{8,10},{9,11},{10,... | collective-permute-start | bytes 786440 | tf_op jit(solution)/shard_map/ppermute | solution.py:384
  208.5 32.9 %collective-permute-start.13 = (bf16[512,256]{1,0:T(8,128)(2,1)S(1)}, bf16[512,256]{1,0:T(8,128)(2,1)S(1)}, u32[]{:S(2)}, u32[]{:S(2)}) collective-permute-start(bf16[512,256]{1,0:T(8,128)(2,1)S(1)} %add_convert_fusion.5.refs_0_), channel_id=1, source_target_pairs={{0,3},{1,0},{2,1},{3,2},{4,7},{5,4},{6,5},{7,6},{8,11},{9,8},{10,9... | collective-permute-start | bytes 786440 | tf_op jit(solution)/shard_map/ppermute | solution.py:384
  235.9 18.4 %collective-permute-start.26 = (bf16[512,256]{1,0:T(8,128)(2,1)}, bf16[512,256]{1,0:T(8,128)(2,1)S(1)}, u32[]{:S(2)}, u32[]{:S(2)}) collective-permute-start(bf16[512,256]{1,0:T(8,128)(2,1)} %get-tuple-element.156), channel_id=1, source_target_pairs={{0,1},{1,2},{2,3},{3,0},{4,5},{5,6},{6,7},{7,4},{8,9},{9,10},{10,1... | collective-permute-start | bytes 786440 | tf_op jit(solution)/shard_map/ppermute | solution.py:384
  236.0 21.4 %collective-permute-start.27 = (bf16[512,256]{1,0:T(8,128)(2,1)}, bf16[512,256]{1,0:T(8,128)(2,1)S(1)}, u32[]{:S(2)}, u32[]{:S(2)}) collective-permute-start(bf16[512,256]{1,0:T(8,128)(2,1)} %get-tuple-element.157), channel_id=1, source_target_pairs={{0,2},{1,3},{2,0},{3,1},{4,6},{5,7},{6,4},{7,5},{8,10},{9,11},{10,... | collective-permute-start | bytes 786440 | tf_op jit(solution)/shard_map/ppermute | solution.py:384
  239.4 18.3 %collective-permute-start.28 = (bf16[512,256]{1,0:T(8,128)(2,1)}, bf16[512,256]{1,0:T(8,128)(2,1)S(1)}, u32[]{:S(2)}, u32[]{:S(2)}) collective-permute-start(bf16[512,256]{1,0:T(8,128)(2,1)} %get-tuple-element.158), channel_id=1, source_target_pairs={{0,3},{1,0},{2,1},{3,2},{4,7},{5,4},{6,5},{7,6},{8,11},{9,8},{10,9... | collective-permute-start | bytes 786440 | tf_op jit(solution)/shard_map/ppermute | solution.py:384
  268.3 157.9 %reduce-scatter.6.cloned.1.call-start = ((), (), s32[]{:S(2)}) async-start(), calls=%async_computation.8 | async-start | bytes 2359296 | tf_op jit(solution)/shard_map/reduce_scatter | solution.py:415
  269.3 24.7 %collective-permute-start.21 = (bf16[512,256]{1,0:T(8,128)(2,1)S(1)}, bf16[512,256]{1,0:T(8,128)(2,1)S(1)}, u32[]{:S(2)}, u32[]{:S(2)}) collective-permute-start(bf16[512,256]{1,0:T(8,128)(2,1)S(1)} %copy-done.33), channel_id=1, source_target_pairs={{0,2},{1,3},{2,0},{3,1},{4,6},{5,7},{6,4},{7,5},{8,10},{9,11},{10,... | collective-permute-start | bytes 786440 | tf_op jit(solution)/shard_map/ppermute | solution.py:384
  272.2 37.8 %collective-permute-start.22 = (bf16[512,256]{1,0:T(8,128)(2,1)S(1)}, bf16[512,256]{1,0:T(8,128)(2,1)S(1)}, u32[]{:S(2)}, u32[]{:S(2)}) collective-permute-start(bf16[512,256]{1,0:T(8,128)(2,1)S(1)} %copy-done.32), channel_id=1, source_target_pairs={{0,3},{1,0},{2,1},{3,2},{4,7},{5,4},{6,5},{7,6},{8,11},{9,8},{10,9... | collective-permute-start | bytes 786440 | tf_op jit(solution)/shard_map/ppermute | solution.py:384
  274.2 36.1 %collective-permute-start.29 = (bf16[512,256]{1,0:T(8,128)(2,1)S(1)}, bf16[512,256]{1,0:T(8,128)(2,1)S(1)}, u32[]{:S(2)}, u32[]{:S(2)}) collective-permute-start(bf16[512,256]{1,0:T(8,128)(2,1)S(1)} %add_convert_fusion.2.refs_0_), channel_id=1, source_target_pairs={{0,1},{1,2},{2,3},{3,0},{4,5},{5,6},{6,7},{7,4},{8,9},{9,10},{10,1... | collective-permute-start | bytes 786440 | tf_op jit(solution)/shard_map/ppermute | solution.py:384
  274.3 52.2 %collective-permute-start.30 = (bf16[512,256]{1,0:T(8,128)(2,1)S(1)}, bf16[512,256]{1,0:T(8,128)(2,1)S(1)}, u32[]{:S(2)}, u32[]{:S(2)}) collective-permute-start(bf16[512,256]{1,0:T(8,128)(2,1)S(1)} %add_convert_fusion.2.refs_0_), channel_id=1, source_target_pairs={{0,2},{1,3},{2,0},{3,1},{4,6},{5,7},{6,4},{7,5},{8,10},{9,11},{10,... | collective-permute-start | bytes 786440 | tf_op jit(solution)/shard_map/ppermute | solution.py:384
  278.4 48.4 %collective-permute-start.31 = (bf16[512,256]{1,0:T(8,128)(2,1)S(1)}, bf16[512,256]{1,0:T(8,128)(2,1)S(1)}, u32[]{:S(2)}, u32[]{:S(2)}) collective-permute-start(bf16[512,256]{1,0:T(8,128)(2,1)S(1)} %add_convert_fusion.2.refs_0_), channel_id=1, source_target_pairs={{0,3},{1,0},{2,1},{3,2},{4,7},{5,4},{6,5},{7,6},{8,11},{9,8},{10,9... | collective-permute-start | bytes 786440 | tf_op jit(solution)/shard_map/ppermute | solution.py:384
  310.2 24.9 %collective-permute-start.23 = (bf16[512,256]{1,0:T(8,128)(2,1)S(1)}, bf16[512,256]{1,0:T(8,128)(2,1)S(1)}, u32[]{:S(2)}, u32[]{:S(2)}) collective-permute-start(bf16[512,256]{1,0:T(8,128)(2,1)S(1)} %add_convert_fusion.3.refs_0_), channel_id=1, source_target_pairs={{0,1},{1,2},{2,3},{3,0},{4,5},{5,6},{6,7},{7,4},{8,9},{9,10},{10,1... | collective-permute-start | bytes 786440 | tf_op jit(solution)/shard_map/ppermute | solution.py:384
  310.2 26.3 %collective-permute-start.24 = (bf16[512,256]{1,0:T(8,128)(2,1)S(1)}, bf16[512,256]{1,0:T(8,128)(2,1)S(1)}, u32[]{:S(2)}, u32[]{:S(2)}) collective-permute-start(bf16[512,256]{1,0:T(8,128)(2,1)S(1)} %add_convert_fusion.3.refs_0_), channel_id=1, source_target_pairs={{0,2},{1,3},{2,0},{3,1},{4,6},{5,7},{6,4},{7,5},{8,10},{9,11},{10,... | collective-permute-start | bytes 786440 | tf_op jit(solution)/shard_map/ppermute | solution.py:384
  310.3 27.7 %collective-permute-start.25 = (bf16[512,256]{1,0:T(8,128)(2,1)S(1)}, bf16[512,256]{1,0:T(8,128)(2,1)S(1)}, u32[]{:S(2)}, u32[]{:S(2)}) collective-permute-start(bf16[512,256]{1,0:T(8,128)(2,1)S(1)} %add_convert_fusion.3.refs_0_), channel_id=1, source_target_pairs={{0,3},{1,0},{2,1},{3,2},{4,7},{5,4},{6,5},{7,6},{8,11},{9,8},{10,9... | collective-permute-start | bytes 786440 | tf_op jit(solution)/shard_map/ppermute | solution.py:384
  347.2 31.5 %collective-permute-start.35 = (bf16[2,128,384]{2,1,0:T(8,128)(2,1)S(1)}, bf16[2,128,384]{2,1,0:T(8,128)(2,1)S(1)}, u32[]{:S(2)}, u32[]{:S(2)}) collective-permute-start(bf16[2,128,384]{2,1,0:T(8,128)(2,1)S(1)} %pad_maximum_fusion.1), channel_id=1, source_target_pairs={{4,0},{8,4},{12,8},{16,12},{20,16},{24,20},{28,24},{5,1},{9,5},{13... | collective-permute-start | bytes 589832 | tf_op jit(solution)/shard_map/ppermute | solution.py:33
  348.5 32.2 %collective-permute-start.36 = (bf16[2,128,384]{2,1,0:T(8,128)(2,1)S(1)}, bf16[2,128,384]{2,1,0:T(8,128)(2,1)S(1)}, u32[]{:S(2)}, u32[]{:S(2)}) collective-permute-start(bf16[2,128,384]{2,1,0:T(8,128)(2,1)S(1)} %pad_maximum_fusion.1), channel_id=1, source_target_pairs={{8,0},{12,4},{16,8},{20,12},{24,16},{28,20},{9,1},{13,5},{17,9},{2... | collective-permute-start | bytes 589832 | tf_op jit(solution)/shard_map/ppermute | solution.py:33
  349.8 33.1 %collective-permute-start.37 = (bf16[2,128,384]{2,1,0:T(8,128)(2,1)S(1)}, bf16[2,128,384]{2,1,0:T(8,128)(2,1)S(1)}, u32[]{:S(2)}, u32[]{:S(2)}) collective-permute-start(bf16[2,128,384]{2,1,0:T(8,128)(2,1)S(1)} %pad_maximum_fusion.1), channel_id=1, source_target_pairs={{12,0},{16,4},{20,8},{24,12},{28,16},{13,1},{17,5},{21,9},{25,13},... | collective-permute-start | bytes 589832 | tf_op jit(solution)/shard_map/ppermute | solution.py:33
  351.1 31.8 %collective-permute-start.38 = (bf16[2,128,384]{2,1,0:T(8,128)(2,1)S(1)}, bf16[2,128,384]{2,1,0:T(8,128)(2,1)S(1)}, u32[]{:S(2)}, u32[]{:S(2)}) collective-permute-start(bf16[2,128,384]{2,1,0:T(8,128)(2,1)S(1)} %pad_maximum_fusion.1), channel_id=1, source_target_pairs={{16,0},{20,4},{24,8},{28,12},{17,1},{21,5},{25,9},{29,13},{18,2},{... | collective-permute-start | bytes 589832 | tf_op jit(solution)/shard_map/ppermute | solution.py:33
  362.5 151.2 %reduce-scatter.8.cloned.1.call-start = ((), (), s32[]{:S(2)}) async-start(), calls=%async_computation.9 | async-start | bytes 2621440 | tf_op jit(solution)/shard_map/reduce_scatter | solution.py:1652
  362.5 61.2 %collective-permute-start.32 = (bf16[1024,256]{1,0:T(8,128)(2,1)}, bf16[1024,256]{1,0:T(8,128)(2,1)S(1)}, u32[]{:S(2)}, u32[]{:S(2)}) collective-permute-start(bf16[1024,256]{1,0:T(8,128)(2,1)} %get-tuple-element.181), channel_id=1, source_target_pairs={{0,1},{1,2},{2,3},{3,0},{4,5},{5,6},{6,7},{7,4},{8,9},{9,10},{10,1... | collective-permute-start | bytes 1572872 | tf_op jit(solution)/shard_map/ppermute | solution.py:384
  378.7 45.0 %collective-permute-start.33 = (bf16[1024,256]{1,0:T(8,128)(2,1)}, bf16[1024,256]{1,0:T(8,128)(2,1)S(1)}, u32[]{:S(2)}, u32[]{:S(2)}) collective-permute-start(bf16[1024,256]{1,0:T(8,128)(2,1)} %get-tuple-element.182), channel_id=1, source_target_pairs={{0,2},{1,3},{2,0},{3,1},{4,6},{5,7},{6,4},{7,5},{8,10},{9,11},{10,... | collective-permute-start | bytes 1572872 | tf_op jit(solution)/shard_map/ppermute | solution.py:384
  380.7 43.0 %collective-permute-start.34 = (bf16[1024,256]{1,0:T(8,128)(2,1)}, bf16[1024,256]{1,0:T(8,128)(2,1)}, u32[]{:S(2)}, u32[]{:S(2)}) collective-permute-start(bf16[1024,256]{1,0:T(8,128)(2,1)} %get-tuple-element.183), channel_id=1, source_target_pairs={{0,3},{1,0},{2,1},{3,2},{4,7},{5,4},{6,5},{7,6},{8,11},{9,8},{10,9... | collective-permute-start | bytes 1572872 | tf_op jit(solution)/shard_map/ppermute | solution.py:384
  445.2 46.0 %collective-permute-start.47 = (bf16[512,1152]{1,0:T(8,128)(2,1)S(1)}, bf16[512,1152]{1,0:T(8,128)(2,1)S(1)}, u32[]{:S(2)}, u32[]{:S(2)}) collective-permute-start(bf16[512,1152]{1,0:T(8,128)(2,1)S(1)} %constant_dynamic-slice_fusion.4), channel_id=1, source_target_pairs={{0,16},{16,0},{1,17},{17,1},{2,18},{18,2},{3,19},{19,3},{4,20},{20... | collective-permute-start | bytes 3538952 | tf_op jit(solution)/shard_map/ppermute | solution.py:407
  465.8 19.7 %collective-permute-start.45 = (f32[192,128]{1,0:T(8,128)}, f32[192,128]{1,0:T(8,128)}, u32[]{:S(2)}, u32[]{:S(2)}) collective-permute-start(f32[192,128]{1,0:T(8,128)} %get-tuple-element.341), channel_id=1, source_target_pairs={{0,2},{1,3},{2,0},{3,1},{4,6},{5,7},{6,4},{7,5},{8,10},{9,11},{10,... | collective-permute-start | bytes 294920 | tf_op jit(solution)/shard_map/ppermute | solution.py:384
  468.3 19.8 %collective-permute-start.46 = (f32[192,128]{1,0:T(8,128)S(1)}, f32[192,128]{1,0:T(8,128)}, u32[]{:S(2)}, u32[]{:S(2)}) collective-permute-start(f32[192,128]{1,0:T(8,128)S(1)} %get-tuple-element.342), channel_id=1, source_target_pairs={{0,3},{1,0},{2,1},{3,2},{4,7},{5,4},{6,5},{7,6},{8,11},{9,8},{10,9... | collective-permute-start | bytes 294920 | tf_op jit(solution)/shard_map/ppermute | solution.py:384
  495.1 14.5 %collective-permute-start.49 = (bf16[128,1152]{1,0:T(8,128)(2,1)S(1)}, bf16[128,1152]{1,0:T(8,128)(2,1)}, u32[]{:S(2)}, u32[]{:S(2)}) collective-permute-start(bf16[128,1152]{1,0:T(8,128)(2,1)S(1)} %get-tuple-element.325), channel_id=1, source_target_pairs={{0,8},{4,12},{8,0},{12,4},{1,9},{5,13},{9,1},{13,5},{2,10},{6,14},... | collective-permute-start | bytes 884744 | tf_op jit(solution)/shard_map/ppermute | solution.py:384
  (65 other events, 711.0 us)
Sparse Core Ops, SparseCore 0:
  12.7 14.3 all-gather.4
  67.9 43.5 all-gather.6
  113.1 10.9 all-gather.8
  125.4 13.3 all-gather.10
  268.4 53.5 reduce-scatter.3
  362.6 45.8 reduce-scatter.5
  436.3 53.7 reduce-scatter.7

commit v3 on v2

--- a/solution.py
+++ b/solution.py
@@ -21,6 +21,7 @@
 VMEM_LIMIT = 56 * 1024 * 1024
 INVERSE_PASSES = 1
 CHUNKS = 2
+SIDES = 2
 
 
 def cost(micros):
@@ -156,40 +157,40 @@
     inner = PACK // GROUP
     key_cols = heads * key_width
 
-    def solve(group, _):
+    def solve(step, _):
         masks = pack_masks()
         row, col, apart, same, lower, strict = masks
-        start = pl.multiple_of(group * PACK, PACK)
-        span = pl.ds(start, PACK)
-        valid = valid_ref[span, :]
-        decay_tile, beta_tile = rates_of(small_ref[span, :], rate_ref[...], bias_ref[...])
         items = []
-        for head in range(heads):
-            decay = column_of(decay_tile, head)
-            beta = column_of(beta_tile, heads + head)
-            first = key_cols + head * key_width
-            window = load_window(pre_ref, group, first, key_width, rows)
-            conv, _ = active_of(window, taps_ref, valid, first, key_width)
-            act = conv * sigmoid(conv)
-            scale = lax.rsqrt(jnp.sum(act * act, axis=1, keepdims=True) + EPSILON)
-            key = (act * scale).astype(BF)
-            keys_ref[span, head * key_width : (head + 1) * key_width] = key
-            gam, last, fading = packed_decay(decay, masks)
-            gram = mm_nt(key, key)
-            system = jnp.where(strict, fading * beta * gram, 0.0)
-            inverse = jnp.where(apart == 0, 1.0, 0.0) - jnp.where(apart == 1, system, 0.0)
-            items.append([beta, key, gam, last, system, inverse])
+        for side in range(SIDES):
+            group = step * SIDES + side
+            span = pl.ds(pl.multiple_of(group * PACK, PACK), PACK)
+            valid = valid_ref[span, :]
+            decay_tile, beta_tile = rates_of(small_ref[span, :], rate_ref[...], bias_ref[...])
+            for head in range(heads):
+                decay = column_of(decay_tile, head)
+                beta = column_of(beta_tile, heads + head)
+                first = key_cols + head * key_width
+                window = load_window(pre_ref, group, first, key_width, rows)
+                conv, _ = active_of(window, taps_ref, valid, first, key_width)
+                act = conv * sigmoid(conv)
+                scale = lax.rsqrt(jnp.sum(act * act, axis=1, keepdims=True) + EPSILON)
+                key = (act * scale).astype(BF)
+                gam, last, fading = packed_decay(decay, masks)
+                gram = mm_nt(key, key)
+                system = jnp.where(strict, fading * beta * gram, 0.0)
+                inverse = jnp.where(apart == 0, 1.0, 0.0) - jnp.where(apart == 1, system, 0.0)
+                items.append([beta, key, gam, last, system, inverse, group, span, valid, head])
         level = 1
         while (1 << level) < GROUP:
             parts = [
                 mm_fine(jnp.where((apart >> level) == 1, item[4], 0.0), item[5]) for item in items
             ]
             steps = [mm_fine(item[5], part) for item, part in zip(items, parts)]
-            for item, step in zip(items, steps):
-                item[5] = item[5] - step
+            for item, step_of in zip(items, steps):
+                item[5] = item[5] - step_of
             level += 1
-        for head in range(heads):
-            beta, key, gam, last, system, inverse = items[head]
+        for beta, key, gam, last, system, inverse, group, span, valid, head in items:
+            keys_ref[span, head * key_width : (head + 1) * key_width] = key
             cols = slice(head * value_width, (head + 1) * value_width)
             first = 2 * key_cols + head * value_width
             window = load_window(pre_ref, group, first, value_width, rows)
@@ -218,7 +219,7 @@
                 )
         return 0
 
-    lax.fori_loop(0, groups, solve, 0)
+    lax.fori_loop(0, groups // SIDES, solve, 0)
 
     unit = jnp.where(
         lax.broadcasted_iota(jnp.int32, (key_width, key_width), 0)
@@ -286,6 +287,7 @@
 
 
 def query_kernel(
+    head_ref,
     pre_ref,
     small_ref,
     taps_ref,
@@ -308,39 +310,35 @@
 ):
     inner = PACK // GROUP
 
-    def ask(group, _):
-        masks = pack_masks()
-        span = pl.ds(pl.multiple_of(group * PACK, PACK), PACK)
-        valid = valid_ref[span, :]
-        decay_tile, _ = rates_of(small_ref[span, :], rate_ref[...], bias_ref[...])
-        for head in range(heads):
-            cols = slice(head * key_width, (head + 1) * key_width)
-            value_at = slice(head * value_width, (head + 1) * value_width)
-            window = load_window(pre_ref, group, head * key_width, key_width, rows)
-            conv, _ = active_of(window, taps_ref, valid, head * key_width, key_width)
-            act = conv * sigmoid(conv)
-            scale = lax.rsqrt(jnp.sum(act * act, axis=1, keepdims=True) + EPSILON)
-            query = (act * (scale * key_width ** (-0.5))).astype(BF)
-            queries_ref[span, cols] = query
-            gam, last, fading = packed_decay(column_of(decay_tile, head), masks)
-            scores = (mm_nt(query, keys_ref[span, cols]) * fading).astype(BF)
-            query_w = (
-                jnp.exp(gam) * query.astype(F32) - mm(scores, w_ref[span, cols])
-            ).astype(BF)
-            start = mm(scores, u_ref[span, value_at])
-            local, carry = [], []
-            for b in range(inner):
-                index = (group * inner + b) * heads + head
-                part = slice(b * GROUP, (b + 1) * GROUP)
-                query_w_ref[index] = query_w[part]
-                moved = mm(query_w[part], states_ref[index])
-                local.append(moved[:, :value_width])
-                carry.append(moved[:, value_width:])
-            local_ref[span, value_at] = start + jnp.concatenate(local, axis=0)
-            carry_ref[span, cols] = jnp.concatenate(carry, axis=0).astype(BF)
-        return 0
-
-    lax.fori_loop(0, rows // PACK, ask, 0)
+    masks = pack_masks()
+    span = slice(0, PACK)
+    valid = valid_ref[span, :]
+    decay_tile, _ = rates_of(small_ref[span, :], rate_ref[...], bias_ref[...])
+    for head in range(heads):
+        cols = slice(head * key_width, (head + 1) * key_width)
+        value_at = slice(head * value_width, (head + 1) * value_width)
+        window = jnp.concatenate([head_ref[:, cols], pre_ref[:, cols]], axis=0)
+        conv, _ = active_of(window, taps_ref, valid, head * key_width, key_width)
+        act = conv * sigmoid(conv)
+        scale = lax.rsqrt(jnp.sum(act * act, axis=1, keepdims=True) + EPSILON)
+        query = (act * (scale * key_width ** (-0.5))).astype(BF)
+        queries_ref[span, cols] = query
+        gam, last, fading = packed_decay(column_of(decay_tile, head), masks)
+        scores = (mm_nt(query, keys_ref[span, cols]) * fading).astype(BF)
+        query_w = (
+            jnp.exp(gam) * query.astype(F32) - mm(scores, w_ref[span, cols])
+        ).astype(BF)
+        start = mm(scores, u_ref[span, value_at])
+        local, carry = [], []
+        for b in range(inner):
+            index = b * heads + head
+            part = slice(b * GROUP, (b + 1) * GROUP)
+            query_w_ref[index] = query_w[part]
+            moved = mm(query_w[part], states_ref[index])
+            local.append(moved[:, :value_width])
+            carry.append(moved[:, value_width:])
+        local_ref[span, value_at] = start + jnp.concatenate(local, axis=0)
+        carry_ref[span, cols] = jnp.concatenate(carry, axis=0).astype(BF)
 
 
 def mixer_query(pre, taps, valid, rate, bias, keys, w, u, states, heads, key_width, value_width):
@@ -354,29 +352,37 @@
         ((rows, heads * value_width), F32),
         ((rows, heads * key_width), BF),
     ]
+    rows_at = lambda width: pl.BlockSpec((PACK, width), lambda i: (i, 0))
+    blocks_at = lambda shape: pl.BlockSpec(
+        (PACK // GROUP * heads,) + shape, lambda i: (i, 0, 0)
+    )
+    head_at = lambda i: jnp.where(i == 0, rows // RIM, i * (PACK // RIM) - 1)
     return pl.pallas_call(
         functools.partial(
             query_kernel, heads=heads, rows=rows, key_width=key_width, value_width=value_width
         ),
-        grid=(1,),
+        grid=(rows // PACK,),
         in_specs=[
-            pl.BlockSpec((rows + RIM, heads * key_width), lambda i: (0, 0)),
-            pl.BlockSpec((rows + RIM, LANES), lambda i: (0, (wide + gate_wide) // LANES)),
+            pl.BlockSpec((RIM, heads * key_width), lambda i: (head_at(i), 0)),
+            rows_at(heads * key_width),
+            pl.BlockSpec((PACK, LANES), lambda i: (i, (wide + gate_wide) // LANES)),
             whole(taps.shape),
-            whole(valid.shape),
+            rows_at(valid.shape[1]),
             whole(rate.shape),
             whole(bias.shape),
-            pl.BlockSpec((rows, heads * key_width), lambda i: (0, 0)),
-            whole(w.shape),
-            whole(u.shape),
-            whole(states.shape),
+            rows_at(heads * key_width),
+            rows_at(w.shape[1]),
+            rows_at(u.shape[1]),
+            blocks_at(states.shape[1:]),
         ],
-        out_specs=[whole(shape) for shape, _ in outs],
+        out_specs=[
+            blocks_at(shape[1:]) if len(shape) == 3 else rows_at(shape[1]) for shape, _ in outs
+        ],
         out_shape=[jax.ShapeDtypeStruct(shape, kind) for shape, kind in outs],
         compiler_params=pltpu.CompilerParams(vmem_limit_bytes=VMEM_LIMIT),
         cost_estimate=cost(10),
         name="mixer_query",
-    )(pre, pre, taps, valid, rate, bias, keys, w, u, states)
+    )(pre, pre, pre, taps, valid, rate, bias, keys, w, u, states)
 
 
 def rotated(shard, axis, by):
@@ -385,7 +391,8 @@
 
 
 def rotations(shard, axis):
-    return [shard] + [rotated(shard, axis, by) for by in range(1, lax.axis_size(axis))]
+    moved = [rotated(shard, axis, by) for by in reversed(range(1, lax.axis_size(axis)))]
+    return [shard] + moved[::-1]
 
 
 def scattered(pieces, axis):
@@ -399,8 +406,41 @@
     return scattered([values] * lax.axis_size(axis), axis)
 
 
-def exchanged(parts):
-    return rotations(scattered(parts, "tensor").astype(BF), "tensor")
+def paired(shard, by):
+    devices = lax.axis_size("tensor")
+    return lax.ppermute(shard, "tensor", [(i, i ^ by) for i in range(devices)])
+
+
+def pair_half(kept, sent, beside=None):
+    width = kept.shape[1] // 2
+    near = paired(sent, 1)
+    if beside is not None:
+        near = lax.optimization_barrier((near, beside))[0]
+    other = (kept[:, width:].astype(F32) + near[:, width:].astype(F32)).astype(BF)
+    return kept[:, :width].astype(F32) + near[:, :width].astype(F32), other
+
+
+def pair_rest(own, other):
+    return own + paired(other, 2).astype(F32)
+
+
+def pair_gather(total):
+    far = paired(total, 2)
+    return [total, far, paired(jnp.concatenate([total, far], axis=1), 1)]
+
+
+def pair_blocks(pieces, place, whole_ref):
+    own, far, near = pieces
+    width = whole_ref.shape[1] // 4
+    for by, piece in ((0, own), (2, far), (1, near[:, :width]), (3, near[:, width:])):
+        whole_ref[:, pl.ds(pl.multiple_of((place ^ by) * width, width), width)] = piece
+
+
+def pair_parts(place, whole_width, compute, kept_ref, sent_ref):
+    width = whole_width // 4
+    for by, ref, col in ((1, sent_ref, 0), (3, sent_ref, 1), (0, kept_ref, 0), (2, kept_ref, 1)):
+        span = pl.ds(pl.multiple_of((place ^ by) * width, width), width)
+        ref[:, col * width : (col + 1) * width] = compute(span).astype(BF)
 
 
 def swapped(shard):
@@ -417,7 +457,7 @@
 
 def owners_by_steps(grad):
     if lax.axis_size("fsdp") != 2:
-        return owners(grad)
+        return grad, owners(grad)
     half = grad.shape[0] // 2
     core = lax.axis_index("fsdp")
     mine = lax.dynamic_slice_in_dim(grad, core * half, half)
@@ -426,7 +466,7 @@
     count = lax.axis_size("heads")
     rows = half // count
     spot = lax.axis_index("heads")
-    return scattered(
+    return grad, scattered(
         [
             lax.dynamic_slice_in_dim(grad, lax.rem(spot + by, count) * rows, rows)
             for by in range(count)
@@ -590,25 +630,25 @@
         gate = gate_ref[:, cols]
         normed = mixed * scale * gain_ref[...] * (gate * sigmoid(gate))
         normed_ref[:, cols] = normed.astype(BF)
-    count = len(partial_refs) // chunks
-    width = weight_ref.shape[1] // count
     steps = pl.num_programs(0) // chunks
-    for by in range(count):
-        at = lax.rem(place_ref[0] + by, count) * width
-        part = mm(normed_ref[...], weight_ref[:, pl.ds(pl.multiple_of(at, width), width)])
-        for chunk in range(chunks):
-
-            @pl.when(step // steps == chunk)
-            def _():
-                partial_refs[chunk * count + by][...] = part.astype(BF)
+    for chunk in range(chunks):
+
+        @pl.when(step // steps == chunk)
+        def _():
+            pair_parts(
+                place_ref[0],
+                weight_ref.shape[1],
+                lambda span: mm(normed_ref[...], weight_ref[:, span]),
+                *partial_refs[2 * chunk : 2 * chunk + 2],
+            )
 
 
 def mixer_output(
-    local, carry, ends, tensor_place, pre, gain, weight, key_width, value_width, chunks, count
+    local, carry, ends, tensor_place, pre, gain, weight, key_width, value_width, chunks
 ):
     rows, cols = local.shape
     heads = cols // value_width
-    width = weight.shape[1] // count
+    width = weight.shape[1] // 2
     gate_block = heads * (2 * key_width + value_width) // cols
     steps = rows // PACK // chunks
     whole = lambda shape: pl.BlockSpec(shape, lambda i, at: (0,) * len(shape))
@@ -645,32 +685,39 @@
                 pl.BlockSpec((PACK, cols), lambda i, at: (i, 0)),
                 whole((heads, key_width, value_width)),
             ]
-            + [part_spec(chunk) for chunk in range(chunks) for _ in range(count)],
+            + [part_spec(chunk) for chunk in range(chunks) for _ in range(2)],
         ),
         out_shape=[
             jax.ShapeDtypeStruct((rows, cols), BF),
             jax.ShapeDtypeStruct((rows, cols), BF),
             jax.ShapeDtypeStruct((heads, key_width, value_width), BF),
         ]
-        + [jax.ShapeDtypeStruct((rows // chunks, width), BF)] * (chunks * count),
+        + [jax.ShapeDtypeStruct((rows // chunks, width), BF)] * (chunks * 2),
         compiler_params=pltpu.CompilerParams(vmem_limit_bytes=VMEM_LIMIT),
         cost_estimate=cost(7),
         name="mixer_output",
     )(tensor_place, local, carry, *ends, pre, gain, weight)
     parts = outs[3:]
-    return outs[0], outs[1], outs[2], [parts[c * count : (c + 1) * count] for c in range(chunks)]
-
-
-def feed_kernel(place_ref, *refs, count, aliased):
-    attn = refs[:count]
-    cot_ref, token_ref, gain_ref, gate_ref, up_ref, down_ref = refs[count : count + 6]
-    outs = refs[count + 6 + aliased :]
+    return outs[0], outs[1], outs[2], [parts[c * 2 : c * 2 + 2] for c in range(chunks)]
+
+
+def feed_kernel(place_ref, *refs, chunks):
+    attn = refs[: 3 * chunks]
+    cot_ref, token_ref, gain_ref, gate_ref, up_ref, down_ref = refs[3 * chunks : 3 * chunks + 6]
+    outs = refs[3 * chunks + 6 :]
     middle_ref, hidden_ref, inner_ref, gate_grad_ref, up_grad_ref = outs[:5]
-    out_refs, mid_refs = outs[5 : 5 + count], outs[5 + count : 5 + 2 * count]
-    whole_ref = outs[5 + 2 * count]
+    out_refs, mid_refs = outs[5:9], outs[9 : 9 + 2 * chunks]
+    whole_ref, kept_ref, sent_ref = outs[9 + 2 * chunks :]
     first = down_ref.shape[0] - inner_ref.shape[1]
     place = place_ref[0]
-    feature_blocks([piece[...] for piece in attn], place, whole_ref)
+    chunk_now = pl.program_id(0) // (pl.num_programs(0) // chunks)
+    for chunk in range(chunks):
+
+        @pl.when(chunk_now == chunk)
+        def _():
+            pieces = [piece[...] for piece in attn[3 * chunk : 3 * chunk + 3]]
+            pair_blocks(pieces, place, whole_ref)
+
     middle = token_ref[...].astype(F32) + whole_ref[...].astype(F32)
     middle_ref[...] = middle
     scale = lax.rsqrt(jnp.mean(middle * middle, axis=1, keepdims=True) + EPSILON)
@@ -685,59 +732,75 @@
     inner_ref[...] = (silu * up).astype(BF)
     gate_grad_ref[...] = (inner_grad * up * (sig * (1.0 + gate * (1.0 - sig)))).astype(BF)
     up_grad_ref[...] = (inner_grad * silu).astype(BF)
-    width = whole_ref.shape[1] // count
-    for by in range(count):
-        at = lax.rem(place + by, count) * width
-        span = pl.ds(pl.multiple_of(at, width), width)
-        mid_refs[by][...] = (
-            mm_nt(gate_grad_ref[...], gate_ref[span, :many])
-            + mm_nt(up_grad_ref[...], up_ref[span, :many])
-        ).astype(BF)
+    features = whole_ref.shape[1]
+    pair_parts(
+        place,
+        features,
+        lambda span: mm_nt(gate_grad_ref[...], gate_ref[span, :many])
+        + mm_nt(up_grad_ref[...], up_ref[span, :many]),
+        kept_ref,
+        sent_ref,
+    )
+    for chunk in range(chunks):
+
+        @pl.when(chunk_now == chunk)
+        def _():
+            mid_refs[2 * chunk][...] = kept_ref[...]
+            mid_refs[2 * chunk + 1][...] = sent_ref[...]
+
+    width = features // 4
+    for by in range(4):
+        span = pl.ds(pl.multiple_of((place ^ by) * width, width), width)
         out_refs[by][...] = mm(inner_ref[...], down_ref[first:, span]).astype(BF)
 
 
-def feed_forward(chunk, chunks, tensor_place, attn, cot, token, gain, feed, down, hidden, before):
+def feed_forward(tensor_place, attn, cot, token, gain, feed, down, hidden):
     rows, features = cot.shape
-    count = len(attn)
-    width = features // count
+    chunks = len(attn)
+    width = features // 2
     steps = rows // PACK // chunks
-    first = chunk * steps
     whole = lambda shape: pl.BlockSpec(shape, lambda i, at: (0,) * len(shape))
-    rows_at = lambda size: pl.BlockSpec((PACK, size), lambda i, at: (first + i, 0))
-    part = pl.BlockSpec((PACK, width), lambda i, at: (i, 0))
-    inputs = [*attn, cot, token, gain, feed, feed, down]
+    rows_at = lambda size: pl.BlockSpec((PACK, size), lambda i, at: (i, 0))
+
+    def part(chunk, size):
+        return pl.BlockSpec(
+            (PACK, size), lambda i, at: (jnp.clip(i - chunk * steps, 0, steps - 1), 0)
+        )
+
     kept = [
         (features, F32),
         (features, BF),
         (hidden, BF),
         (hidden, BF),
         (hidden, BF),
-    ] + [(width, BF)] * count
+    ] + [(width // 2, BF)] * 4
     outs = pl.pallas_call(
-        functools.partial(feed_kernel, count=count, aliased=len(before)),
+        functools.partial(feed_kernel, chunks=chunks),
         grid_spec=pltpu.PrefetchScalarGridSpec(
             num_scalar_prefetch=1,
-            grid=(steps,),
-            in_specs=[part] * count
+            grid=(rows // PACK,),
+            in_specs=[
+                part(chunk, piece.shape[1]) for chunk in range(chunks) for piece in attn[chunk]
+            ]
             + [rows_at(features)] * 2
             + [
                 whole(gain.shape),
                 pl.BlockSpec((features, feed.shape[1] // 2), lambda i, at: (0, 0)),
                 pl.BlockSpec((features, feed.shape[1] // 2), lambda i, at: (0, 1)),
                 whole(down.shape),
-            ]
-            + [pl.BlockSpec(memory_space=pl.ANY)] * len(before),
-            out_specs=[rows_at(size) for size, _ in kept] + [part] * count,
-            scratch_shapes=[pltpu.VMEM((PACK, features), BF)],
+            ],
+            out_specs=[rows_at(size) for size, _ in kept]
+            + [part(chunk, width) for chunk in range(chunks) for _ in range(2)],
+            scratch_shapes=[pltpu.VMEM((PACK, features), BF)]
+            + [pltpu.VMEM((PACK, width), BF)] * 2,
         ),
         out_shape=[jax.ShapeDtypeStruct((rows, size), kind) for size, kind in kept]
-        + [jax.ShapeDtypeStruct((rows // chunks, width), BF)] * count,
-        input_output_aliases={1 + len(inputs) + i: i for i in range(len(before))},
+        + [jax.ShapeDtypeStruct((rows // chunks, width), BF)] * (2 * chunks),
         compiler_params=pltpu.CompilerParams(vmem_limit_bytes=VMEM_LIMIT),
-        cost_estimate=cost(10),
+        cost_estimate=cost(20),
         name="feed_forward",
-    )(tensor_place, *inputs, *before)
-    return outs[: 5 + count], outs[5 + count :]
+    )(tensor_place, *[piece for pieces in attn for piece in pieces], cot, token, gain, feed, feed, down)
+    return outs[:9], [outs[9 + 2 * chunk : 11 + 2 * chunk] for chunk in range(chunks)]
 
 
 def gate_back_kernel(
@@ -775,7 +838,7 @@
         ffn_gain_grad_ref[...] = jnp.zeros_like(ffn_gain_grad_ref)
         enter_grad_ref[...] = jnp.zeros_like(enter_grad_ref)
 
-    feature_blocks([piece[...] for piece in pieces], place_ref[0], whole_ref)
+    pair_blocks([piece[...] for piece in pieces], place_ref[0], whole_ref)
     middle = middle_ref[...]
     scale_mid = lax.rsqrt(jnp.mean(middle * middle, axis=1, keepdims=True) + EPSILON)
     hidden_grad = whole_ref[...].astype(F32)
@@ -862,7 +925,9 @@
         grid_spec=pltpu.PrefetchScalarGridSpec(
             num_scalar_prefetch=1,
             grid=(steps,),
-            in_specs=[pl.BlockSpec((PACK, width), lambda i, at: (i, 0))] * len(pieces)
+            in_specs=[
+                pl.BlockSpec((PACK, piece.shape[1]), lambda i, at: (i, 0)) for piece in pieces
+            ]
             + [
                 rows_at(features),
                 rows_at(features),
@@ -1005,7 +1070,92 @@
     return conv_grad
 
 
+def true_kernel(
+    small_ref,
+    rate_ref,
+    bias_ref,
+    w_ref,
+    u_ref,
+    states_ref,
+    enter_ref,
+    true_ref,
+    whole_ref,
+    renewed_ref,
+    *,
+    heads,
+    rows,
+    key_width,
+    value_width,
+):
+    inner = PACK // GROUP
+
+    span = slice(0, PACK)
+    decay_tile, _ = rates_of(small_ref[span, :], rate_ref[...], bias_ref[...])
+    for head in range(heads):
+        cols = slice(head * key_width, (head + 1) * key_width)
+        value_at = slice(head * value_width, (head + 1) * value_width)
+        decay = column_of(decay_tile, head)
+        w = w_ref[span, cols]
+        u = u_ref[span, value_at]
+        renewed = []
+        for b in range(inner):
+            index = b * heads + head
+            part = slice(b * GROUP, (b + 1) * GROUP)
+            whole = jnp.exp(jnp.sum(decay[part], axis=0, keepdims=True))
+            whole_ref[index] = jnp.broadcast_to(whole, (8, LANES))
+            state = (
+                states_ref[index, :, :value_width].astype(F32)
+                + mm(states_ref[index, :, value_width:], enter_ref[head])
+            ).astype(BF)
+            true_ref[index] = state
+            renewed.append((u[part].astype(F32) - mm(w[part], state)).astype(BF))
+        renewed_ref[span, value_at] = jnp.concatenate(renewed, axis=0)
+
+
+def mixer_true(pre, rate, bias, w, u, states, enter, heads, key_width, value_width):
+    rows = pre.shape[0] - RIM
+    wide = heads * (2 * key_width + value_width)
+    gate_wide = heads * value_width
+    count = rows // GROUP
+    whole = lambda shape: pl.BlockSpec(shape, lambda i: (0,) * len(shape))
+    outs = [
+        ((count * heads, key_width, value_width), BF),
+        ((count * heads, 8, LANES), F32),
+        ((rows, heads * value_width), BF),
+    ]
+    given = [rate, bias, w, u, states, enter]
+    rows_at = lambda width: pl.BlockSpec((PACK, width), lambda i: (i, 0))
+    blocks_at = lambda shape: pl.BlockSpec(
+        (PACK // GROUP * heads,) + shape, lambda i: (i, 0, 0)
+    )
+    return pl.pallas_call(
+        functools.partial(
+            true_kernel, heads=heads, rows=rows, key_width=key_width, value_width=value_width
+        ),
+        grid=(rows // PACK,),
+        in_specs=[
+            pl.BlockSpec((PACK, LANES), lambda i: (i, (wide + gate_wide) // LANES)),
+            whole(rate.shape),
+            whole(bias.shape),
+            rows_at(w.shape[1]),
+            rows_at(u.shape[1]),
+            blocks_at(states.shape[1:]),
+            whole(enter.shape),
+        ],
+        out_specs=[
+            blocks_at((key_width, value_width)),
+            blocks_at((8, LANES)),
+            rows_at(heads * value_width),
+        ],
+        out_shape=[jax.ShapeDtypeStruct(shape, kind) for shape, kind in outs],
+        compiler_params=pltpu.CompilerParams(vmem_limit_bytes=VMEM_LIMIT),
+        cost_estimate=cost(6),
+        name="mixer_true",
+    )(pre, *given)
+
+
 def ready_kernel(
+    head_ref,
     pre_ref,
     small_ref,
     taps_ref,
@@ -1014,14 +1164,9 @@
     bias_ref,
     queries_ref,
     keys_ref,
-    w_ref,
-    u_ref,
-    states_ref,
-    enter_ref,
+    true_ref,
+    renewed_ref,
     mixed_grad_ref,
-    true_ref,
-    whole_ref,
-    renewed_ref,
     base_ref,
     key_part_ref,
     conv_grad_ref,
@@ -1033,69 +1178,57 @@
     key_width,
     value_width,
 ):
-    groups = rows // PACK
     inner = PACK // GROUP
-    taps_grad_ref[...] = jnp.zeros_like(taps_grad_ref)
-    def ready(group, _):
-        masks = pack_masks()
-        row, col, apart, same, lower, strict = masks
-        span = pl.ds(pl.multiple_of(group * PACK, PACK), PACK)
-        valid = valid_ref[pl.ds(pl.multiple_of(group * PACK + RIM, RIM), PACK), :]
-        decay_tile, _ = rates_of(small_ref[span, :], rate_ref[...], bias_ref[...])
-        lane = lax.broadcasted_iota(jnp.int32, (PACK, LANES), 1)
-        along = jnp.zeros((PACK, LANES), F32)
-        for head in range(heads):
-            cols = slice(head * key_width, (head + 1) * key_width)
-            value_at = slice(head * value_width, (head + 1) * value_width)
-            query = queries_ref[span, cols]
-            key = keys_ref[span, cols]
-            gam, last, fading = packed_decay(column_of(decay_tile, head), masks)
-            whole = jnp.exp(last)
-            scores = mm_nt(query, key) * fading
-            w = w_ref[span, cols]
-            u = u_ref[span, value_at]
-            out_grad = mixed_grad_ref[span, value_at]
-            renewed, grown_grad = [], []
-            for b in range(inner):
-                index = (group * inner + b) * heads + head
-                part = slice(b * GROUP, (b + 1) * GROUP)
-                whole_ref[index] = jnp.broadcast_to(whole[b * GROUP : b * GROUP + 1], (8, LANES))
-                state = (
-                    states_ref[index, :, :value_width].astype(F32)
-                    + mm(states_ref[index, :, value_width:], enter_ref[head])
-                ).astype(BF)
-                true_ref[index] = state
-                renewed.append(u[part].astype(F32) - mm(w[part], state))
-                grown_grad.append(mm_nt(out_grad[part], state))
-            renewed = jnp.concatenate(renewed, axis=0).astype(BF)
-            renewed_ref[span, value_at] = renewed
-            base_ref[span, value_at] = mm_tn(scores, out_grad)
-            scores_grad = jnp.where(lower, mm_nt(out_grad, renewed), 0.0)
-            pair_grad = (scores_grad * fading).astype(BF)
-            grown_grad = jnp.exp(gam) * jnp.concatenate(grown_grad, axis=0)
-            query_grad = mm(pair_grad, key) + grown_grad
-            along = jnp.where(
-                lane == head,
-                net_of(scores_grad * scores, apart)
-                + jnp.sum(grown_grad * query.astype(F32), axis=1, keepdims=True),
-                along,
-            )
-            key_part_ref[span, cols] = mm_tn(pair_grad, query)
-            window = load_window(pre_ref, group, head * key_width, key_width, rows)
-            conv_grad_ref[span, cols] = conv_back(
-                query_grad,
-                window,
-                taps_ref,
-                valid,
-                head * key_width,
-                key_width,
-                key_width ** (-0.5),
-                taps_grad_ref,
-            )
-        along_ref[span, :] = along
-        return 0
-
-    lax.fori_loop(0, groups, ready, 0)
+    group = pl.program_id(0)
+
+    @pl.when(group == 0)
+    def _():
+        taps_grad_ref[...] = jnp.zeros_like(taps_grad_ref)
+    masks = pack_masks()
+    row, col, apart, same, lower, strict = masks
+    span = slice(0, PACK)
+    valid = valid_ref[pl.ds(pl.multiple_of(group * PACK + RIM, RIM), PACK), :]
+    decay_tile, _ = rates_of(small_ref[span, :], rate_ref[...], bias_ref[...])
+    lane = lax.broadcasted_iota(jnp.int32, (PACK, LANES), 1)
+    along = jnp.zeros((PACK, LANES), F32)
+    for head in range(heads):
+        cols = slice(head * key_width, (head + 1) * key_width)
+        value_at = slice(head * value_width, (head + 1) * value_width)
+        query = queries_ref[span, cols]
+        key = keys_ref[span, cols]
+        gam, last, fading = packed_decay(column_of(decay_tile, head), masks)
+        scores = mm_nt(query, key) * fading
+        renewed = renewed_ref[span, value_at]
+        out_grad = mixed_grad_ref[span, value_at]
+        grown_grad = []
+        for b in range(inner):
+            index = b * heads + head
+            part = slice(b * GROUP, (b + 1) * GROUP)
+            grown_grad.append(mm_nt(out_grad[part], true_ref[index]))
+        base_ref[span, value_at] = mm_tn(scores, out_grad)
+        scores_grad = jnp.where(lower, mm_nt(out_grad, renewed), 0.0)
+        pair_grad = (scores_grad * fading).astype(BF)
+        grown_grad = jnp.exp(gam) * jnp.concatenate(grown_grad, axis=0)
+        query_grad = mm(pair_grad, key) + grown_grad
+        along = jnp.where(
+            lane == head,
+            net_of(scores_grad * scores, apart)
+            + jnp.sum(grown_grad * query.astype(F32), axis=1, keepdims=True),
+            along,
+        )
+        key_part_ref[span, cols] = mm_tn(pair_grad, query)
+        window = jnp.concatenate([head_ref[:, cols], pre_ref[:, cols]], axis=0)
+        conv_grad_ref[span, cols] = conv_back(
+            query_grad,
+            window,
+            taps_ref,
+            valid,
+            head * key_width,
+            key_width,
+            key_width ** (-0.5),
+            taps_grad_ref,
+        )
+    along_ref[span, :] = along
 
 
 def mixer_ready(
@@ -1106,10 +1239,8 @@
     bias,
     queries,
     keys,
-    w,
-    u,
-    states,
-    enter,
+    true,
+    renewed,
     mixed_grad,
     heads,
     key_width,
@@ -1118,45 +1249,45 @@
     rows = pre.shape[0] - RIM
     wide = heads * (2 * key_width + value_width)
     gate_wide = heads * value_width
-    count = rows // GROUP
     key_cols = heads * key_width
     whole = lambda shape: pl.BlockSpec(shape, lambda i: (0,) * len(shape))
     outs = [
-        ((count * heads, key_width, value_width), BF),
-        ((count * heads, 8, LANES), F32),
-        ((rows, heads * value_width), BF),
         ((rows, heads * value_width), F32),
         ((rows, key_cols), F32),
         ((rows, key_cols), F32),
         ((8, key_cols), F32),
         ((rows, LANES), F32),
     ]
+    rows_at = lambda width: pl.BlockSpec((PACK, width), lambda i: (i, 0))
+    head_at = lambda i: jnp.where(i == 0, rows // RIM, i * (PACK // RIM) - 1)
     return pl.pallas_call(
         functools.partial(
             ready_kernel, heads=heads, rows=rows, key_width=key_width, value_width=value_width
         ),
-        grid=(1,),
+        grid=(rows // PACK,),
         in_specs=[
-            pl.BlockSpec((rows + RIM, key_cols), lambda i: (0, 0)),
-            pl.BlockSpec((rows + RIM, LANES), lambda i: (0, (wide + gate_wide) // LANES)),
+            pl.BlockSpec((RIM, key_cols), lambda i: (head_at(i), 0)),
+            rows_at(key_cols),
+            pl.BlockSpec((PACK, LANES), lambda i: (i, (wide + gate_wide) // LANES)),
             whole(taps.shape),
             whole(valid.shape),
             whole(rate.shape),
             whole(bias.shape),
-            whole(queries.shape),
-            pl.BlockSpec((rows, key_cols), lambda i: (0, 0)),
-            whole(w.shape),
-            whole(u.shape),
-            whole(states.shape),
-            whole(enter.shape),
-            whole(mixed_grad.shape),
+            rows_at(key_cols),
+            rows_at(key_cols),
+            pl.BlockSpec((PACK // GROUP * heads,) + true.shape[1:], lambda i: (i, 0, 0)),
+            rows_at(renewed.shape[1]),
+            rows_at(mixed_grad.shape[1]),
         ],
-        out_specs=[whole(shape) for shape, _ in outs],
+        out_specs=[
+            whole(shape) if shape[0] == 8 else rows_at(shape[1]) for shape, _ in outs
+        ],
         out_shape=[jax.ShapeDtypeStruct(shape, kind) for shape, kind in outs],
         compiler_params=pltpu.CompilerParams(vmem_limit_bytes=VMEM_LIMIT),
-        cost_estimate=cost(14),
+        cost_estimate=cost(11),
         name="mixer_ready",
     )(
+        pre,
         pre,
         pre,
         taps,
@@ -1165,16 +1296,15 @@
         bias,
         queries,
         keys,
-        w,
-        u,
-        states,
-        enter,
+        true,
+        renewed,
         mixed_grad,
     )
 
 
 def backward_kernel(
     keep_ref,
+    head_ref,
     pre_ref,
     small_ref,
     taps_ref,
@@ -1216,37 +1346,44 @@
     inner = PACK // GROUP
     key_cols = heads * key_width
     wide = heads * (2 * key_width + value_width)
-    taps_grad_ref[...] = jnp.zeros_like(taps_grad_ref)
-    taps_grad_ref[:, :key_cols] = query_taps_ref[...]
-    rate_grad_ref[...] = jnp.zeros_like(rate_grad_ref)
-    conv_grad_ref[0:RIM, :] = jnp.zeros((RIM, wide), F32)
-    conv_grad_ref[RIM + rows :, :] = jnp.zeros((RIM, wide), F32)
-    conv_grad_ref[RIM : RIM + rows, :key_cols] = query_conv_ref[...]
-    small_grad_ref[rows:, :] = jnp.zeros((RIM, LANES), BF)
-
-    for head in range(heads):
-        flow = next4_ref[head, :, :value_width].astype(F32)
-        for near in (next3_ref, next2_ref, next1_ref):
-            flow = near[head, :, :value_width].astype(F32) + mm_tn(
-                near[head, :, value_width:], flow
-            )
-        flow_ref[head] = flow
-    for block in reversed(range(rows // GROUP)):
+    step = pl.program_id(0)
+
+    @pl.when(step == 0)
+    def _():
+        taps_grad_ref[...] = jnp.zeros_like(taps_grad_ref)
+        taps_grad_ref[:, :key_cols] = query_taps_ref[...]
+        rate_grad_ref[...] = jnp.zeros_like(rate_grad_ref)
+        conv_grad_ref[0:RIM, :] = jnp.zeros((RIM, wide), F32)
+        conv_grad_ref[RIM + rows :, :] = jnp.zeros((RIM, wide), F32)
+        conv_grad_ref[RIM : RIM + rows, :key_cols] = query_conv_ref[...]
+        small_grad_ref[rows:, :] = jnp.zeros((RIM, LANES), BF)
+
         for head in range(heads):
-            index = block * heads + head
-            flow = flow_ref[head]
-            flow_low = flow.astype(BF)
-            later_ref[index] = flow_low
-            flow_ref[head] = keep_ref[block] * (
-                whole_ref[index, 0:1, 0:1] * flow
-                - mm_tn(fold_ref[index], flow_low)
-                + source_ref[index]
-            )
-
-    def back(group, _):
+            flow = next4_ref[head, :, :value_width].astype(F32)
+            for near in (next3_ref, next2_ref, next1_ref):
+                flow = near[head, :, :value_width].astype(F32) + mm_tn(
+                    near[head, :, value_width:], flow
+                )
+            flow_ref[head] = flow
+        for block in reversed(range(rows // GROUP)):
+            for head in range(heads):
+                index = block * heads + head
+                flow = flow_ref[head]
+                flow_low = flow.astype(BF)
+                later_ref[index] = flow_low
+                flow_ref[head] = keep_ref[block] * (
+                    whole_ref[index, 0:1, 0:1] * flow
+                    - mm_tn(fold_ref[index], flow_low)
+                    + source_ref[index]
+                )
+
+    @pl.when(step > 0)
+    def _():
+        group = step - 1
         masks = pack_masks()
         row, col, apart, same, lower, strict = masks
-        span = pl.ds(pl.multiple_of(group * PACK, PACK), PACK)
+        span = pl.ds(0, PACK)
+        out_span = pl.ds(pl.multiple_of(group * PACK, PACK), PACK)
         small = small_ref[span, :]
         valid = valid_ref[pl.ds(pl.multiple_of(group * PACK + RIM, RIM), PACK), :]
         decay_tile, beta_tile = rates_of(small, rate_ref[...], bias_ref[...])
@@ -1271,9 +1408,10 @@
             renewed_grad, drops = [], []
             for b in range(inner):
                 index = (group * inner + b) * heads + head
+                near = b * heads + head
                 flow = later_ref[index]
                 renewed_grad.append(mm(tail[b * GROUP : (b + 1) * GROUP], flow))
-                shared = true_ref[index].astype(F32) * flow.astype(F32)
+                shared = true_ref[near].astype(F32) * flow.astype(F32)
                 shared = jnp.sum(jnp.sum(shared, axis=1, keepdims=True), axis=0, keepdims=True)
                 drops.append(
                     jnp.broadcast_to(shared * whole_ref[index, 0:1, 0:1], (GROUP, 1))
@@ -1286,10 +1424,10 @@
                 index = (group * inner + b) * heads + head
                 part = slice(b * GROUP, (b + 1) * GROUP)
                 tail_grad.append(mm_nt(renewed[part], later_ref[index]))
-                w_grad.append(mm_nt(renewed_low[part], true_ref[index]))
+                w_grad.append(mm_nt(renewed_low[part], true_ref[b * heads + head]))
             tail_grad = jnp.concatenate(tail_grad, axis=0)
             w_grad = -jnp.concatenate(w_grad, axis=0)
-            inverse = inverse_ref[group * heads + head]
+            inverse = inverse_ref[head]
             keys_grad = mm_tn(inverse, w_grad)
             values_grad = mm_tn(inverse, renewed_low)
             system_grad = jnp.where(strict, -(mm_nt(keys_grad, w) + mm_nt(values_grad, u)), 0.0)
@@ -1338,7 +1476,9 @@
                 (key_cols + head * key_width, key_width, key_grad, 1.0),
                 (2 * key_cols + head * value_width, value_width, value_grad, None),
             ):
-                window = load_window(pre_ref, group, first, width, rows)
+                window = jnp.concatenate(
+                    [head_ref[:, first : first + width], pre_ref[:, first : first + width]], axis=0
+                )
                 conv_grad_ref[
                     pl.ds(pl.multiple_of(group * PACK + RIM, RIM), PACK), first : first + width
                 ] = conv_back(
@@ -1351,12 +1491,9 @@
             lane < heads, small_rows * slope, small_rows * beta_tile * (1.0 - beta_tile)
         )
         small_grad = jnp.where(lane < 2 * heads, small_grad, 0.0)
-        small_grad_ref[span, :] = small_grad.astype(BF)
+        small_grad_ref[out_span, :] = small_grad.astype(BF)
         rate_grad_ref[0:1, :] += jnp.sum(small_rows * decay_tile, axis=0, keepdims=True)
         rate_grad_ref[1:2, :] += jnp.sum(small_grad, axis=0, keepdims=True)
-        return 0
-
-    lax.fori_loop(0, groups, back, 0)
 
     def convolve_back(start, target, count, first):
         cols = slice(first, first + LANES)
@@ -1371,15 +1508,17 @@
             total = term if total is None else total + term
         pre_grad_ref[pl.ds(target, count), cols] = total[:count].astype(BF)
 
-    def spread(group, _):
-        base = pl.multiple_of(group * PACK, PACK)
+    @pl.when(step == groups)
+    def _():
+        def spread(group, _):
+            base = pl.multiple_of(group * PACK, PACK)
+            for first in range(0, wide, LANES):
+                convolve_back(pl.multiple_of(base + RIM, RIM), base, PACK, first)
+            return 0
+
+        lax.fori_loop(0, groups, spread, 0)
         for first in range(0, wide, LANES):
-            convolve_back(pl.multiple_of(base + RIM, RIM), base, PACK, first)
-        return 0
-
-    lax.fori_loop(0, groups, spread, 0)
-    for first in range(0, wide, LANES):
-        convolve_back(0, rows, RIM, first)
+            convolve_back(0, rows, RIM, first)
 
 
 def mixer_backward(
@@ -1412,18 +1551,43 @@
         ((8, wide), F32),
         ((8, LANES), F32),
     ]
-    given = [taps, valid, rate, bias, keys, inverse, w, u, fold, source, *found, *nexts]
+    groups = rows // PACK
+    step = PACK // GROUP * heads
+    at = lambda i: jnp.maximum(i - 1, 0)
+    rows_at = lambda width: pl.BlockSpec((PACK, width), lambda i: (at(i), 0))
+    blocks_at = lambda many, shape: pl.BlockSpec((many,) + shape, lambda i: (at(i), 0, 0))
+    true, whole_decays, renewed, base, key_part, query_conv, query_taps, along = found
+    head_at = lambda i: jnp.where(at(i) == 0, rows // RIM, at(i) * (PACK // RIM) - 1)
     return pl.pallas_call(
         functools.partial(
             backward_kernel, heads=heads, rows=rows, key_width=key_width, value_width=value_width
         ),
-        grid=(1,),
+        grid=(groups + 1,),
         in_specs=[
             pl.BlockSpec(memory_space=pltpu.SMEM),
-            pl.BlockSpec((rows + RIM, wide), lambda i: (0, 0)),
-            pl.BlockSpec((rows + RIM, LANES), lambda i: (0, (wide + gate_wide) // LANES)),
+            pl.BlockSpec((RIM, wide), lambda i: (head_at(i), 0)),
+            rows_at(wide),
+            pl.BlockSpec((PACK, LANES), lambda i: (at(i), (wide + gate_wide) // LANES)),
+            whole(taps.shape),
+            whole(valid.shape),
+            whole(rate.shape),
+            whole(bias.shape),
+            rows_at(keys.shape[1]),
+            blocks_at(heads, inverse.shape[1:]),
+            rows_at(w.shape[1]),
+            rows_at(u.shape[1]),
+            whole(fold.shape),
+            whole(source.shape),
+            blocks_at(step, true.shape[1:]),
+            whole(whole_decays.shape),
+            rows_at(renewed.shape[1]),
+            rows_at(base.shape[1]),
+            rows_at(key_part.shape[1]),
+            whole(query_conv.shape),
+            whole(query_taps.shape),
+            rows_at(along.shape[1]),
         ]
-        + [whole(array.shape) for array in given],
+        + [whole(near.shape) for near in nexts],
         out_specs=[whole(shape) for shape, _ in outs],
         out_shape=[jax.ShapeDtypeStruct(shape, kind) for shape, kind in outs],
         scratch_shapes=[
@@ -1434,7 +1598,7 @@
         compiler_params=pltpu.CompilerParams(vmem_limit_bytes=VMEM_LIMIT),
         cost_estimate=cost(25),
         name="mixer_backward",
-    )(keep, pre, pre, *given)
+    )(keep, pre, pre, pre, taps, valid, rate, bias, keys, inverse, w, u, fold, source, *found, *nexts)
 
 
 def spread_into(piece, whole_shape, start, axis_number):
@@ -1525,7 +1689,9 @@
     token_rows, hidden_in, scale_in, pre = project(
         tensor_array, token_pieces, norm_row, in_full
     )
-    cot_held, *_ = lax.optimization_barrier((cotangent, *token_pieces[1:]))
+    cot_held, *_ = lax.optimization_barrier(
+        (cotangent, down_full, feed_full, valid, keep, taps, rate, bias, *token_pieces[1:])
+    )
     cot_rows = lax.all_gather(cot_held, "tensor", axis=1, tiled=True)
 
     keys, inverse, w, u, fold, states, end = mixer_forward(
@@ -1547,35 +1713,28 @@
         key_width,
         value_width,
         CHUNKS,
-        count,
-    )
-
-    kept, mid_parts = (), []
-    attn_chunks = [exchanged(parts) for parts in attn_parts]
-    for chunk in range(CHUNKS):
-        kept, mid = feed_forward(
-            chunk,
-            CHUNKS,
-            tensor_array,
-            attn_chunks[chunk],
-            cot_rows,
-            token_rows,
-            ffn_row,
-            feed_full,
-            down_full,
-            hidden,
-            kept,
-        )
-        mid_parts.append(mid)
+    )
+
+    settled = mixer_true(pre, rate, bias, w, u, states, enter, heads, key_width, value_width)
+    halves = [
+        pair_half(*parts, settled if chunk == 0 else None) for chunk, parts in enumerate(attn_parts)
+    ]
+    attn_chunks = [pair_gather(pair_rest(*half).astype(BF)) for half in halves]
+    true, whole_decays, renewed = settled
+    kept, mid_parts = feed_forward(
+        tensor_array, attn_chunks, cot_rows, token_rows, ffn_row, feed_full, down_full, hidden
+    )
     middle, hidden_mid, inner_act, gate_grad, up_grad, *out_parts = kept
     back_kept, sums = (), []
-    mid_chunks = [exchanged(parts) for parts in mid_parts]
-    inner_held = lax.optimization_barrier((inner_act, mid_chunks[0][0]))[0]
     feed_local = weight_grads(
-        (hidden_mid, gate_grad), (hidden_mid, up_grad), (cot_rows, inner_held)
-    )
+        (hidden_mid, gate_grad), (hidden_mid, up_grad), (cot_rows, inner_act)
+    )
+    halves = [
+        pair_half(*parts, feed_local if chunk == 0 else None)
+        for chunk, parts in enumerate(mid_parts)
+    ]
+    mid_chunks = [pair_gather(pair_rest(*half).astype(BF)) for half in halves]
     feed_grads = owners(feed_local)
-    mid_chunks[0][0] = lax.optimization_barrier((mid_chunks[0][0], feed_local))[0]
     for chunk in range(CHUNKS):
         back_kept, found = gate_back(
             chunk,
@@ -1603,7 +1762,7 @@
     nexts = [shifted(enter_low, FH, -by) for by in range(1, reach + 1)]
     attn_held, feed_grads = lax.optimization_barrier((attn_grad, feed_grads))
     out_local = weight_grads((attn_held, normed), (hidden_in, outgate_grad))
-    out_grads = owners(out_local)
+    out_sums = lax.psum_scatter(out_local, FH, scatter_dimension=0, tiled=True)
     mixed_held, out_held = lax.optimization_barrier((mixed_grad, out_parts, out_local))[:2]
     found = mixer_ready(
         pre,
@@ -1613,16 +1772,17 @@
         bias,
         queries,
         keys,
-        w,
-        u,
-        states,
-        enter,
+        true,
+        renewed,
         mixed_held,
         heads,
         key_width,
         value_width,
     )
-    output_terms = scattered(out_held, "tensor")
+    found = [true, whole_decays, renewed, *found]
+    output_terms = out_held[0].astype(F32)
+    for by in (1, 2, 3):
+        output_terms = output_terms + paired(out_held[by], by).astype(F32)
     middle_own = lax.dynamic_slice_in_dim(middle, tensor_place * slice_width, slice_width, 1)
     output_rows = (middle_own + output_terms).astype(BF)
     pre_grad, small_grad, taps_grad, rate_grad = mixer_backward(
@@ -1645,13 +1805,13 @@
         value_width,
     )
 
-    pre_grad, out_grads = lax.optimization_barrier((pre_grad, out_grads))
     in_dot, norm_gain_grad, rim_terms, in_part = input_terms(
         tensor_array, pre_grad, small_grad, outgate_grad, in_full, token_rows, scale_in, norm_row, count
     )
+    out_grads = out_sums.astype(F32)
     in_grad = lax.psum_scatter(in_part, "tensor", scatter_dimension=1, tiled=True).astype(F32)
-    late_held = lax.optimization_barrier((pre_grad, in_part))[0]
-    late_grads = owners_by_steps(weight_grads((hidden_in, late_held), (hidden_in, small_grad)))
+    late_local = weight_grads((hidden_in, pre_grad), (hidden_in, small_grad))
+    late_half, late_grads = owners_by_steps(late_local)
     rim = shifted(jnp.concatenate([rim_terms, in_dot[rows:]], axis=1), FH, -1)
     in_dot = in_dot[:rows, 0] + jnp.pad(rim[:, full_width], (rows - RIM, 0))
     rim_blocks = [
@@ -1680,6 +1840,7 @@
     )
     flat = jnp.concatenate([piece.reshape(-1) for piece in pieces])
     flat = jnp.pad(flat, (0, -flat.size % (8 * LANES))).reshape(-1, LANES)
+    flat = lax.optimization_barrier((flat, late_half))[0]
     flat = total_batches(flat).reshape(-1)
     joined = scattered(
         [jnp.concatenate([flat, in_dot, block]).reshape(-1, LANES) for block in rim_blocks], "tensor"

time: 533 us -> 505 us (0.947)
  waiting for transfers between devices: 195 us -> 169 us
  starting transfers between devices: 75.5 us -> 91.4 us
  Pallas kernels: 177 us -> 163 us
    ppermute x39 -> x12, waiting for transfers between devices: 190 us -> 58.7 us  [rotated(): lax.ppermute(shard, axis, [(i, (i + by) % devices) for i in range(devices)])]
    ppermute x0 -> x19, waiting for transfers between devices: none -> 109 us  [paired(): return lax.ppermute(shard, 'tensor', [(i, i ^ by) for i in range(devices)])]
    ppermute x0 -> x19, starting transfers between devices: none -> 39.2 us  [paired(): return lax.ppermute(shard, 'tensor', [(i, i ^ by) for i in range(devices)])]
    ppermute x39 -> x12, starting transfers between devices: 51.1 us -> 18.6 us  [rotated(): lax.ppermute(shard, axis, [(i, (i + by) % devices) for i in range(devices)])]
    reduce_scatter x1, starting transfers between devices: 0.04 us -> 8.56 us  [per_device(): lax.psum_scatter(in_part, 'tensor', scatter_dimension=1, tiled=True)]
    pallas_call x1, Pallas kernels: 16.1 us -> 9.06 us  [mixer_ready(): pl.pallas_call(functools.partial(ready_kernel, heads=heads, rows=rows, ke...]
    unnamed x131 -> x135, local copies, waits for them, and re-layouts: 16.1 us -> 16.1 us
  transfers between devices with their start and end apart: 58 -> 50, of which waited for: 30 -> 21; matrix products, arithmetic and copies ran while one was open for 9% -> 10% of each run, Pallas kernels for 30% -> 25%
where the time goes in v3:
time: 505 us; the launch traced here: 499 us
  waiting for transfers between devices  169 us (33%)
  Pallas kernels  163 us (32%)
  starting transfers between devices  91.4 us (18%)
  local copies, waits for them, and re-layouts  39.7 us (8%)
  other arithmetic  20.9 us (4%)
  between operations  15.4 us (3%)
    ppermute x19, waiting for transfers between devices, paired(): return lax.ppermute(shard, 'tensor', [(i, i ^ by) for i in range(devices)])  109 us
    ppermute x12, waiting for transfers between devices, rotated(): lax.ppermute(shard, axis, [(i, (i + by) % devices) for i in range(devices)])  58.7 us
    ppermute x19, starting transfers between devices, paired(): return lax.ppermute(shard, 'tensor', [(i, i ^ by) for i in range(devices)])  39.2 us
    pallas_call x1, Pallas kernels, mixer_backward(): pl.pallas_call(functools.partial(backward_kernel, heads=heads, rows=rows,...  29.7 us
    pallas_call x3, Pallas kernels, weight_grads(): pl.pallas_call(functools.partial(weight_kernel, rows=[right.shape[0] for...  24.4 us
    pallas_call x1, Pallas kernels, feed_forward(): pl.pallas_call(functools.partial(feed_kernel, chunks=chunks), grid_spec=p...  19.5 us
    ppermute x10, starting transfers between devices, shifted(): return lax.ppermute(shard, axis, pairs)  19.5 us
    pallas_call x1, Pallas kernels, mixer_forward(): pl.pallas_call(functools.partial(forward_kernel, heads=heads, rows=rows,...  18.8 us
  transfers between devices with their start and end apart: 50, of which 21 were waited for; matrix products, arithmetic and copies ran while one was open for 10% of the time, Pallas kernels for 25%

profile of v3, /device:TPU:8, one launch (start us, length us, event | category | flops | bytes accessed | tf_op | source)
XLA Modules:
  0.0 499.3 jit_solution(15627999573506168969)
XLA Ops:
  15.2 3.4 collective-permute-start
  22.1 2.6 collective-permute-start.2
  28.2 31.3 %collective-permute-done.3.refs_3_ = bf16[1040,256]{1,0:T(8,128)(2,1)S(1)} collective-permute-done((bf16[1040,256]{1,0:T(8,128)(2,1)S(1)}, bf16[1040,256]{1,0:T(8,128)(2,1)S(1)}, u32[]{:S(2)}, u32[]{:S(2)}) %collective-permute-start.3) | collective-permute-done | bytes 532512 | tf_op jit(solution)/shard_map/ppermute | solution.py:390
  59.5 10.3 %collective-permute-done.1.refs_1_ = bf16[1040,256]{1,0:T(8,128)(2,1)S(1)} collective-permute-done((bf16[1040,256]{1,0:T(8,128)(2,1)S(1)}, bf16[1040,256]{1,0:T(8,128)(2,1)S(1)}, u32[]{:S(2)}, u32[]{:S(2)}) %collective-permute-start.1) | collective-permute-done | bytes 532512 | tf_op jit(solution)/shard_map/ppermute | solution.py:390
  70.6 12.1 %project.1 = (bf16[1040,1024]{1,0:T(8,128)(2,1)}, bf16[1040,1024]{1,0:T(8,128)(2,1)}, f32[1040,128]{1,0:T(8,128)}, f32[1040,1792]{1,0:T(8,128)}) custom-call(s32[1]{0:T(128)} %bitcast.place_ref, bf16[1040,256]{1,0:T(8,128)(2,1)} %copy-done.25, bf16[1040,256]{1,0:T(8,128)(2,1)} %copy-done.40, bf16[1040,256]{1,0:T(8,128)(2,1)} %copy-done.39, ...), custom_call_target="tpu_custom_call" | custom-call | flops 8000000000 | bytes 24000000 | tf_op jit(solution)/shard_map/project/pallas_call | solution.py:563
  82.7 18.8 %mixer_forward.1 = (bf16[1024,768]{1,0:T(8,128)(2,1)}, bf16[8,256,256]{2,1,0:T(8,128)(2,1)}, bf16[1024,256]{1,0:T(8,128)(2,1)}, bf16[1024,512]{1,0:T(8,128)(2,1)...) custom-call(f32[16]{0:T(128)} %convert_subtract_fusion.keep_ref, ...), custom_call_target="tpu_custom_call" | custom-call | flops 20000000000 | bytes 60000000 | tf_op jit(solution)/shard_map/mixer_forward/pallas_call | solution.py:262
  102.8 2.6 collective-permute-start.6
  105.4 3.0 collective-permute-start.5
  108.4 2.8 collective-permute-start.4
  111.1 8.9 %mixer_query.1 = (bf16[1024,256]{1,0:T(8,128)(2,1)}, bf16[32,64,128]{2,1,0:T(8,128)(2,1)}, f32[1024,512]{1,0:T(8,128)}, bf16[1024,256]{1,0:T(8,128)(2,1)}) custom-call(f32[1040,1792]{1,0:T(8,128)} %get-tuple-element.100.pre_ref.small_ref.head_ref.gate_ref.refs_8_, f32[1040,1792]{1,0:T(8,128)} %get-tuple-element.100.pre_ref.small_ref.head_ref.gate_ref.refs_8_, ...), custom_call_target="tpu_custom_call" | custom-call | flops 10000000000 | bytes 30000000 | tf_op jit(solution)/shard_map/mixer_query/pallas_call | solution.py:360
  120.9 8.1 %mixer_output.1 = (bf16[1024,512]{1,0:T(8,128)(2,1)}, bf16[1024,512]{1,0:T(8,128)(2,1)}, bf16[2,128,256]{2,1,0:T(8,128)(2,1)}, bf16[512,512]{1,0:T(8,128)(2,1)},...) custom-call(s32[1]{0:T(128)} %bitcast.place_ref, ...), custom_call_target="tpu_custom_call" | custom-call | flops 7000000000 | bytes 21000000 | tf_op jit(solution)/shard_map/mixer_output/pallas_call | solution.py:661
  131.1 14.3 %collective-permute-done.12 = bf16[512,512]{1,0:T(8,128)(2,1)S(1)} collective-permute-done((bf16[512,512]{1,0:T(8,128)(2,1)}, bf16[512,512]{1,0:T(8,128)(2,1)S(1)}, u32[]{:S(2)}, u32[]{:S(2)}) %collective-permute-start.12) | collective-permute-done | bytes 524320 | tf_op jit(solution)/shard_map/ppermute | solution.py:411
  146.4 3.6 collective-permute-start.13
  150.0 8.3 %mixer_true.1 = (bf16[32,128,256]{2,1,0:T(8,128)(2,1)}, f32[32,8,128]{2,1,0:T(8,128)}, bf16[1024,512]{1,0:T(8,128)(2,1)}) custom-call(f32[1040,1792]{1,0:T(8,128)} %get-tuple-element.100.pre_ref.small_ref.head_ref.gate_ref.refs_8_, f32[1,128]{1,0:T(1,128)} %get-tuple-element.310.rate_ref, f32[1,128]{1,0:T(1,128)} %get-tuple-element.309.bias_ref, ...), custom_call_target="tpu_custom_call" | custom-call | flops 6000000000 | bytes 18000000 | tf_op jit(solution)/shard_map/mixer_true/pallas_call | solution.py:1131
  158.7 8.4 %collective-permute-done.13 = bf16[512,256]{1,0:T(8,128)(2,1)S(1)} collective-permute-done((bf16[512,256]{1,0:T(8,128)(2,1)S(1)}, bf16[512,256]{1,0:T(8,128)(2,1)S(1)}, u32[]{:S(2)}, u32[]{:S(2)}) %collective-permute-start.13) | collective-permute-done | bytes 262176 | tf_op jit(solution)/shard_map/ppermute | solution.py:411
  167.3 3.4 collective-permute-start.14
  170.7 7.7 %collective-permute-done.9 = bf16[512,256]{1,0:T(8,128)(2,1)S(1)} collective-permute-done((bf16[512,256]{1,0:T(8,128)(2,1)S(1)}, bf16[512,256]{1,0:T(8,128)(2,1)S(1)}, u32[]{:S(2)}, u32[]{:S(2)}) %collective-permute-start.9) | collective-permute-done | bytes 262176 | tf_op jit(solution)/shard_map/ppermute | solution.py:411
  178.5 3.4 collective-permute-start.10
  182.0 4.6 collective-permute-done.14.refs_4_
  186.6 4.1 collective-permute-start.15
  191.4 3.4 collective-permute-start.11
  194.8 8.7 %collective-permute-done.15.refs_5_ = bf16[512,512]{1,0:T(8,128)(2,1)S(1)} collective-permute-done((bf16[512,512]{1,0:T(8,128)(2,1)S(1)}, bf16[512,512]{1,0:T(8,128)(2,1)S(1)}, u32[]{:S(2)}, u32[]{:S(2)}) %collective-permute-start.15) | collective-permute-done | bytes 524320 | tf_op jit(solution)/shard_map/ppermute | solution.py:411
  203.5 10.6 %collective-permute-done.11.refs_2_ = bf16[512,512]{1,0:T(8,128)(2,1)S(1)} collective-permute-done((bf16[512,512]{1,0:T(8,128)(2,1)S(1)}, bf16[512,512]{1,0:T(8,128)(2,1)S(1)}, u32[]{:S(2)}, u32[]{:S(2)}) %collective-permute-start.11) | collective-permute-done | bytes 524320 | tf_op jit(solution)/shard_map/ppermute | solution.py:411
  214.9 19.5 %feed_forward.1 = (f32[1024,1024]{1,0:T(8,128)}, bf16[1024,1024]{1,0:T(8,128)(2,1)}, bf16[1024,704]{1,0:T(8,128)(2,1)}, bf16[1024,704]{1,0:T(8,128)(2,1)}, bf16[...) custom-call(s32[1]{0:T(128)} %bitcast.place_ref, ...), custom_call_target="tpu_custom_call" | custom-call | flops 20000000000 | bytes 60000000 | tf_op jit(solution)/shard_map/feed_forward/pallas_call | solution.py:777
  234.4 10.4 %weight_grads.3 = bf16[1024,2304]{1,0:T(8,128)(2,1)} custom-call(bf16[1024,1024]{1,0:T(8,128)(2,1)} %get-tuple-element.128.refs_0_.refs_2_, bf16[1024,704]{1,0:T(8,128)(2,1)} %get-tuple-element.129.refs_1_, bf16[1024,1024]{1,0:T(8,128)(2,1)} %get-tuple-element.128.refs_0_.refs_2_, bf16[1024,704]{1,0:T(8,128)(2,1)} %get-tuple-element.130.refs_3_, ...), custom_call_target="tpu_custom_call" | custom-call | flops 5000000000 | bytes 15000000 | tf_op jit(solution)/shard_map/weight_grads/pallas_call | solution.py:506
  245.8 2.5 collective-permute-start.20
  248.5 12.6 %collective-permute-done.20 = bf16[512,512]{1,0:T(8,128)(2,1)S(1)} collective-permute-done((bf16[512,512]{1,0:T(8,128)(2,1)S(1)}, bf16[512,512]{1,0:T(8,128)(2,1)S(1)}, u32[]{:S(2)}, u32[]{:S(2)}) %collective-permute-start.20) | collective-permute-done | bytes 524320 | tf_op jit(solution)/shard_map/ppermute | solution.py:411
  262.6 12.6 %collective-permute-done.21 = bf16[512,256]{1,0:T(8,128)(2,1)S(1)} collective-permute-done((bf16[512,256]{1,0:T(8,128)(2,1)S(1)}, bf16[512,256]{1,0:T(8,128)(2,1)S(1)}, u32[]{:S(2)}, u32[]{:S(2)}) %collective-permute-start.21) | collective-permute-done | bytes 262176 | tf_op jit(solution)/shard_map/ppermute | solution.py:411
  278.5 14.9 %collective-permute-done.22.refs_1_ = bf16[512,256]{1,0:T(8,128)(2,1)S(1)} collective-permute-done((bf16[512,256]{1,0:T(8,128)(2,1)S(1)}, bf16[512,256]{1,0:T(8,128)(2,1)S(1)}, u32[]{:S(2)}, u32[]{:S(2)}) %collective-permute-start.22) | collective-permute-done | bytes 262176 | tf_op jit(solution)/shard_map/ppermute | solution.py:411
  295.5 2.8 collective-permute-done.17
  298.3 3.5 collective-permute-start.18
  304.9 8.2 %collective-permute-done.18.refs_1_ = bf16[512,256]{1,0:T(8,128)(2,1)S(1)} collective-permute-done((bf16[512,256]{1,0:T(8,128)(2,1)S(1)}, bf16[512,256]{1,0:T(8,128)(2,1)S(1)}, u32[]{:S(2)}, u32[]{:S(2)}) %collective-permute-start.18) | collective-permute-done | bytes 262176 | tf_op jit(solution)/shard_map/ppermute | solution.py:411
  313.2 2.9 collective-permute-start.19
  316.9 7.5 %gate_back.2 = (bf16[1024,1024]{1,0:T(8,128)(2,1)}, bf16[1024,512]{1,0:T(8,128)(2,1)}, bf16[1024,512]{1,0:T(8,128)(2,1)}, f32[32,128,256]{2,1,0:T(8,128)}, f32[1...) custom-call(s32[1]{0:T(128)} %bitcast.place_ref, bf16[512,256]{1,0:T(8,128)(2,1)} %copy-done.10, ...), custom_call_target="tpu_custom_call" | custom-call | flops 7000000000 | bytes 21000000 | tf_op jit(solution)/shard_map/gate_back/pallas_call | solution.py:916
  324.4 2.9 collective-permute-done.19.refs_2_
  328.0 7.4 %gate_back.3 = (bf16[1024,1024]{1,0:T(8,128)(2,1)}, bf16[1024,512]{1,0:T(8,128)(2,1)}, bf16[1024,512]{1,0:T(8,128)(2,1)}, f32[32,128,256]{2,1,0:T(8,128)}, f32[1...) custom-call(s32[1]{0:T(128)} %bitcast.place_ref, ...), custom_call_target="tpu_custom_call", output_to_operand_aliasing={{0}: (13, {}), {1}: (14, {}), {2}: (15, {}), {3}: (16, {}),... | custom-call | flops 7000000000 | bytes 21000000 | tf_op jit(solution)/shard_map/gate_back/pallas_call | solution.py:916
  345.3 6.5 %weight_grads.4 = bf16[1024,1024]{1,0:T(8,128)(2,1)} custom-call(bf16[1024,1024]{1,0:T(8,128)(2,1)} %get-tuple-element.144.refs_0_, bf16[1024,512]{1,0:T(8,128)(2,1)} %get-tuple-element.145.refs_1_, bf16[1040,1024]{1,0:T(8,128)(2,1)} %get-tuple-element.146.refs_2_.refs_0_, bf16[1024,512]{1,0:T(8,128)(2,1)} %get-tuple-element.147.refs_3_.gate_grad_ref), custom_call_target="tpu_custom_call" | custom-call | flops 5000000000 | bytes 15000000 | tf_op jit(solution)/shard_map/weight_grads/pallas_call | solution.py:506
  351.8 8.6 %reduce-scatter.6.cloned.1.call-start = ((), (), s32[]{:S(2)}) async-start(), calls=%async_computation.8 | async-start | bytes 2621440 | tf_op jit(solution)/shard_map/reduce_scatter | solution.py:1812
  362.2 9.1 %mixer_ready.1 = (f32[1024,512]{1,0:T(8,128)}, f32[1024,256]{1,0:T(8,128)}, f32[1024,256]{1,0:T(8,128)}, f32[8,256]{1,0:T(8,128)}, f32[1024,128]{1,0:T(8,128)}) custom-call(f32[1040,1792]{1,0:T(8,128)} %get-tuple-element.100.pre_ref.small_ref.head_ref.gate_ref.refs_8_, f32[1040,1792]{1,0:T(8,128)} %get-tuple-element.100.pre_ref.small_ref.head_ref.gate_ref.refs_8_, ...), custom_call_target="tpu_custom_call" | custom-call | flops 11000000512 | bytes 33000000 | tf_op jit(solution)/shard_map/mixer_ready/pallas_call | solution.py:1263
  373.9 29.7 %mixer_backward.1 = (bf16[1040,1024]{1,0:T(8,128)(2,1)}, bf16[1040,128]{1,0:T(8,128)(2,1)}, f32[8,1024]{1,0:T(8,128)}, f32[8,128]{1,0:T(8,128)}) custom-call(f32[16]{0:T(128)} %convert_subtract_fusion.keep_ref, f32[1040,1792]{1,0:T(8,128)} %get-tuple-element.100.pre_ref.small_ref.head_ref.gate_ref.refs_8_, ...), custom_call_target="tpu_custom_call" | custom-call | flops 24999999488 | bytes 75000000 | tf_op jit(solution)/shard_map/mixer_backward/pallas_call | solution.py:1561
  407.1 9.0 %input_terms.1 = (f32[1040,128]{1,0:T(8,128)}, f32[8,1024]{1,0:T(8,128)}, f32[16,1024]{1,0:T(8,128)}, bf16[1024,1024]{1,0:T(8,128)(2,1)}) custom-call(s32[1]{0:T(128)} %bitcast.place_ref, bf16[1040,1024]{1,0:T(8,128)(2,1)} %get-tuple-element.166.pre_grad_ref.refs_1_, bf16[1040,128]{1,0:T(8,128)(2,1)} %get-tuple-element.167.small_grad_ref.refs_3_, ...), custom_call_target="tpu_custom_call" | custom-call | flops 8000000000 | bytes 24000000 | tf_op jit(solution)/shard_map/input_terms/pallas_call | solution.py:1021
  417.6 7.5 %weight_grads.5 = bf16[1024,1152]{1,0:T(8,128)(2,1)} custom-call(bf16[1040,1024]{1,0:T(8,128)(2,1)} %get-tuple-element.146.refs_2_.refs_0_, bf16[1040,1024]{1,0:T(8,128)(2,1)} %get-tuple-element.166.pre_grad_ref.refs_1_, bf16[1040,1024]{1,0:T(8,128)(2,1)} %get-tuple-element.146.refs_2_.refs_0_, bf16[1040,128]{1,0:T(8,128)(2,1)} %get-tuple-element.167.small_grad_ref.refs_3_), custom_call_target="tpu_custom_call" | custom-call | flops 5000000000 | bytes 15000000 | tf_op jit(solution)/shard_map/weight_grads/pallas_call | solution.py:506
  426.5 4.1 collective-permute-start.31
  445.8 2.7 add_convert_fusion.1
  452.1 3.9 collective-permute-start.38
  456.5 2.7 collective-permute-start.42
  461.9 7.7 %collective-permute-done.38 = f32[192,128]{1,0:T(8,128)S(1)} collective-permute-done((f32[192,128]{1,0:T(8,128)S(1)}, f32[192,128]{1,0:T(8,128)S(1)}, u32[]{:S(2)}, u32[]{:S(2)}) %collective-permute-start.38) | collective-permute-done | bytes 98336 | tf_op jit(solution)/shard_map/ppermute | solution.py:390
  469.6 5.9 %collective-permute-done.39 = f32[192,128]{1,0:T(8,128)S(1)} collective-permute-done((f32[192,128]{1,0:T(8,128)S(1)}, f32[192,128]{1,0:T(8,128)S(1)}, u32[]{:S(2)}, u32[]{:S(2)}) %collective-permute-start.39) | collective-permute-done | bytes 98336 | tf_op jit(solution)/shard_map/ppermute | solution.py:390
  (301 shorter events, 94.4 us)
Async XLA Ops:
  7.2 62.6 %all-gather.7.cloned.1.call-start = ((), (), s32[]{:S(2)}) async-start(), calls=%async_computation.4 | async-start | bytes 3735552 | tf_op jit(solution)/shard_map/all_gather | solution.py:451
  9.7 60.1 %all-gather.9.cloned.1.call-start = ((), (), s32[]{:S(2)}) async-start(), calls=%async_computation.5 | async-start | bytes 4718592 | tf_op jit(solution)/shard_map/all_gather | solution.py:451
  12.4 57.5 %all-gather.5.cloned.1.call-start = ((), (), s32[]{:S(2)}) async-start(), calls=%async_computation.3 | async-start | bytes 5505024 | tf_op jit(solution)/shard_map/all_gather | solution.py:451
  15.2 104.9 %all-gather.11.cloned.1.call-start = ((), (), s32[]{:S(2)}) async-start(), calls=%async_computation.6 | async-start | bytes 2621440 | tf_op jit(solution)/shard_map/all_gather | solution.py:1695
  15.2 6.4 %collective-permute-start = (bf16[16,256]{1,0:T(8,128)(2,1)S(1)}, bf16[16,256]{1,0:T(8,128)(2,1)S(1)}, u32[]{:S(2)}, u32[]{:S(2)}) collective-permute-start(bf16[16,256]{1,0:T(8,128)(2,1)S(1)} %slice.164), channel_id=1, source_target_pairs={{0,4},{4,8},{8,12},{12,16},{16,20},{20,24},{24,28},{1,5},{5,9},{9,... | collective-permute-start | bytes 24584 | tf_op jit(solution)/shard_map/ppermute | solution.py:34
  21.6 37.9 %collective-permute-start.3 = (bf16[1040,256]{1,0:T(8,128)(2,1)S(1)}, bf16[1040,256]{1,0:T(8,128)(2,1)S(1)}, u32[]{:S(2)}, u32[]{:S(2)}) collective-permute-start(bf16[1040,256]{1,0:T(8,128)(2,1)S(1)} %constant_dynamic-update-slice_fusion.refs_0_), channel_id=1, source_target_pairs={{0,3},{1,0},{2,1},{3,2},{4,7},{5,4},{6,5},{7,6},{8,11},{9,8},{10,9... | collective-permute-start | bytes 1597448 | tf_op jit(solution)/shard_map/ppermute | solution.py:390
  22.1 37.4 %collective-permute-start.2 = (bf16[1040,256]{1,0:T(8,128)(2,1)S(1)}, bf16[1040,256]{1,0:T(8,128)(2,1)S(1)}, u32[]{:S(2)}, u32[]{:S(2)}) collective-permute-start(bf16[1040,256]{1,0:T(8,128)(2,1)S(1)} %constant_dynamic-update-slice_fusion.refs_0_), channel_id=1, source_target_pairs={{0,2},{1,3},{2,0},{3,1},{4,6},{5,7},{6,4},{7,5},{8,10},{9,11},{10,... | collective-permute-start | bytes 1597448 | tf_op jit(solution)/shard_map/ppermute | solution.py:390
  24.7 45.1 %collective-permute-start.1 = (bf16[1040,256]{1,0:T(8,128)(2,1)S(1)}, bf16[1040,256]{1,0:T(8,128)(2,1)S(1)}, u32[]{:S(2)}, u32[]{:S(2)}) collective-permute-start(bf16[1040,256]{1,0:T(8,128)(2,1)S(1)} %constant_dynamic-update-slice_fusion.refs_0_), channel_id=1, source_target_pairs={{0,1},{1,2},{2,3},{3,0},{4,5},{5,6},{6,7},{7,4},{8,9},{9,10},{10,1... | collective-permute-start | bytes 1597448 | tf_op jit(solution)/shard_map/ppermute | solution.py:390
  69.8 274.3 %reduce-scatter.4.cloned.1.call-start = ((), (), s32[]{:S(2)}) async-start(), calls=%async_computation.7 | async-start | bytes 5308416 | tf_op jit(solution)/shard_map/reduce_scatter | solution.py:455
  101.5 18.6 %collective-permute-start.7 = (bf16[2,128,384]{2,1,0:T(8,128)(2,1)}, bf16[2,128,384]{2,1,0:T(8,128)(2,1)S(1)}, u32[]{:S(2)}, u32[]{:S(2)}) collective-permute-start(bf16[2,128,384]{2,1,0:T(8,128)(2,1)} %get-tuple-element.107), channel_id=1, source_target_pairs={{0,16},{4,20},{8,24},{12,28},{1,17},{5,21},{9,25},{13,29},{2,18},{... | collective-permute-start | bytes 589832 | tf_op jit(solution)/shard_map/ppermute | solution.py:34
  102.8 17.3 %collective-permute-start.6 = (bf16[2,128,384]{2,1,0:T(8,128)(2,1)}, bf16[2,128,384]{2,1,0:T(8,128)(2,1)S(1)}, u32[]{:S(2)}, u32[]{:S(2)}) collective-permute-start(bf16[2,128,384]{2,1,0:T(8,128)(2,1)} %get-tuple-element.107), channel_id=1, source_target_pairs={{0,12},{4,16},{8,20},{12,24},{16,28},{1,13},{5,17},{9,21},{13,25},... | collective-permute-start | bytes 589832 | tf_op jit(solution)/shard_map/ppermute | solution.py:34
  105.4 14.8 %collective-permute-start.5 = (bf16[2,128,384]{2,1,0:T(8,128)(2,1)}, bf16[2,128,384]{2,1,0:T(8,128)(2,1)S(1)}, u32[]{:S(2)}, u32[]{:S(2)}) collective-permute-start(bf16[2,128,384]{2,1,0:T(8,128)(2,1)} %get-tuple-element.107), channel_id=1, source_target_pairs={{0,8},{4,12},{8,16},{12,20},{16,24},{20,28},{1,9},{5,13},{9,17},{1... | collective-permute-start | bytes 589832 | tf_op jit(solution)/shard_map/ppermute | solution.py:34
  108.4 11.7 %collective-permute-start.4 = (bf16[2,128,384]{2,1,0:T(8,128)(2,1)}, bf16[2,128,384]{2,1,0:T(8,128)(2,1)S(1)}, u32[]{:S(2)}, u32[]{:S(2)}) collective-permute-start(bf16[2,128,384]{2,1,0:T(8,128)(2,1)} %get-tuple-element.107), channel_id=1, source_target_pairs={{0,4},{4,8},{8,12},{12,16},{16,20},{20,24},{24,28},{1,5},{5,9},{9,... | collective-permute-start | bytes 589832 | tf_op jit(solution)/shard_map/ppermute | solution.py:34
  129.0 16.3 %collective-permute-start.12 = (bf16[512,512]{1,0:T(8,128)(2,1)}, bf16[512,512]{1,0:T(8,128)(2,1)S(1)}, u32[]{:S(2)}, u32[]{:S(2)}) collective-permute-start(bf16[512,512]{1,0:T(8,128)(2,1)} %get-tuple-element.118), channel_id=1, source_target_pairs={{0,1},{1,0},{2,3},{3,2},{4,5},{5,4},{6,7},{7,6},{8,9},{9,8},{10,11... | collective-permute-start | bytes 1572872 | tf_op jit(solution)/shard_map/ppermute | solution.py:411
  129.8 28.4 %collective-permute-start.8 = (bf16[512,512]{1,0:T(8,128)(2,1)}, bf16[512,512]{1,0:T(8,128)(2,1)S(1)}, u32[]{:S(2)}, u32[]{:S(2)}) collective-permute-start(bf16[512,512]{1,0:T(8,128)(2,1)} %get-tuple-element.111), channel_id=1, source_target_pairs={{0,1},{1,0},{2,3},{3,2},{4,5},{5,4},{6,7},{7,6},{8,9},{9,8},{10,11... | collective-permute-start | bytes 1572872 | tf_op jit(solution)/shard_map/ppermute | solution.py:411
  146.4 20.8 %collective-permute-start.13 = (bf16[512,256]{1,0:T(8,128)(2,1)S(1)}, bf16[512,256]{1,0:T(8,128)(2,1)S(1)}, u32[]{:S(2)}, u32[]{:S(2)}) collective-permute-start(bf16[512,256]{1,0:T(8,128)(2,1)S(1)} %add_convert_fusion.7), channel_id=1, source_target_pairs={{0,2},{1,3},{2,0},{3,1},{4,6},{5,7},{6,4},{7,5},{8,10},{9,11},{10,... | collective-permute-start | bytes 786440 | tf_op jit(solution)/shard_map/ppermute | solution.py:411
  158.4 20.0 %collective-permute-start.9 = (bf16[512,256]{1,0:T(8,128)(2,1)S(1)}, bf16[512,256]{1,0:T(8,128)(2,1)S(1)}, u32[]{:S(2)}, u32[]{:S(2)}) collective-permute-start(bf16[512,256]{1,0:T(8,128)(2,1)S(1)} %add_convert_fusion.9), channel_id=1, source_target_pairs={{0,2},{1,3},{2,0},{3,1},{4,6},{5,7},{6,4},{7,5},{8,10},{9,11},{10,... | collective-permute-start | bytes 786440 | tf_op jit(solution)/shard_map/ppermute | solution.py:411
  167.3 19.3 %collective-permute-start.14 = (bf16[512,256]{1,0:T(8,128)(2,1)S(1)}, bf16[512,256]{1,0:T(8,128)(2,1)S(1)}, u32[]{:S(2)}, u32[]{:S(2)}) collective-permute-start(bf16[512,256]{1,0:T(8,128)(2,1)S(1)} %add_convert_fusion.6.refs_3_), channel_id=1, source_target_pairs={{0,2},{1,3},{2,0},{3,1},{4,6},{5,7},{6,4},{7,5},{8,10},{9,11},{10,... | collective-permute-start | bytes 786440 | tf_op jit(solution)/shard_map/ppermute | solution.py:411
  178.5 12.8 %collective-permute-start.10 = (bf16[512,256]{1,0:T(8,128)(2,1)S(1)}, bf16[512,256]{1,0:T(8,128)(2,1)S(1)}, u32[]{:S(2)}, u32[]{:S(2)}) collective-permute-start(bf16[512,256]{1,0:T(8,128)(2,1)S(1)} %add_convert_fusion.8.refs_0_), channel_id=1, source_target_pairs={{0,2},{1,3},{2,0},{3,1},{4,6},{5,7},{6,4},{7,5},{8,10},{9,11},{10,... | collective-permute-start | bytes 786440 | tf_op jit(solution)/shard_map/ppermute | solution.py:411
  186.6 16.9 %collective-permute-start.15 = (bf16[512,512]{1,0:T(8,128)(2,1)S(1)}, bf16[512,512]{1,0:T(8,128)(2,1)S(1)}, u32[]{:S(2)}, u32[]{:S(2)}) collective-permute-start(bf16[512,512]{1,0:T(8,128)(2,1)S(1)} %pad_maximum_fusion.2), channel_id=1, source_target_pairs={{0,1},{1,0},{2,3},{3,2},{4,5},{5,4},{6,7},{7,6},{8,9},{9,8},{10,11... | collective-permute-start | bytes 1572872 | tf_op jit(solution)/shard_map/ppermute | solution.py:411
  191.4 22.7 %collective-permute-start.11 = (bf16[512,512]{1,0:T(8,128)(2,1)S(1)}, bf16[512,512]{1,0:T(8,128)(2,1)S(1)}, u32[]{:S(2)}, u32[]{:S(2)}) collective-permute-start(bf16[512,512]{1,0:T(8,128)(2,1)S(1)} %pad_maximum_fusion.1), channel_id=1, source_target_pairs={{0,1},{1,0},{2,3},{3,2},{4,5},{5,4},{6,7},{7,6},{8,9},{9,8},{10,11... | collective-permute-start | bytes 1572872 | tf_op jit(solution)/shard_map/ppermute | solution.py:411
  244.8 242.3 %reduce-scatter.8.cloned.1.call-start = ((), (), s32[]{:S(2)}) async-start(), calls=%async_computation.9 | async-start | bytes 2359296 | tf_op jit(solution)/shard_map/reduce_scatter | solution.py:1765
  245.8 15.3 %collective-permute-start.20 = (bf16[512,512]{1,0:T(8,128)(2,1)S(1)}, bf16[512,512]{1,0:T(8,128)(2,1)S(1)}, u32[]{:S(2)}, u32[]{:S(2)}) collective-permute-start(bf16[512,512]{1,0:T(8,128)(2,1)S(1)} %copy-done.43), channel_id=1, source_target_pairs={{0,1},{1,0},{2,3},{3,2},{4,5},{5,4},{6,7},{7,6},{8,9},{9,8},{10,11... | collective-permute-start | bytes 1572872 | tf_op jit(solution)/shard_map/ppermute | solution.py:411
  248.3 27.7 %collective-permute-start.16 = (bf16[512,512]{1,0:T(8,128)(2,1)S(1)}, bf16[512,512]{1,0:T(8,128)(2,1)S(1)}, u32[]{:S(2)}, u32[]{:S(2)}) collective-permute-start(bf16[512,512]{1,0:T(8,128)(2,1)S(1)} %copy-done.42), channel_id=1, source_target_pairs={{0,1},{1,0},{2,3},{3,2},{4,5},{5,4},{6,7},{7,6},{8,9},{9,8},{10,11... | collective-permute-start | bytes 1572872 | tf_op jit(solution)/shard_map/ppermute | solution.py:411
  261.2 14.0 %collective-permute-start.21 = (bf16[512,256]{1,0:T(8,128)(2,1)S(1)}, bf16[512,256]{1,0:T(8,128)(2,1)S(1)}, u32[]{:S(2)}, u32[]{:S(2)}) collective-permute-start(bf16[512,256]{1,0:T(8,128)(2,1)S(1)} %add_convert_fusion.3), channel_id=1, source_target_pairs={{0,2},{1,3},{2,0},{3,1},{4,6},{5,7},{6,4},{7,5},{8,10},{9,11},{10,... | collective-permute-start | bytes 786440 | tf_op jit(solution)/shard_map/ppermute | solution.py:411
  275.3 18.1 %collective-permute-start.22 = (bf16[512,256]{1,0:T(8,128)(2,1)S(1)}, bf16[512,256]{1,0:T(8,128)(2,1)S(1)}, u32[]{:S(2)}, u32[]{:S(2)}) collective-permute-start(bf16[512,256]{1,0:T(8,128)(2,1)S(1)} %add_convert_fusion.2.refs_0_), channel_id=1, source_target_pairs={{0,2},{1,3},{2,0},{3,1},{4,6},{5,7},{6,4},{7,5},{8,10},{9,11},{10,... | collective-permute-start | bytes 786440 | tf_op jit(solution)/shard_map/ppermute | solution.py:411
  276.1 22.2 %collective-permute-start.17 = (bf16[512,256]{1,0:T(8,128)(2,1)S(1)}, bf16[512,256]{1,0:T(8,128)(2,1)S(1)}, u32[]{:S(2)}, u32[]{:S(2)}) collective-permute-start(bf16[512,256]{1,0:T(8,128)(2,1)S(1)} %add_convert_fusion.5), channel_id=1, source_target_pairs={{0,2},{1,3},{2,0},{3,1},{4,6},{5,7},{6,4},{7,5},{8,10},{9,11},{10,... | collective-permute-start | bytes 786440 | tf_op jit(solution)/shard_map/ppermute | solution.py:411
  293.5 22.7 %collective-permute-start.23 = (bf16[512,512]{1,0:T(8,128)(2,1)S(1)}, bf16[512,512]{1,0:T(8,128)(2,1)S(1)}, u32[]{:S(2)}, u32[]{:S(2)}) collective-permute-start(bf16[512,512]{1,0:T(8,128)(2,1)S(1)} %pad_maximum_fusion.4), channel_id=1, source_target_pairs={{0,1},{1,0},{2,3},{3,2},{4,5},{5,4},{6,7},{7,6},{8,9},{9,8},{10,11... | collective-permute-start | bytes 1572872 | tf_op jit(solution)/shard_map/ppermute | solution.py:411
  298.3 14.8 %collective-permute-start.18 = (bf16[512,256]{1,0:T(8,128)(2,1)S(1)}, bf16[512,256]{1,0:T(8,128)(2,1)S(1)}, u32[]{:S(2)}, u32[]{:S(2)}) collective-permute-start(bf16[512,256]{1,0:T(8,128)(2,1)S(1)} %add_convert_fusion.4.refs_0_), channel_id=1, source_target_pairs={{0,2},{1,3},{2,0},{3,1},{4,6},{5,7},{6,4},{7,5},{8,10},{9,11},{10,... | collective-permute-start | bytes 786440 | tf_op jit(solution)/shard_map/ppermute | solution.py:411
  313.2 14.1 %collective-permute-start.19 = (bf16[512,512]{1,0:T(8,128)(2,1)S(1)}, bf16[512,512]{1,0:T(8,128)(2,1)S(1)}, u32[]{:S(2)}, u32[]{:S(2)}) collective-permute-start(bf16[512,512]{1,0:T(8,128)(2,1)S(1)} %pad_maximum_fusion.3), channel_id=1, source_target_pairs={{0,1},{1,0},{2,3},{3,2},{4,5},{5,4},{6,7},{7,6},{8,9},{9,8},{10,11... | collective-permute-start | bytes 1572872 | tf_op jit(solution)/shard_map/ppermute | solution.py:411
  336.5 34.8 %collective-permute-start.30 = (bf16[2,128,384]{2,1,0:T(8,128)(2,1)S(1)}, bf16[2,128,384]{2,1,0:T(8,128)(2,1)S(1)}, u32[]{:S(2)}, u32[]{:S(2)}) collective-permute-start(bf16[2,128,384]{2,1,0:T(8,128)(2,1)S(1)} %pad_maximum_fusion.5), channel_id=1, source_target_pairs={{16,0},{20,4},{24,8},{28,12},{17,1},{21,5},{25,9},{29,13},{18,2},{... | collective-permute-start | bytes 589832 | tf_op jit(solution)/shard_map/ppermute | solution.py:34
  337.8 34.2 %collective-permute-start.29 = (bf16[2,128,384]{2,1,0:T(8,128)(2,1)S(1)}, bf16[2,128,384]{2,1,0:T(8,128)(2,1)S(1)}, u32[]{:S(2)}, u32[]{:S(2)}) collective-permute-start(bf16[2,128,384]{2,1,0:T(8,128)(2,1)S(1)} %pad_maximum_fusion.5), channel_id=1, source_target_pairs={{12,0},{16,4},{20,8},{24,12},{28,16},{13,1},{17,5},{21,9},{25,13},... | collective-permute-start | bytes 589832 | tf_op jit(solution)/shard_map/ppermute | solution.py:34
  339.1 34.0 %collective-permute-start.28 = (bf16[2,128,384]{2,1,0:T(8,128)(2,1)S(1)}, bf16[2,128,384]{2,1,0:T(8,128)(2,1)S(1)}, u32[]{:S(2)}, u32[]{:S(2)}) collective-permute-start(bf16[2,128,384]{2,1,0:T(8,128)(2,1)S(1)} %pad_maximum_fusion.5), channel_id=1, source_target_pairs={{8,0},{12,4},{16,8},{20,12},{24,16},{28,20},{9,1},{13,5},{17,9},{2... | collective-permute-start | bytes 589832 | tf_op jit(solution)/shard_map/ppermute | solution.py:34
  340.4 32.7 %collective-permute-start.27 = (bf16[2,128,384]{2,1,0:T(8,128)(2,1)S(1)}, bf16[2,128,384]{2,1,0:T(8,128)(2,1)S(1)}, u32[]{:S(2)}, u32[]{:S(2)}) collective-permute-start(bf16[2,128,384]{2,1,0:T(8,128)(2,1)S(1)} %pad_maximum_fusion.5), channel_id=1, source_target_pairs={{4,0},{8,4},{12,8},{16,12},{20,16},{24,20},{28,24},{5,1},{9,5},{13... | collective-permute-start | bytes 589832 | tf_op jit(solution)/shard_map/ppermute | solution.py:34
  351.8 138.0 %reduce-scatter.6.cloned.1.call-start = ((), (), s32[]{:S(2)}) async-start(), calls=%async_computation.8 | async-start | bytes 2621440 | tf_op jit(solution)/shard_map/reduce_scatter | solution.py:1812
  360.4 84.6 %collective-permute-start.24 = (bf16[1024,256]{1,0:T(8,128)(2,1)}, bf16[1024,256]{1,0:T(8,128)(2,1)S(1)}, u32[]{:S(2)}, u32[]{:S(2)}) collective-permute-start(bf16[1024,256]{1,0:T(8,128)(2,1)} %get-tuple-element.149), channel_id=1, source_target_pairs={{0,1},{1,0},{2,3},{3,2},{4,5},{5,4},{6,7},{7,6},{8,9},{9,8},{10,11... | collective-permute-start | bytes 1572872 | tf_op jit(solution)/shard_map/ppermute | solution.py:411
  371.3 74.5 %collective-permute-start.25 = (bf16[1024,256]{1,0:T(8,128)(2,1)}, bf16[1024,256]{1,0:T(8,128)(2,1)}, u32[]{:S(2)}, u32[]{:S(2)}) collective-permute-start(bf16[1024,256]{1,0:T(8,128)(2,1)} %get-tuple-element.150), channel_id=1, source_target_pairs={{0,2},{1,3},{2,0},{3,1},{4,6},{5,7},{6,4},{7,5},{8,10},{9,11},{10,... | collective-permute-start | bytes 1572872 | tf_op jit(solution)/shard_map/ppermute | solution.py:411
  372.1 73.7 %collective-permute-start.26 = (bf16[1024,256]{1,0:T(8,128)(2,1)}, bf16[1024,256]{1,0:T(8,128)(2,1)}, u32[]{:S(2)}, u32[]{:S(2)}) collective-permute-start(bf16[1024,256]{1,0:T(8,128)(2,1)} %get-tuple-element.151), channel_id=1, source_target_pairs={{0,3},{1,2},{2,1},{3,0},{4,7},{5,6},{6,5},{7,4},{8,11},{9,10},{10,... | collective-permute-start | bytes 1572872 | tf_op jit(solution)/shard_map/ppermute | solution.py:411
  426.5 12.2 %collective-permute-start.31 = (bf16[512,1152]{1,0:T(8,128)(2,1)S(1)}, bf16[512,1152]{1,0:T(8,128)(2,1)S(1)}, u32[]{:S(2)}, u32[]{:S(2)}) collective-permute-start(bf16[512,1152]{1,0:T(8,128)(2,1)S(1)} %constant_dynamic-slice_fusion.4), channel_id=1, source_target_pairs={{0,16},{16,0},{1,17},{17,1},{2,18},{18,2},{3,19},{19,3},{4,20},{20... | collective-permute-start | bytes 3538952 | tf_op jit(solution)/shard_map/ppermute | solution.py:447
  431.3 6.6 %collective-permute-start.36 = (f32[16,1152]{1,0:T(8,128)}, f32[16,1152]{1,0:T(8,128)}, u32[]{:S(2)}, u32[]{:S(2)}) collective-permute-start(f32[16,1152]{1,0:T(8,128)} %pad_maximum_fusion.7), channel_id=1, source_target_pairs={{4,0},{8,4},{12,8},{16,12},{20,16},{24,20},{28,24},{5,1},{9,5},{13... | collective-permute-start | bytes 221192 | tf_op jit(solution)/shard_map/ppermute | solution.py:34
  442.5 6.0 %collective-permute-start.35 = (f32[152,128]{1,0:T(8,128)S(1)}, f32[152,128]{1,0:T(8,128)S(1)}, u32[]{:S(2)}, u32[]{:S(2)}) collective-permute-start(f32[152,128]{1,0:T(8,128)S(1)} %add.247), channel_id=1, source_target_pairs={{0,12},{4,0},{8,4},{12,8},{1,13},{5,1},{9,5},{13,9},{2,14},{6,2},{... | collective-permute-start | bytes 233480 | tf_op jit(solution)/shard_map/ppermute | solution.py:390
  444.6 6.1 %collective-permute-start.34 = (f32[152,128]{1,0:T(8,128)S(1)}, f32[152,128]{1,0:T(8,128)S(1)}, u32[]{:S(2)}, u32[]{:S(2)}) collective-permute-start(f32[152,128]{1,0:T(8,128)S(1)} %add.247), channel_id=1, source_target_pairs={{0,8},{4,12},{8,0},{12,4},{1,9},{5,13},{9,1},{13,5},{2,10},{6,14},... | collective-permute-start | bytes 233480 | tf_op jit(solution)/shard_map/ppermute | solution.py:390
  450.8 9.8 %collective-permute-start.37 = (f32[192,128]{1,0:T(8,128)S(1)}, f32[192,128]{1,0:T(8,128)S(1)}, u32[]{:S(2)}, u32[]{:S(2)}) collective-permute-start(f32[192,128]{1,0:T(8,128)S(1)} %get-tuple-element.300), channel_id=1, source_target_pairs={{0,1},{1,2},{2,3},{3,0},{4,5},{5,6},{6,7},{7,4},{8,9},{9,10},{10,1... | collective-permute-start | bytes 294920 | tf_op jit(solution)/shard_map/ppermute | solution.py:390
  452.1 17.5 %collective-permute-start.38 = (f32[192,128]{1,0:T(8,128)S(1)}, f32[192,128]{1,0:T(8,128)S(1)}, u32[]{:S(2)}, u32[]{:S(2)}) collective-permute-start(f32[192,128]{1,0:T(8,128)S(1)} %get-tuple-element.301), channel_id=1, source_target_pairs={{0,2},{1,3},{2,0},{3,1},{4,6},{5,7},{6,4},{7,5},{8,10},{9,11},{10,... | collective-permute-start | bytes 294920 | tf_op jit(solution)/shard_map/ppermute | solution.py:390
  456.1 19.4 %collective-permute-start.39 = (f32[192,128]{1,0:T(8,128)S(1)}, f32[192,128]{1,0:T(8,128)S(1)}, u32[]{:S(2)}, u32[]{:S(2)}) collective-permute-start(f32[192,128]{1,0:T(8,128)S(1)} %get-tuple-element.302), channel_id=1, source_target_pairs={{0,3},{1,0},{2,1},{3,2},{4,7},{5,4},{6,5},{7,6},{8,11},{9,8},{10,9... | collective-permute-start | bytes 294920 | tf_op jit(solution)/shard_map/ppermute | solution.py:390
  456.2 26.9 %collective-permute-start.40 = (bf16[128,1152]{1,0:T(8,128)(2,1)S(1)}, bf16[128,1152]{1,0:T(8,128)(2,1)S(1)}, u32[]{:S(2)}, u32[]{:S(2)}) collective-permute-start(bf16[128,1152]{1,0:T(8,128)(2,1)S(1)} %get-tuple-element.285), channel_id=1, source_target_pairs={{0,4},{4,8},{8,12},{12,0},{1,5},{5,9},{9,13},{13,1},{2,6},{6,10},{... | collective-permute-start | bytes 884744 | tf_op jit(solution)/shard_map/ppermute | solution.py:390
  456.5 26.6 %collective-permute-start.42 = (bf16[128,1152]{1,0:T(8,128)(2,1)S(1)}, bf16[128,1152]{1,0:T(8,128)(2,1)}, u32[]{:S(2)}, u32[]{:S(2)}) collective-permute-start(bf16[128,1152]{1,0:T(8,128)(2,1)S(1)} %get-tuple-element.286), channel_id=1, source_target_pairs={{0,12},{4,0},{8,4},{12,8},{1,13},{5,1},{9,5},{13,9},{2,14},{6,2},{... | collective-permute-start | bytes 884744 | tf_op jit(solution)/shard_map/ppermute | solution.py:390
  460.5 22.5 %collective-permute-start.41 = (bf16[128,1152]{1,0:T(8,128)(2,1)S(1)}, bf16[128,1152]{1,0:T(8,128)(2,1)}, u32[]{:S(2)}, u32[]{:S(2)}) collective-permute-start(bf16[128,1152]{1,0:T(8,128)(2,1)S(1)} %get-tuple-element.287), channel_id=1, source_target_pairs={{0,8},{4,12},{8,0},{12,4},{1,9},{5,13},{9,1},{13,5},{2,10},{6,14},... | collective-permute-start | bytes 884744 | tf_op jit(solution)/shard_map/ppermute | solution.py:390
  (59 other events, 568.3 us)
Sparse Core Ops, SparseCore 0:
  9.8 12.5 all-gather.6
  24.0 13.2 all-gather.8
  38.9 14.0 all-gather.4
  70.0 45.0 all-gather.10
  244.9 53.1 reduce-scatter.3
  352.0 46.0 reduce-scatter.7
  432.7 54.4 reduce-scatter.5

commit v4 on v3

--- a/solution.py
+++ b/solution.py
@@ -21,7 +21,7 @@
 VMEM_LIMIT = 56 * 1024 * 1024
 INVERSE_PASSES = 1
 CHUNKS = 2
-SIDES = 2
+SIDES = 4
 
 
 def cost(micros):
@@ -758,13 +758,14 @@
     rows, features = cot.shape
     chunks = len(attn)
     width = features // 2
-    steps = rows // PACK // chunks
+    step_rows = rows // chunks
+    steps = 1
     whole = lambda shape: pl.BlockSpec(shape, lambda i, at: (0,) * len(shape))
-    rows_at = lambda size: pl.BlockSpec((PACK, size), lambda i, at: (i, 0))
+    rows_at = lambda size: pl.BlockSpec((step_rows, size), lambda i, at: (i, 0))
 
     def part(chunk, size):
         return pl.BlockSpec(
-            (PACK, size), lambda i, at: (jnp.clip(i - chunk * steps, 0, steps - 1), 0)
+            (step_rows, size), lambda i, at: (jnp.clip(i - chunk * steps, 0, steps - 1), 0)
         )
 
     kept = [
@@ -778,7 +779,7 @@
         functools.partial(feed_kernel, chunks=chunks),
         grid_spec=pltpu.PrefetchScalarGridSpec(
             num_scalar_prefetch=1,
-            grid=(rows // PACK,),
+            grid=(chunks,),
             in_specs=[
                 part(chunk, piece.shape[1]) for chunk in range(chunks) for piece in attn[chunk]
             ]
@@ -791,8 +792,8 @@
             ],
             out_specs=[rows_at(size) for size, _ in kept]
             + [part(chunk, width) for chunk in range(chunks) for _ in range(2)],
-            scratch_shapes=[pltpu.VMEM((PACK, features), BF)]
-            + [pltpu.VMEM((PACK, width), BF)] * 2,
+            scratch_shapes=[pltpu.VMEM((step_rows, features), BF)]
+            + [pltpu.VMEM((step_rows, width), BF)] * 2,
         ),
         out_shape=[jax.ShapeDtypeStruct((rows, size), kind) for size, kind in kept]
         + [jax.ShapeDtypeStruct((rows // chunks, width), BF)] * (2 * chunks),

time: 505 us -> 497 us (0.984)
  starting transfers between devices: 91.4 us -> 82 us
    reduce_scatter x1, starting transfers between devices: 8.56 us -> 0.21 us  [per_device(): lax.psum_scatter(in_part, 'tensor', scatter_dimension=1, tiled=True)]
where the time goes in v4:
time: 497 us; the launch traced here: 491 us
  waiting for transfers between devices  170 us (34%)
  Pallas kernels  163 us (33%)
  starting transfers between devices  82 us (16%)
  local copies, waits for them, and re-layouts  39.7 us (8%)
  other arithmetic  20.9 us (4%)
  between operations  15.4 us (3%)
    ppermute x19, waiting for transfers between devices, paired(): return lax.ppermute(shard, 'tensor', [(i, i ^ by) for i in range(devices)])  110 us
    ppermute x12, waiting for transfers between devices, rotated(): lax.ppermute(shard, axis, [(i, (i + by) % devices) for i in range(devices)])  59.1 us
    ppermute x19, starting transfers between devices, paired(): return lax.ppermute(shard, 'tensor', [(i, i ^ by) for i in range(devices)])  39 us
    pallas_call x1, Pallas kernels, mixer_backward(): pl.pallas_call(functools.partial(backward_kernel, heads=heads, rows=rows,...  30.1 us
    pallas_call x3, Pallas kernels, weight_grads(): pl.pallas_call(functools.partial(weight_kernel, rows=[right.shape[0] for...  24.4 us
    pallas_call x1, Pallas kernels, feed_forward(): pl.pallas_call(functools.partial(feed_kernel, chunks=chunks), grid_spec=p...  19.9 us
    ppermute x10, starting transfers between devices, shifted(): return lax.ppermute(shard, axis, pairs)  19.2 us
    ppermute x12, starting transfers between devices, rotated(): lax.ppermute(shard, axis, [(i, (i + by) % devices) for i in range(devices)])  18.1 us
  transfers between devices with their start and end apart: 50, of which 21 were waited for; matrix products, arithmetic and copies ran while one was open for 10% of the time, Pallas kernels for 25%

profile of v4, /device:TPU:8, one launch (start us, length us, event | category | flops | bytes accessed | tf_op | source)
XLA Modules:
  0.0 490.8 jit_solution(15697996848972985657)
XLA Ops:
  15.2 3.4 collective-permute-start
  22.1 2.6 collective-permute-start.2
  28.2 31.3 %collective-permute-done.3.refs_3_ = bf16[1040,256]{1,0:T(8,128)(2,1)S(1)} collective-permute-done((bf16[1040,256]{1,0:T(8,128)(2,1)S(1)}, bf16[1040,256]{1,0:T(8,128)(2,1)S(1)}, u32[]{:S(2)}, u32[]{:S(2)}) %collective-permute-start.3) | collective-permute-done | bytes 532512 | tf_op jit(solution)/shard_map/ppermute | solution.py:390
  59.5 10.3 %collective-permute-done.1.refs_1_ = bf16[1040,256]{1,0:T(8,128)(2,1)S(1)} collective-permute-done((bf16[1040,256]{1,0:T(8,128)(2,1)S(1)}, bf16[1040,256]{1,0:T(8,128)(2,1)S(1)}, u32[]{:S(2)}, u32[]{:S(2)}) %collective-permute-start.1) | collective-permute-done | bytes 532512 | tf_op jit(solution)/shard_map/ppermute | solution.py:390
  70.6 12.3 %project.1 = (bf16[1040,1024]{1,0:T(8,128)(2,1)}, bf16[1040,1024]{1,0:T(8,128)(2,1)}, f32[1040,128]{1,0:T(8,128)}, f32[1040,1792]{1,0:T(8,128)}) custom-call(s32[1]{0:T(128)} %bitcast.place_ref, bf16[1040,256]{1,0:T(8,128)(2,1)} %copy-done.25, bf16[1040,256]{1,0:T(8,128)(2,1)} %copy-done.40, bf16[1040,256]{1,0:T(8,128)(2,1)} %copy-done.39, ...), custom_call_target="tpu_custom_call" | custom-call | flops 8000000000 | bytes 24000000 | tf_op jit(solution)/shard_map/project/pallas_call | solution.py:563
  82.9 18.0 %mixer_forward.1 = (bf16[1024,768]{1,0:T(8,128)(2,1)}, bf16[8,256,256]{2,1,0:T(8,128)(2,1)}, bf16[1024,256]{1,0:T(8,128)(2,1)}, bf16[1024,512]{1,0:T(8,128)(2,1)...) custom-call(f32[16]{0:T(128)} %convert_subtract_fusion.keep_ref, ...), custom_call_target="tpu_custom_call" | custom-call | flops 20000000000 | bytes 60000000 | tf_op jit(solution)/shard_map/mixer_forward/pallas_call | solution.py:262
  102.2 2.6 collective-permute-start.6
  104.8 3.0 collective-permute-start.5
  107.8 2.5 collective-permute-start.4
  110.3 8.9 %mixer_query.1 = (bf16[1024,256]{1,0:T(8,128)(2,1)}, bf16[32,64,128]{2,1,0:T(8,128)(2,1)}, f32[1024,512]{1,0:T(8,128)}, bf16[1024,256]{1,0:T(8,128)(2,1)}) custom-call(f32[1040,1792]{1,0:T(8,128)} %get-tuple-element.100.pre_ref.small_ref.head_ref.gate_ref.refs_8_, f32[1040,1792]{1,0:T(8,128)} %get-tuple-element.100.pre_ref.small_ref.head_ref.gate_ref.refs_8_, ...), custom_call_target="tpu_custom_call" | custom-call | flops 10000000000 | bytes 30000000 | tf_op jit(solution)/shard_map/mixer_query/pallas_call | solution.py:360
  120.1 8.1 %mixer_output.1 = (bf16[1024,512]{1,0:T(8,128)(2,1)}, bf16[1024,512]{1,0:T(8,128)(2,1)}, bf16[2,128,256]{2,1,0:T(8,128)(2,1)}, bf16[512,512]{1,0:T(8,128)(2,1)},...) custom-call(s32[1]{0:T(128)} %bitcast.place_ref, ...), custom_call_target="tpu_custom_call" | custom-call | flops 7000000000 | bytes 21000000 | tf_op jit(solution)/shard_map/mixer_output/pallas_call | solution.py:661
  130.3 14.2 %collective-permute-done.12 = bf16[512,512]{1,0:T(8,128)(2,1)S(1)} collective-permute-done((bf16[512,512]{1,0:T(8,128)(2,1)}, bf16[512,512]{1,0:T(8,128)(2,1)S(1)}, u32[]{:S(2)}, u32[]{:S(2)}) %collective-permute-start.12) | collective-permute-done | bytes 524320 | tf_op jit(solution)/shard_map/ppermute | solution.py:411
  145.5 3.6 collective-permute-start.13
  149.2 8.3 %mixer_true.1 = (bf16[32,128,256]{2,1,0:T(8,128)(2,1)}, f32[32,8,128]{2,1,0:T(8,128)}, bf16[1024,512]{1,0:T(8,128)(2,1)}) custom-call(f32[1040,1792]{1,0:T(8,128)} %get-tuple-element.100.pre_ref.small_ref.head_ref.gate_ref.refs_8_, f32[1,128]{1,0:T(1,128)} %get-tuple-element.310.rate_ref, f32[1,128]{1,0:T(1,128)} %get-tuple-element.309.bias_ref, ...), custom_call_target="tpu_custom_call" | custom-call | flops 6000000000 | bytes 18000000 | tf_op jit(solution)/shard_map/mixer_true/pallas_call | solution.py:1132
  158.0 8.3 %collective-permute-done.13 = bf16[512,256]{1,0:T(8,128)(2,1)S(1)} collective-permute-done((bf16[512,256]{1,0:T(8,128)(2,1)S(1)}, bf16[512,256]{1,0:T(8,128)(2,1)S(1)}, u32[]{:S(2)}, u32[]{:S(2)}) %collective-permute-start.13) | collective-permute-done | bytes 262176 | tf_op jit(solution)/shard_map/ppermute | solution.py:411
  166.4 3.4 collective-permute-start.14
  169.9 7.7 %collective-permute-done.9 = bf16[512,256]{1,0:T(8,128)(2,1)S(1)} collective-permute-done((bf16[512,256]{1,0:T(8,128)(2,1)S(1)}, bf16[512,256]{1,0:T(8,128)(2,1)S(1)}, u32[]{:S(2)}, u32[]{:S(2)}) %collective-permute-start.9) | collective-permute-done | bytes 262176 | tf_op jit(solution)/shard_map/ppermute | solution.py:411
  177.6 3.4 collective-permute-start.10
  181.1 4.5 collective-permute-done.14.refs_4_
  185.6 4.3 collective-permute-start.15
  190.5 3.5 collective-permute-start.11
  194.0 8.7 %collective-permute-done.15.refs_5_ = bf16[512,512]{1,0:T(8,128)(2,1)S(1)} collective-permute-done((bf16[512,512]{1,0:T(8,128)(2,1)S(1)}, bf16[512,512]{1,0:T(8,128)(2,1)S(1)}, u32[]{:S(2)}, u32[]{:S(2)}) %collective-permute-start.15) | collective-permute-done | bytes 524320 | tf_op jit(solution)/shard_map/ppermute | solution.py:411
  202.7 10.7 %collective-permute-done.11.refs_2_ = bf16[512,512]{1,0:T(8,128)(2,1)S(1)} collective-permute-done((bf16[512,512]{1,0:T(8,128)(2,1)S(1)}, bf16[512,512]{1,0:T(8,128)(2,1)S(1)}, u32[]{:S(2)}, u32[]{:S(2)}) %collective-permute-start.11) | collective-permute-done | bytes 524320 | tf_op jit(solution)/shard_map/ppermute | solution.py:411
  214.2 19.9 %feed_forward.1 = (f32[1024,1024]{1,0:T(8,128)}, bf16[1024,1024]{1,0:T(8,128)(2,1)}, bf16[1024,704]{1,0:T(8,128)(2,1)}, bf16[1024,704]{1,0:T(8,128)(2,1)}, bf16[...) custom-call(s32[1]{0:T(128)} %bitcast.place_ref, ...), custom_call_target="tpu_custom_call" | custom-call | flops 20000000000 | bytes 60000000 | tf_op jit(solution)/shard_map/feed_forward/pallas_call | solution.py:778
  234.1 10.4 %weight_grads.3 = bf16[1024,2304]{1,0:T(8,128)(2,1)} custom-call(bf16[1024,1024]{1,0:T(8,128)(2,1)} %get-tuple-element.128.refs_0_.refs_2_, bf16[1024,704]{1,0:T(8,128)(2,1)} %get-tuple-element.129.refs_1_, bf16[1024,1024]{1,0:T(8,128)(2,1)} %get-tuple-element.128.refs_0_.refs_2_, bf16[1024,704]{1,0:T(8,128)(2,1)} %get-tuple-element.130.refs_3_, ...), custom_call_target="tpu_custom_call" | custom-call | flops 5000000000 | bytes 15000000 | tf_op jit(solution)/shard_map/weight_grads/pallas_call | solution.py:506
  245.5 2.5 collective-permute-start.20
  248.2 12.6 %collective-permute-done.20 = bf16[512,512]{1,0:T(8,128)(2,1)S(1)} collective-permute-done((bf16[512,512]{1,0:T(8,128)(2,1)S(1)}, bf16[512,512]{1,0:T(8,128)(2,1)S(1)}, u32[]{:S(2)}, u32[]{:S(2)}) %collective-permute-start.20) | collective-permute-done | bytes 524320 | tf_op jit(solution)/shard_map/ppermute | solution.py:411
  262.3 12.6 %collective-permute-done.21 = bf16[512,256]{1,0:T(8,128)(2,1)S(1)} collective-permute-done((bf16[512,256]{1,0:T(8,128)(2,1)S(1)}, bf16[512,256]{1,0:T(8,128)(2,1)S(1)}, u32[]{:S(2)}, u32[]{:S(2)}) %collective-permute-start.21) | collective-permute-done | bytes 262176 | tf_op jit(solution)/shard_map/ppermute | solution.py:411
  278.1 14.9 %collective-permute-done.22.refs_1_ = bf16[512,256]{1,0:T(8,128)(2,1)S(1)} collective-permute-done((bf16[512,256]{1,0:T(8,128)(2,1)S(1)}, bf16[512,256]{1,0:T(8,128)(2,1)S(1)}, u32[]{:S(2)}, u32[]{:S(2)}) %collective-permute-start.22) | collective-permute-done | bytes 262176 | tf_op jit(solution)/shard_map/ppermute | solution.py:411
  295.2 2.9 collective-permute-done.17
  298.1 3.5 collective-permute-start.18
  304.7 8.4 %collective-permute-done.18.refs_1_ = bf16[512,256]{1,0:T(8,128)(2,1)S(1)} collective-permute-done((bf16[512,256]{1,0:T(8,128)(2,1)S(1)}, bf16[512,256]{1,0:T(8,128)(2,1)S(1)}, u32[]{:S(2)}, u32[]{:S(2)}) %collective-permute-start.18) | collective-permute-done | bytes 262176 | tf_op jit(solution)/shard_map/ppermute | solution.py:411
  313.1 2.7 collective-permute-start.19
  316.6 7.5 %gate_back.2 = (bf16[1024,1024]{1,0:T(8,128)(2,1)}, bf16[1024,512]{1,0:T(8,128)(2,1)}, bf16[1024,512]{1,0:T(8,128)(2,1)}, f32[32,128,256]{2,1,0:T(8,128)}, f32[1...) custom-call(s32[1]{0:T(128)} %bitcast.place_ref, bf16[512,256]{1,0:T(8,128)(2,1)} %copy-done.10, ...), custom_call_target="tpu_custom_call" | custom-call | flops 7000000000 | bytes 21000000 | tf_op jit(solution)/shard_map/gate_back/pallas_call | solution.py:917
  324.1 2.8 collective-permute-done.19.refs_2_
  327.7 7.4 %gate_back.3 = (bf16[1024,1024]{1,0:T(8,128)(2,1)}, bf16[1024,512]{1,0:T(8,128)(2,1)}, bf16[1024,512]{1,0:T(8,128)(2,1)}, f32[32,128,256]{2,1,0:T(8,128)}, f32[1...) custom-call(s32[1]{0:T(128)} %bitcast.place_ref, ...), custom_call_target="tpu_custom_call", output_to_operand_aliasing={{0}: (13, {}), {1}: (14, {}), {2}: (15, {}), {3}: (16, {}),... | custom-call | flops 7000000000 | bytes 21000000 | tf_op jit(solution)/shard_map/gate_back/pallas_call | solution.py:917
  345.0 6.5 %weight_grads.4 = bf16[1024,1024]{1,0:T(8,128)(2,1)} custom-call(bf16[1024,1024]{1,0:T(8,128)(2,1)} %get-tuple-element.144.refs_0_, bf16[1024,512]{1,0:T(8,128)(2,1)} %get-tuple-element.145.refs_1_, bf16[1040,1024]{1,0:T(8,128)(2,1)} %get-tuple-element.146.refs_2_.refs_0_, bf16[1024,512]{1,0:T(8,128)(2,1)} %get-tuple-element.147.refs_3_.gate_grad_ref), custom_call_target="tpu_custom_call" | custom-call | flops 5000000000 | bytes 15000000 | tf_op jit(solution)/shard_map/weight_grads/pallas_call | solution.py:506
  353.5 8.9 %mixer_ready.1 = (f32[1024,512]{1,0:T(8,128)}, f32[1024,256]{1,0:T(8,128)}, f32[1024,256]{1,0:T(8,128)}, f32[8,256]{1,0:T(8,128)}, f32[1024,128]{1,0:T(8,128)}) custom-call(f32[1040,1792]{1,0:T(8,128)} %get-tuple-element.100.pre_ref.small_ref.head_ref.gate_ref.refs_8_, f32[1040,1792]{1,0:T(8,128)} %get-tuple-element.100.pre_ref.small_ref.head_ref.gate_ref.refs_8_, ...), custom_call_target="tpu_custom_call" | custom-call | flops 11000000512 | bytes 33000000 | tf_op jit(solution)/shard_map/mixer_ready/pallas_call | solution.py:1264
  365.0 30.1 %mixer_backward.1 = (bf16[1040,1024]{1,0:T(8,128)(2,1)}, bf16[1040,128]{1,0:T(8,128)(2,1)}, f32[8,1024]{1,0:T(8,128)}, f32[8,128]{1,0:T(8,128)}) custom-call(f32[16]{0:T(128)} %convert_subtract_fusion.keep_ref, f32[1040,1792]{1,0:T(8,128)} %get-tuple-element.100.pre_ref.small_ref.head_ref.gate_ref.refs_8_, ...), custom_call_target="tpu_custom_call" | custom-call | flops 24999999488 | bytes 75000000 | tf_op jit(solution)/shard_map/mixer_backward/pallas_call | solution.py:1562
  398.7 9.0 %input_terms.1 = (f32[1040,128]{1,0:T(8,128)}, f32[8,1024]{1,0:T(8,128)}, f32[16,1024]{1,0:T(8,128)}, bf16[1024,1024]{1,0:T(8,128)(2,1)}) custom-call(s32[1]{0:T(128)} %bitcast.place_ref, bf16[1040,1024]{1,0:T(8,128)(2,1)} %get-tuple-element.166.pre_grad_ref.refs_1_, bf16[1040,128]{1,0:T(8,128)(2,1)} %get-tuple-element.167.small_grad_ref.refs_3_, ...), custom_call_target="tpu_custom_call" | custom-call | flops 8000000000 | bytes 24000000 | tf_op jit(solution)/shard_map/input_terms/pallas_call | solution.py:1022
  409.2 7.5 %weight_grads.5 = bf16[1024,1152]{1,0:T(8,128)(2,1)} custom-call(bf16[1040,1024]{1,0:T(8,128)(2,1)} %get-tuple-element.146.refs_2_.refs_0_, bf16[1040,1024]{1,0:T(8,128)(2,1)} %get-tuple-element.166.pre_grad_ref.refs_1_, bf16[1040,1024]{1,0:T(8,128)(2,1)} %get-tuple-element.146.refs_2_.refs_0_, bf16[1040,128]{1,0:T(8,128)(2,1)} %get-tuple-element.167.small_grad_ref.refs_3_), custom_call_target="tpu_custom_call" | custom-call | flops 5000000000 | bytes 15000000 | tf_op jit(solution)/shard_map/weight_grads/pallas_call | solution.py:506
  418.1 3.8 collective-permute-start.31
  437.2 2.7 add_convert_fusion.1
  439.9 2.5 collective-permute-done.34
  443.4 4.2 collective-permute-start.38
  448.0 2.7 collective-permute-start.42
  453.0 7.8 %collective-permute-done.38 = f32[192,128]{1,0:T(8,128)S(1)} collective-permute-done((f32[192,128]{1,0:T(8,128)S(1)}, f32[192,128]{1,0:T(8,128)S(1)}, u32[]{:S(2)}, u32[]{:S(2)}) %collective-permute-start.38) | collective-permute-done | bytes 98336 | tf_op jit(solution)/shard_map/ppermute | solution.py:390
  460.8 6.1 %collective-permute-done.39 = f32[192,128]{1,0:T(8,128)S(1)} collective-permute-done((f32[192,128]{1,0:T(8,128)S(1)}, f32[192,128]{1,0:T(8,128)S(1)}, u32[]{:S(2)}, u32[]{:S(2)}) %collective-permute-start.39) | collective-permute-done | bytes 98336 | tf_op jit(solution)/shard_map/ppermute | solution.py:390
  (301 shorter events, 91.6 us)
Async XLA Ops:
  7.2 62.6 %all-gather.7.cloned.1.call-start = ((), (), s32[]{:S(2)}) async-start(), calls=%async_computation.4 | async-start | bytes 3735552 | tf_op jit(solution)/shard_map/all_gather | solution.py:451
  9.7 60.1 %all-gather.9.cloned.1.call-start = ((), (), s32[]{:S(2)}) async-start(), calls=%async_computation.5 | async-start | bytes 4718592 | tf_op jit(solution)/shard_map/all_gather | solution.py:451
  12.4 57.5 %all-gather.5.cloned.1.call-start = ((), (), s32[]{:S(2)}) async-start(), calls=%async_computation.3 | async-start | bytes 5505024 | tf_op jit(solution)/shard_map/all_gather | solution.py:451
  15.2 104.1 %all-gather.11.cloned.1.call-start = ((), (), s32[]{:S(2)}) async-start(), calls=%async_computation.6 | async-start | bytes 2621440 | tf_op jit(solution)/shard_map/all_gather | solution.py:1696
  15.2 6.4 %collective-permute-start = (bf16[16,256]{1,0:T(8,128)(2,1)S(1)}, bf16[16,256]{1,0:T(8,128)(2,1)S(1)}, u32[]{:S(2)}, u32[]{:S(2)}) collective-permute-start(bf16[16,256]{1,0:T(8,128)(2,1)S(1)} %slice.164), channel_id=1, source_target_pairs={{0,4},{4,8},{8,12},{12,16},{16,20},{20,24},{24,28},{1,5},{5,9},{9,... | collective-permute-start | bytes 24584 | tf_op jit(solution)/shard_map/ppermute | solution.py:34
  21.6 37.9 %collective-permute-start.3 = (bf16[1040,256]{1,0:T(8,128)(2,1)S(1)}, bf16[1040,256]{1,0:T(8,128)(2,1)S(1)}, u32[]{:S(2)}, u32[]{:S(2)}) collective-permute-start(bf16[1040,256]{1,0:T(8,128)(2,1)S(1)} %constant_dynamic-update-slice_fusion.refs_0_), channel_id=1, source_target_pairs={{0,3},{1,0},{2,1},{3,2},{4,7},{5,4},{6,5},{7,6},{8,11},{9,8},{10,9... | collective-permute-start | bytes 1597448 | tf_op jit(solution)/shard_map/ppermute | solution.py:390
  22.1 37.4 %collective-permute-start.2 = (bf16[1040,256]{1,0:T(8,128)(2,1)S(1)}, bf16[1040,256]{1,0:T(8,128)(2,1)S(1)}, u32[]{:S(2)}, u32[]{:S(2)}) collective-permute-start(bf16[1040,256]{1,0:T(8,128)(2,1)S(1)} %constant_dynamic-update-slice_fusion.refs_0_), channel_id=1, source_target_pairs={{0,2},{1,3},{2,0},{3,1},{4,6},{5,7},{6,4},{7,5},{8,10},{9,11},{10,... | collective-permute-start | bytes 1597448 | tf_op jit(solution)/shard_map/ppermute | solution.py:390
  24.7 45.1 %collective-permute-start.1 = (bf16[1040,256]{1,0:T(8,128)(2,1)S(1)}, bf16[1040,256]{1,0:T(8,128)(2,1)S(1)}, u32[]{:S(2)}, u32[]{:S(2)}) collective-permute-start(bf16[1040,256]{1,0:T(8,128)(2,1)S(1)} %constant_dynamic-update-slice_fusion.refs_0_), channel_id=1, source_target_pairs={{0,1},{1,2},{2,3},{3,0},{4,5},{5,6},{6,7},{7,4},{8,9},{9,10},{10,1... | collective-permute-start | bytes 1597448 | tf_op jit(solution)/shard_map/ppermute | solution.py:390
  69.8 274.0 %reduce-scatter.4.cloned.1.call-start = ((), (), s32[]{:S(2)}) async-start(), calls=%async_computation.7 | async-start | bytes 5308416 | tf_op jit(solution)/shard_map/reduce_scatter | solution.py:455
  100.9 18.3 %collective-permute-start.7 = (bf16[2,128,384]{2,1,0:T(8,128)(2,1)}, bf16[2,128,384]{2,1,0:T(8,128)(2,1)S(1)}, u32[]{:S(2)}, u32[]{:S(2)}) collective-permute-start(bf16[2,128,384]{2,1,0:T(8,128)(2,1)} %get-tuple-element.107), channel_id=1, source_target_pairs={{0,16},{4,20},{8,24},{12,28},{1,17},{5,21},{9,25},{13,29},{2,18},{... | collective-permute-start | bytes 589832 | tf_op jit(solution)/shard_map/ppermute | solution.py:34
  102.2 17.1 %collective-permute-start.6 = (bf16[2,128,384]{2,1,0:T(8,128)(2,1)}, bf16[2,128,384]{2,1,0:T(8,128)(2,1)S(1)}, u32[]{:S(2)}, u32[]{:S(2)}) collective-permute-start(bf16[2,128,384]{2,1,0:T(8,128)(2,1)} %get-tuple-element.107), channel_id=1, source_target_pairs={{0,12},{4,16},{8,20},{12,24},{16,28},{1,13},{5,17},{9,21},{13,25},... | collective-permute-start | bytes 589832 | tf_op jit(solution)/shard_map/ppermute | solution.py:34
  104.8 14.5 %collective-permute-start.5 = (bf16[2,128,384]{2,1,0:T(8,128)(2,1)}, bf16[2,128,384]{2,1,0:T(8,128)(2,1)S(1)}, u32[]{:S(2)}, u32[]{:S(2)}) collective-permute-start(bf16[2,128,384]{2,1,0:T(8,128)(2,1)} %get-tuple-element.107), channel_id=1, source_target_pairs={{0,8},{4,12},{8,16},{12,20},{16,24},{20,28},{1,9},{5,13},{9,17},{1... | collective-permute-start | bytes 589832 | tf_op jit(solution)/shard_map/ppermute | solution.py:34
  107.8 11.4 %collective-permute-start.4 = (bf16[2,128,384]{2,1,0:T(8,128)(2,1)}, bf16[2,128,384]{2,1,0:T(8,128)(2,1)S(1)}, u32[]{:S(2)}, u32[]{:S(2)}) collective-permute-start(bf16[2,128,384]{2,1,0:T(8,128)(2,1)} %get-tuple-element.107), channel_id=1, source_target_pairs={{0,4},{4,8},{8,12},{12,16},{16,20},{20,24},{24,28},{1,5},{5,9},{9,... | collective-permute-start | bytes 589832 | tf_op jit(solution)/shard_map/ppermute | solution.py:34
  128.2 16.3 %collective-permute-start.12 = (bf16[512,512]{1,0:T(8,128)(2,1)}, bf16[512,512]{1,0:T(8,128)(2,1)S(1)}, u32[]{:S(2)}, u32[]{:S(2)}) collective-permute-start(bf16[512,512]{1,0:T(8,128)(2,1)} %get-tuple-element.118), channel_id=1, source_target_pairs={{0,1},{1,0},{2,3},{3,2},{4,5},{5,4},{6,7},{7,6},{8,9},{9,8},{10,11... | collective-permute-start | bytes 1572872 | tf_op jit(solution)/shard_map/ppermute | solution.py:411
  129.0 28.4 %collective-permute-start.8 = (bf16[512,512]{1,0:T(8,128)(2,1)}, bf16[512,512]{1,0:T(8,128)(2,1)S(1)}, u32[]{:S(2)}, u32[]{:S(2)}) collective-permute-start(bf16[512,512]{1,0:T(8,128)(2,1)} %get-tuple-element.111), channel_id=1, source_target_pairs={{0,1},{1,0},{2,3},{3,2},{4,5},{5,4},{6,7},{7,6},{8,9},{9,8},{10,11... | collective-permute-start | bytes 1572872 | tf_op jit(solution)/shard_map/ppermute | solution.py:411
  145.5 20.8 %collective-permute-start.13 = (bf16[512,256]{1,0:T(8,128)(2,1)S(1)}, bf16[512,256]{1,0:T(8,128)(2,1)S(1)}, u32[]{:S(2)}, u32[]{:S(2)}) collective-permute-start(bf16[512,256]{1,0:T(8,128)(2,1)S(1)} %add_convert_fusion.7), channel_id=1, source_target_pairs={{0,2},{1,3},{2,0},{3,1},{4,6},{5,7},{6,4},{7,5},{8,10},{9,11},{10,... | collective-permute-start | bytes 786440 | tf_op jit(solution)/shard_map/ppermute | solution.py:411
  157.6 20.0 %collective-permute-start.9 = (bf16[512,256]{1,0:T(8,128)(2,1)S(1)}, bf16[512,256]{1,0:T(8,128)(2,1)S(1)}, u32[]{:S(2)}, u32[]{:S(2)}) collective-permute-start(bf16[512,256]{1,0:T(8,128)(2,1)S(1)} %add_convert_fusion.9), channel_id=1, source_target_pairs={{0,2},{1,3},{2,0},{3,1},{4,6},{5,7},{6,4},{7,5},{8,10},{9,11},{10,... | collective-permute-start | bytes 786440 | tf_op jit(solution)/shard_map/ppermute | solution.py:411
  166.4 19.2 %collective-permute-start.14 = (bf16[512,256]{1,0:T(8,128)(2,1)S(1)}, bf16[512,256]{1,0:T(8,128)(2,1)S(1)}, u32[]{:S(2)}, u32[]{:S(2)}) collective-permute-start(bf16[512,256]{1,0:T(8,128)(2,1)S(1)} %add_convert_fusion.6.refs_3_), channel_id=1, source_target_pairs={{0,2},{1,3},{2,0},{3,1},{4,6},{5,7},{6,4},{7,5},{8,10},{9,11},{10,... | collective-permute-start | bytes 786440 | tf_op jit(solution)/shard_map/ppermute | solution.py:411
  177.6 12.8 %collective-permute-start.10 = (bf16[512,256]{1,0:T(8,128)(2,1)S(1)}, bf16[512,256]{1,0:T(8,128)(2,1)S(1)}, u32[]{:S(2)}, u32[]{:S(2)}) collective-permute-start(bf16[512,256]{1,0:T(8,128)(2,1)S(1)} %add_convert_fusion.8.refs_0_), channel_id=1, source_target_pairs={{0,2},{1,3},{2,0},{3,1},{4,6},{5,7},{6,4},{7,5},{8,10},{9,11},{10,... | collective-permute-start | bytes 786440 | tf_op jit(solution)/shard_map/ppermute | solution.py:411
  185.6 17.1 %collective-permute-start.15 = (bf16[512,512]{1,0:T(8,128)(2,1)S(1)}, bf16[512,512]{1,0:T(8,128)(2,1)S(1)}, u32[]{:S(2)}, u32[]{:S(2)}) collective-permute-start(bf16[512,512]{1,0:T(8,128)(2,1)S(1)} %pad_maximum_fusion.2), channel_id=1, source_target_pairs={{0,1},{1,0},{2,3},{3,2},{4,5},{5,4},{6,7},{7,6},{8,9},{9,8},{10,11... | collective-permute-start | bytes 1572872 | tf_op jit(solution)/shard_map/ppermute | solution.py:411
  190.5 22.8 %collective-permute-start.11 = (bf16[512,512]{1,0:T(8,128)(2,1)S(1)}, bf16[512,512]{1,0:T(8,128)(2,1)S(1)}, u32[]{:S(2)}, u32[]{:S(2)}) collective-permute-start(bf16[512,512]{1,0:T(8,128)(2,1)S(1)} %pad_maximum_fusion.1), channel_id=1, source_target_pairs={{0,1},{1,0},{2,3},{3,2},{4,5},{5,4},{6,7},{7,6},{8,9},{9,8},{10,11... | collective-permute-start | bytes 1572872 | tf_op jit(solution)/shard_map/ppermute | solution.py:411
  244.5 234.1 %reduce-scatter.8.cloned.1.call-start = ((), (), s32[]{:S(2)}) async-start(), calls=%async_computation.9 | async-start | bytes 2359296 | tf_op jit(solution)/shard_map/reduce_scatter | solution.py:1766
  245.5 15.3 %collective-permute-start.20 = (bf16[512,512]{1,0:T(8,128)(2,1)S(1)}, bf16[512,512]{1,0:T(8,128)(2,1)S(1)}, u32[]{:S(2)}, u32[]{:S(2)}) collective-permute-start(bf16[512,512]{1,0:T(8,128)(2,1)S(1)} %copy-done.43), channel_id=1, source_target_pairs={{0,1},{1,0},{2,3},{3,2},{4,5},{5,4},{6,7},{7,6},{8,9},{9,8},{10,11... | collective-permute-start | bytes 1572872 | tf_op jit(solution)/shard_map/ppermute | solution.py:411
  248.0 27.7 %collective-permute-start.16 = (bf16[512,512]{1,0:T(8,128)(2,1)S(1)}, bf16[512,512]{1,0:T(8,128)(2,1)S(1)}, u32[]{:S(2)}, u32[]{:S(2)}) collective-permute-start(bf16[512,512]{1,0:T(8,128)(2,1)S(1)} %copy-done.42), channel_id=1, source_target_pairs={{0,1},{1,0},{2,3},{3,2},{4,5},{5,4},{6,7},{7,6},{8,9},{9,8},{10,11... | collective-permute-start | bytes 1572872 | tf_op jit(solution)/shard_map/ppermute | solution.py:411
  260.9 14.0 %collective-permute-start.21 = (bf16[512,256]{1,0:T(8,128)(2,1)S(1)}, bf16[512,256]{1,0:T(8,128)(2,1)S(1)}, u32[]{:S(2)}, u32[]{:S(2)}) collective-permute-start(bf16[512,256]{1,0:T(8,128)(2,1)S(1)} %add_convert_fusion.3), channel_id=1, source_target_pairs={{0,2},{1,3},{2,0},{3,1},{4,6},{5,7},{6,4},{7,5},{8,10},{9,11},{10,... | collective-permute-start | bytes 786440 | tf_op jit(solution)/shard_map/ppermute | solution.py:411
  275.0 18.1 %collective-permute-start.22 = (bf16[512,256]{1,0:T(8,128)(2,1)S(1)}, bf16[512,256]{1,0:T(8,128)(2,1)S(1)}, u32[]{:S(2)}, u32[]{:S(2)}) collective-permute-start(bf16[512,256]{1,0:T(8,128)(2,1)S(1)} %add_convert_fusion.2.refs_0_), channel_id=1, source_target_pairs={{0,2},{1,3},{2,0},{3,1},{4,6},{5,7},{6,4},{7,5},{8,10},{9,11},{10,... | collective-permute-start | bytes 786440 | tf_op jit(solution)/shard_map/ppermute | solution.py:411
  275.9 22.2 %collective-permute-start.17 = (bf16[512,256]{1,0:T(8,128)(2,1)S(1)}, bf16[512,256]{1,0:T(8,128)(2,1)S(1)}, u32[]{:S(2)}, u32[]{:S(2)}) collective-permute-start(bf16[512,256]{1,0:T(8,128)(2,1)S(1)} %add_convert_fusion.5), channel_id=1, source_target_pairs={{0,2},{1,3},{2,0},{3,1},{4,6},{5,7},{6,4},{7,5},{8,10},{9,11},{10,... | collective-permute-start | bytes 786440 | tf_op jit(solution)/shard_map/ppermute | solution.py:411
  293.1 22.7 %collective-permute-start.23 = (bf16[512,512]{1,0:T(8,128)(2,1)S(1)}, bf16[512,512]{1,0:T(8,128)(2,1)S(1)}, u32[]{:S(2)}, u32[]{:S(2)}) collective-permute-start(bf16[512,512]{1,0:T(8,128)(2,1)S(1)} %pad_maximum_fusion.4), channel_id=1, source_target_pairs={{0,1},{1,0},{2,3},{3,2},{4,5},{5,4},{6,7},{7,6},{8,9},{9,8},{10,11... | collective-permute-start | bytes 1572872 | tf_op jit(solution)/shard_map/ppermute | solution.py:411
  298.1 14.9 %collective-permute-start.18 = (bf16[512,256]{1,0:T(8,128)(2,1)S(1)}, bf16[512,256]{1,0:T(8,128)(2,1)S(1)}, u32[]{:S(2)}, u32[]{:S(2)}) collective-permute-start(bf16[512,256]{1,0:T(8,128)(2,1)S(1)} %add_convert_fusion.4.refs_0_), channel_id=1, source_target_pairs={{0,2},{1,3},{2,0},{3,1},{4,6},{5,7},{6,4},{7,5},{8,10},{9,11},{10,... | collective-permute-start | bytes 786440 | tf_op jit(solution)/shard_map/ppermute | solution.py:411
  313.1 13.8 %collective-permute-start.19 = (bf16[512,512]{1,0:T(8,128)(2,1)S(1)}, bf16[512,512]{1,0:T(8,128)(2,1)S(1)}, u32[]{:S(2)}, u32[]{:S(2)}) collective-permute-start(bf16[512,512]{1,0:T(8,128)(2,1)S(1)} %pad_maximum_fusion.3), channel_id=1, source_target_pairs={{0,1},{1,0},{2,3},{3,2},{4,5},{5,4},{6,7},{7,6},{8,9},{9,8},{10,11... | collective-permute-start | bytes 1572872 | tf_op jit(solution)/shard_map/ppermute | solution.py:411
  336.2 26.3 %collective-permute-start.30 = (bf16[2,128,384]{2,1,0:T(8,128)(2,1)S(1)}, bf16[2,128,384]{2,1,0:T(8,128)(2,1)S(1)}, u32[]{:S(2)}, u32[]{:S(2)}) collective-permute-start(bf16[2,128,384]{2,1,0:T(8,128)(2,1)S(1)} %pad_maximum_fusion.5), channel_id=1, source_target_pairs={{16,0},{20,4},{24,8},{28,12},{17,1},{21,5},{25,9},{29,13},{18,2},{... | collective-permute-start | bytes 589832 | tf_op jit(solution)/shard_map/ppermute | solution.py:34
  337.5 25.9 %collective-permute-start.29 = (bf16[2,128,384]{2,1,0:T(8,128)(2,1)S(1)}, bf16[2,128,384]{2,1,0:T(8,128)(2,1)S(1)}, u32[]{:S(2)}, u32[]{:S(2)}) collective-permute-start(bf16[2,128,384]{2,1,0:T(8,128)(2,1)S(1)} %pad_maximum_fusion.5), channel_id=1, source_target_pairs={{12,0},{16,4},{20,8},{24,12},{28,16},{13,1},{17,5},{21,9},{25,13},... | collective-permute-start | bytes 589832 | tf_op jit(solution)/shard_map/ppermute | solution.py:34
  338.8 25.5 %collective-permute-start.28 = (bf16[2,128,384]{2,1,0:T(8,128)(2,1)S(1)}, bf16[2,128,384]{2,1,0:T(8,128)(2,1)S(1)}, u32[]{:S(2)}, u32[]{:S(2)}) collective-permute-start(bf16[2,128,384]{2,1,0:T(8,128)(2,1)S(1)} %pad_maximum_fusion.5), channel_id=1, source_target_pairs={{8,0},{12,4},{16,8},{20,12},{24,16},{28,20},{9,1},{13,5},{17,9},{2... | collective-permute-start | bytes 589832 | tf_op jit(solution)/shard_map/ppermute | solution.py:34
  340.1 24.2 %collective-permute-start.27 = (bf16[2,128,384]{2,1,0:T(8,128)(2,1)S(1)}, bf16[2,128,384]{2,1,0:T(8,128)(2,1)S(1)}, u32[]{:S(2)}, u32[]{:S(2)}) collective-permute-start(bf16[2,128,384]{2,1,0:T(8,128)(2,1)S(1)} %pad_maximum_fusion.5), channel_id=1, source_target_pairs={{4,0},{8,4},{12,8},{16,12},{20,16},{24,20},{28,24},{5,1},{9,5},{13... | collective-permute-start | bytes 589832 | tf_op jit(solution)/shard_map/ppermute | solution.py:34
  351.5 129.8 %reduce-scatter.6.cloned.1.call-start = ((), (), s32[]{:S(2)}) async-start(), calls=%async_computation.8 | async-start | bytes 2621440 | tf_op jit(solution)/shard_map/reduce_scatter | solution.py:1813
  351.7 84.6 %collective-permute-start.24 = (bf16[1024,256]{1,0:T(8,128)(2,1)}, bf16[1024,256]{1,0:T(8,128)(2,1)S(1)}, u32[]{:S(2)}, u32[]{:S(2)}) collective-permute-start(bf16[1024,256]{1,0:T(8,128)(2,1)} %get-tuple-element.149), channel_id=1, source_target_pairs={{0,1},{1,0},{2,3},{3,2},{4,5},{5,4},{6,7},{7,6},{8,9},{9,8},{10,11... | collective-permute-start | bytes 1572872 | tf_op jit(solution)/shard_map/ppermute | solution.py:411
  362.5 74.7 %collective-permute-start.25 = (bf16[1024,256]{1,0:T(8,128)(2,1)}, bf16[1024,256]{1,0:T(8,128)(2,1)}, u32[]{:S(2)}, u32[]{:S(2)}) collective-permute-start(bf16[1024,256]{1,0:T(8,128)(2,1)} %get-tuple-element.150), channel_id=1, source_target_pairs={{0,2},{1,3},{2,0},{3,1},{4,6},{5,7},{6,4},{7,5},{8,10},{9,11},{10,... | collective-permute-start | bytes 1572872 | tf_op jit(solution)/shard_map/ppermute | solution.py:411
  363.4 73.8 %collective-permute-start.26 = (bf16[1024,256]{1,0:T(8,128)(2,1)}, bf16[1024,256]{1,0:T(8,128)(2,1)}, u32[]{:S(2)}, u32[]{:S(2)}) collective-permute-start(bf16[1024,256]{1,0:T(8,128)(2,1)} %get-tuple-element.151), channel_id=1, source_target_pairs={{0,3},{1,2},{2,1},{3,0},{4,7},{5,6},{6,5},{7,4},{8,11},{9,10},{10,... | collective-permute-start | bytes 1572872 | tf_op jit(solution)/shard_map/ppermute | solution.py:411
  418.1 11.9 %collective-permute-start.31 = (bf16[512,1152]{1,0:T(8,128)(2,1)S(1)}, bf16[512,1152]{1,0:T(8,128)(2,1)S(1)}, u32[]{:S(2)}, u32[]{:S(2)}) collective-permute-start(bf16[512,1152]{1,0:T(8,128)(2,1)S(1)} %constant_dynamic-slice_fusion.4), channel_id=1, source_target_pairs={{0,16},{16,0},{1,17},{17,1},{2,18},{18,2},{3,19},{19,3},{4,20},{20... | collective-permute-start | bytes 3538952 | tf_op jit(solution)/shard_map/ppermute | solution.py:447
  422.6 6.6 %collective-permute-start.36 = (f32[16,1152]{1,0:T(8,128)}, f32[16,1152]{1,0:T(8,128)}, u32[]{:S(2)}, u32[]{:S(2)}) collective-permute-start(f32[16,1152]{1,0:T(8,128)} %pad_maximum_fusion.7), channel_id=1, source_target_pairs={{4,0},{8,4},{12,8},{16,12},{20,16},{24,20},{28,24},{5,1},{9,5},{13... | collective-permute-start | bytes 221192 | tf_op jit(solution)/shard_map/ppermute | solution.py:34
  436.3 6.1 %collective-permute-start.34 = (f32[152,128]{1,0:T(8,128)S(1)}, f32[152,128]{1,0:T(8,128)S(1)}, u32[]{:S(2)}, u32[]{:S(2)}) collective-permute-start(f32[152,128]{1,0:T(8,128)S(1)} %add.247), channel_id=1, source_target_pairs={{0,8},{4,12},{8,0},{12,4},{1,9},{5,13},{9,1},{13,5},{2,10},{6,14},... | collective-permute-start | bytes 233480 | tf_op jit(solution)/shard_map/ppermute | solution.py:390
  436.3 6.1 %collective-permute-start.33 = (f32[152,128]{1,0:T(8,128)S(1)}, f32[152,128]{1,0:T(8,128)S(1)}, u32[]{:S(2)}, u32[]{:S(2)}) collective-permute-start(f32[152,128]{1,0:T(8,128)S(1)} %add.247), channel_id=1, source_target_pairs={{0,4},{4,8},{8,12},{12,0},{1,5},{5,9},{9,13},{13,1},{2,6},{6,10},{... | collective-permute-start | bytes 233480 | tf_op jit(solution)/shard_map/ppermute | solution.py:390
  442.4 9.4 %collective-permute-start.37 = (f32[192,128]{1,0:T(8,128)S(1)}, f32[192,128]{1,0:T(8,128)S(1)}, u32[]{:S(2)}, u32[]{:S(2)}) collective-permute-start(f32[192,128]{1,0:T(8,128)S(1)} %get-tuple-element.300), channel_id=1, source_target_pairs={{0,1},{1,2},{2,3},{3,0},{4,5},{5,6},{6,7},{7,4},{8,9},{9,10},{10,1... | collective-permute-start | bytes 294920 | tf_op jit(solution)/shard_map/ppermute | solution.py:390
  443.4 17.4 %collective-permute-start.38 = (f32[192,128]{1,0:T(8,128)S(1)}, f32[192,128]{1,0:T(8,128)S(1)}, u32[]{:S(2)}, u32[]{:S(2)}) collective-permute-start(f32[192,128]{1,0:T(8,128)S(1)} %get-tuple-element.301), channel_id=1, source_target_pairs={{0,2},{1,3},{2,0},{3,1},{4,6},{5,7},{6,4},{7,5},{8,10},{9,11},{10,... | collective-permute-start | bytes 294920 | tf_op jit(solution)/shard_map/ppermute | solution.py:390
  447.6 19.3 %collective-permute-start.39 = (f32[192,128]{1,0:T(8,128)S(1)}, f32[192,128]{1,0:T(8,128)S(1)}, u32[]{:S(2)}, u32[]{:S(2)}) collective-permute-start(f32[192,128]{1,0:T(8,128)S(1)} %get-tuple-element.302), channel_id=1, source_target_pairs={{0,3},{1,0},{2,1},{3,2},{4,7},{5,4},{6,5},{7,6},{8,11},{9,8},{10,9... | collective-permute-start | bytes 294920 | tf_op jit(solution)/shard_map/ppermute | solution.py:390
  447.7 26.8 %collective-permute-start.40 = (bf16[128,1152]{1,0:T(8,128)(2,1)S(1)}, bf16[128,1152]{1,0:T(8,128)(2,1)S(1)}, u32[]{:S(2)}, u32[]{:S(2)}) collective-permute-start(bf16[128,1152]{1,0:T(8,128)(2,1)S(1)} %get-tuple-element.285), channel_id=1, source_target_pairs={{0,4},{4,8},{8,12},{12,0},{1,5},{5,9},{9,13},{13,1},{2,6},{6,10},{... | collective-permute-start | bytes 884744 | tf_op jit(solution)/shard_map/ppermute | solution.py:390
  448.0 26.6 %collective-permute-start.42 = (bf16[128,1152]{1,0:T(8,128)(2,1)S(1)}, bf16[128,1152]{1,0:T(8,128)(2,1)}, u32[]{:S(2)}, u32[]{:S(2)}) collective-permute-start(bf16[128,1152]{1,0:T(8,128)(2,1)S(1)} %get-tuple-element.286), channel_id=1, source_target_pairs={{0,12},{4,0},{8,4},{12,8},{1,13},{5,1},{9,5},{13,9},{2,14},{6,2},{... | collective-permute-start | bytes 884744 | tf_op jit(solution)/shard_map/ppermute | solution.py:390
  451.8 22.7 %collective-permute-start.41 = (bf16[128,1152]{1,0:T(8,128)(2,1)S(1)}, bf16[128,1152]{1,0:T(8,128)(2,1)}, u32[]{:S(2)}, u32[]{:S(2)}) collective-permute-start(bf16[128,1152]{1,0:T(8,128)(2,1)S(1)} %get-tuple-element.287), channel_id=1, source_target_pairs={{0,8},{4,12},{8,0},{12,4},{1,9},{5,13},{9,1},{13,5},{2,10},{6,14},... | collective-permute-start | bytes 884744 | tf_op jit(solution)/shard_map/ppermute | solution.py:390
  (59 other events, 569.1 us)
Sparse Core Ops, SparseCore 0:
  9.8 12.5 all-gather.6
  24.0 13.2 all-gather.8
  38.9 14.0 all-gather.4
  70.0 45.0 all-gather.10
  244.7 53.8 reduce-scatter.3
  351.6 46.1 reduce-scatter.7
  424.0 54.5 reduce-scatter.5
